TPU v7x, 32 devices: a whole 2x2x4 slice. The times are simulated.
32 devices in a mesh: dp: 16 (over z, x, core), lat: 2 (over y).
Axes of the slice: x: 2, y: 2, z: 4, core: 2. Of those that a mesh axis runs over, the one named last changes fastest.
Arguments:
- fields: bfloat16 [16, 48, 72, 641], P('dp', 'lat'), may hold values from -6 to 6
- noise_fields: bfloat16 [16, 2, 48, 576], P('dp', None, 'lat'), may hold values from -6 to 6
- step_counts: int32 [16], P('dp'), may hold values from 1 to 2, as said below
- spectral_flat: bfloat16 [2, 9986048], P('lat', 'dp'), may hold values from -0.25 to 0.25
- mlp_flat: bfloat16 [1650688], P(('dp', 'lat')), may hold values from -1.2 to 1.4
- cotangent: bfloat16 [16, 48, 72, 641], P('dp', 'lat'), may hold values from -6 to 6
Outputs:
- output_fields: bfloat16 [16, 48, 72, 641], P('dp', 'lat')
- fields_grad: bfloat16 [16, 48, 72, 641], P('dp', 'lat')
- spectral_grad: float32 [2, 9986048], P('lat', 'dp')
- mlp_grad: float32 [1650688], P(('dp', 'lat'))
Inputs may be any that keep to these rules, and one draw needn't show every extreme that they name: `step_counts`: some date has 2 steps and some date has 1.
All inputs are finite; a program needn't handle non-finite values.
Results may differ from a plain program's by a relative error of at most 0.02.
Values may be sent and summed in bfloat16 or wider, within the bound.
A program may use at most 448 MiB of HBM per device.

v0:
```python
from functools import partial
import math

import jax
import jax.numpy as jnp
import numpy as np
from jax import lax
from jax.sharding import PartitionSpec as P

D = 641
HID = 1282
NOISE = 8
NLAT = 48
NLON = 72
LDEG = 48
ORDERS = 36
STEPS = 2


HIGHEST = lax.Precision.HIGHEST


def shortened(shard):
    return jax.tree.map(lambda a: a.astype(jnp.bfloat16) if a.dtype == jnp.float32 else a, shard)


def legendre_values(lat_total, degree_total, order_total):
    colatitude = np.pi * (np.arange(lat_total) + 0.5) / lat_total
    cosine = np.cos(colatitude)
    sine_part = np.sin(colatitude)
    legendre = np.zeros((lat_total, degree_total, order_total))
    diagonal = np.full(lat_total, 1.0 / math.sqrt(4.0 * math.pi))
    for column in range(order_total):
        if column > 0:
            diagonal = diagonal * math.sqrt((2.0 * column + 1.0) / (2.0 * column)) * sine_part
        legendre[:, column, column] = diagonal
        legendre[:, column + 1, column] = math.sqrt(2.0 * column + 3.0) * cosine * diagonal
        for degree in range(column + 2, degree_total):
            factor_one = math.sqrt(
                (4.0 * degree * degree - 1.0) / (degree * degree - column * column)
            )
            factor_two = math.sqrt(
                ((degree - 1.0) ** 2 - column * column) / (4.0 * (degree - 1.0) ** 2 - 1.0)
            )
            legendre[:, degree, column] = factor_one * (
                cosine * legendre[:, degree - 1, column]
                - factor_two * legendre[:, degree - 2, column]
            )
    return (colatitude, legendre)


def spectral_tables(lat_total, lon_total, degree_total, order_total):
    colatitude, legendre = legendre_values(lat_total, degree_total, order_total)
    quadrature = np.sin(colatitude) * np.pi / lat_total
    angles = 2.0 * np.pi * np.outer(np.arange(lon_total), np.arange(order_total)) / lon_total
    fourier = np.concatenate([np.cos(angles), -np.sin(angles)], axis=1) * (2.0 * np.pi / lon_total)
    weights = np.where(np.arange(order_total) == 0, 1.0, 2.0)
    inverse = np.concatenate(
        [np.cos(angles).T * weights[:, None], -np.sin(angles).T * weights[:, None]], axis=0
    )
    doubled = np.concatenate([legendre, legendre], axis=2)
    analysis = doubled * quadrature[:, None, None]
    return tuple(
        (np.asarray(member, np.float32) for member in (fourier, inverse, analysis, doubled))
    )


def normalize(values, scale_gain, shift_vec):
    centered = values - jnp.mean(values, axis=-1, keepdims=True)
    inverse_scale = lax.rsqrt(jnp.mean(centered * centered, axis=-1, keepdims=True) + 1e-06)
    unit = centered * inverse_scale
    return (unit * scale_gain + shift_vec, unit, inverse_scale)


def normalize_back(upstream, unit, inverse_scale, scale_gain):
    scaled = upstream * scale_gain
    mean_one = jnp.mean(scaled, axis=-1, keepdims=True)
    mean_two = jnp.mean(scaled * unit, axis=-1, keepdims=True)
    grad_input = inverse_scale * (scaled - mean_one - unit * mean_two)
    return (grad_input, jnp.sum(upstream * unit, axis=(0, 1, 2)), jnp.sum(upstream, axis=(0, 1, 2)))


def unpack_mlp(flat):
    pieces = []
    offset = 0
    for length in (D, D, D, D, HID, D):
        pieces.append(flat[offset : offset + length].astype(jnp.float32))
        offset = offset + length
    w_in = flat[offset : offset + D * HID].reshape(D, HID)
    offset = offset + D * HID
    w_out = flat[offset : offset + HID * D].reshape(HID, D)
    return (tuple(pieces), w_in, w_out)


def build_weights(spectral_whole, mlp_whole, degrees_here):
    count_all = degrees_here * (D + NOISE) * D
    spectral = spectral_whole[0, :count_all].reshape(degrees_here, D + NOISE, D)
    vectors, w_in, w_out = unpack_mlp(mlp_whole)
    return (spectral, vectors, w_in, w_out)


def forward_step(current, noise_step, step_mask, tables, weights):
    (
        fourier,
        inverse,
        analysis_here,
        synthesis_here,
        analysis_rows,
        synthesis_rows,
        analysis_degrees,
        synthesis_degrees,
    ) = tables
    spectral, vectors, w_in, w_out = weights
    gain_one, shift_one, gain_two, shift_two, bias_hidden, bias_out = vectors
    normed, unit_one, scale_one = normalize(current, gain_one, shift_one)
    joined = jnp.concatenate([normed, noise_step], axis=-1)
    grid_modes = jnp.einsum("bjnc,nk->bjkc", joined, fourier, precision=HIGHEST)
    by_order = lax.all_to_all(
        shortened(grid_modes), "lat", split_axis=2, concat_axis=1, tiled=True
    ).astype(grid_modes.dtype)
    coeffs = jnp.einsum("jlk,bjkc->blkc", analysis_here, by_order, precision=HIGHEST).astype(
        jnp.bfloat16
    )
    by_degree = lax.all_to_all(coeffs, "lat", split_axis=1, concat_axis=2, tiled=True)
    mixed_modes = jnp.einsum(
        "blkc,lcd->blkd", by_degree, spectral, preferred_element_type=jnp.float32
    ).astype(jnp.bfloat16)
    mixed_orders = lax.all_to_all(mixed_modes, "lat", split_axis=2, concat_axis=1, tiled=True)
    lat_modes = jnp.einsum(
        "jlk,blkd->bjkd", synthesis_here, mixed_orders.astype(jnp.float32), precision=HIGHEST
    )
    lat_rows = lax.all_to_all(
        shortened(lat_modes), "lat", split_axis=1, concat_axis=2, tiled=True
    ).astype(lat_modes.dtype)
    branch = jnp.einsum("bjkd,kn->bjnd", lat_rows, inverse, precision=HIGHEST)
    middle = current + step_mask * branch
    normed_two, unit_two, scale_two = normalize(middle, gain_two, shift_two)
    hidden_in = normed_two.astype(jnp.bfloat16)
    preactivation = (
        jnp.einsum("bjnd,dh->bjnh", hidden_in, w_in, preferred_element_type=jnp.float32)
        + bias_hidden
    )
    active = jax.nn.gelu(preactivation, approximate=False).astype(jnp.bfloat16)
    result = (
        jnp.einsum("bjnh,hd->bjnd", active, w_out, preferred_element_type=jnp.float32) + bias_out
    )
    kept_values = (
        unit_one,
        scale_one,
        by_degree,
        unit_two,
        scale_two,
        hidden_in,
        preactivation,
        active,
    )
    return (middle + step_mask * result, kept_values)


def backward_step(grad_state, step_mask, kept_values, tables, weights):
    (
        fourier,
        inverse,
        analysis_here,
        synthesis_here,
        analysis_rows,
        synthesis_rows,
        analysis_degrees,
        synthesis_degrees,
    ) = tables
    spectral, vectors, w_in, w_out = weights
    gain_one, shift_one, gain_two, shift_two, bias_hidden, bias_out = vectors
    unit_one, scale_one, by_degree, unit_two, scale_two, hidden_in, preactivation, active = (
        kept_values
    )
    grad_result = (step_mask * grad_state).astype(jnp.bfloat16)
    grad_bias_out = jnp.sum(grad_result.astype(jnp.float32), axis=(0, 1, 2))
    grad_w_out = jnp.einsum(
        "bjnh,bjnd->hd", active, grad_result, preferred_element_type=jnp.float32
    )
    grad_active = jnp.einsum(
        "bjnd,hd->bjnh", grad_result, w_out, preferred_element_type=jnp.float32
    )
    unused, gelu_back = jax.vjp(partial(jax.nn.gelu, approximate=False), preactivation)
    grad_preact = gelu_back(grad_active)[0].astype(jnp.bfloat16)
    grad_bias_hidden = jnp.sum(grad_preact.astype(jnp.float32), axis=(0, 1, 2))
    grad_w_in = jnp.einsum(
        "bjnd,bjnh->dh", hidden_in, grad_preact, preferred_element_type=jnp.float32
    )
    grad_hidden_in = jnp.einsum(
        "bjnh,dh->bjnd", grad_preact, w_in, preferred_element_type=jnp.float32
    )
    grad_norm_two, grad_gain_two, grad_shift_two = normalize_back(
        grad_hidden_in, unit_two, scale_two, gain_two
    )
    grad_middle = grad_state + grad_norm_two
    grad_branch = step_mask * grad_middle
    grad_rows = jnp.einsum("bjnd,kn->bjkd", grad_branch, inverse, precision=HIGHEST)
    grad_modes = lax.all_to_all(
        shortened(grad_rows), "lat", split_axis=2, concat_axis=1, tiled=True
    ).astype(grad_rows.dtype)
    grad_mixed = jnp.einsum("jlk,bjkd->blkd", synthesis_here, grad_modes, precision=HIGHEST).astype(
        jnp.bfloat16
    )
    grad_degree = lax.all_to_all(grad_mixed, "lat", split_axis=1, concat_axis=2, tiled=True)
    grad_spectral = jnp.einsum(
        "blkc,blkd->lcd", by_degree, grad_degree, preferred_element_type=jnp.float32
    )
    grad_coeffs = jnp.einsum(
        "blkd,lcd->blkc", grad_degree, spectral, preferred_element_type=jnp.float32
    ).astype(jnp.bfloat16)
    grad_coeff_orders = lax.all_to_all(grad_coeffs, "lat", split_axis=2, concat_axis=1, tiled=True)
    grad_grid = jnp.einsum(
        "jlk,blkc->bjkc", analysis_here, grad_coeff_orders.astype(jnp.float32), precision=HIGHEST
    )
    grad_lat = lax.all_to_all(
        shortened(grad_grid), "lat", split_axis=1, concat_axis=2, tiled=True
    ).astype(grad_grid.dtype)
    model_width = grad_state.shape[3]
    grad_normed = jnp.einsum(
        "bjkc,nk->bjnc", grad_lat[..., :model_width], fourier, precision=HIGHEST
    )
    grad_norm_one, grad_gain_one, grad_shift_one = normalize_back(
        grad_normed, unit_one, scale_one, gain_one
    )
    vectors_grad = (
        grad_gain_one,
        grad_shift_one,
        grad_gain_two,
        grad_shift_two,
        grad_bias_hidden,
        grad_bias_out,
    )
    return (grad_middle + grad_norm_one, (grad_spectral, vectors_grad, grad_w_in, grad_w_out))


def shards(fields, noise_fields, step_counts, spectral_flat, mlp_flat, cotangent):
    lat_count = lax.axis_size("lat")
    lat_index = lax.axis_index("lat")
    dates_here = fields.shape[0]
    rows_here = fields.shape[1]
    degrees_here = LDEG // lat_count
    orders_here = 2 * ORDERS // lat_count
    fourier, inverse, analysis, synthesis = [
        jnp.asarray(member) for member in spectral_tables(NLAT, NLON, LDEG, ORDERS)
    ]
    analysis_here = lax.dynamic_slice_in_dim(analysis, lat_index * orders_here, orders_here, 2)
    synthesis_here = lax.dynamic_slice_in_dim(synthesis, lat_index * orders_here, orders_here, 2)
    analysis_rows = lax.dynamic_slice_in_dim(analysis, lat_index * rows_here, rows_here, 0)
    synthesis_rows = lax.dynamic_slice_in_dim(synthesis, lat_index * rows_here, rows_here, 0)
    analysis_degrees = lax.dynamic_slice_in_dim(analysis, lat_index * degrees_here, degrees_here, 1)
    synthesis_degrees = lax.dynamic_slice_in_dim(
        synthesis, lat_index * degrees_here, degrees_here, 1
    )
    tables = (
        fourier,
        inverse,
        analysis_here,
        synthesis_here,
        analysis_rows,
        synthesis_rows,
        analysis_degrees,
        synthesis_degrees,
    )
    spectral_whole = lax.all_gather(spectral_flat, "dp", axis=1, tiled=True)
    mlp_whole = lax.all_gather(mlp_flat, ("dp", "lat"), axis=0, tiled=True)
    weights = build_weights(spectral_whole, mlp_whole, degrees_here)
    noise_steps = noise_fields.astype(jnp.float32).reshape(
        dates_here, STEPS, rows_here, NLON, NOISE
    )
    current = fields.astype(jnp.float32)
    kept_steps = []
    for step_index in range(STEPS):
        step_mask = (step_index < step_counts).astype(jnp.float32).reshape(dates_here, 1, 1, 1)
        current, kept_values = forward_step(
            current, noise_steps[:, step_index], step_mask, tables, weights
        )
        kept_steps.append((step_mask, kept_values))
    output_fields = current.astype(jnp.bfloat16)
    grad_state = cotangent.astype(jnp.float32)
    totals = None
    for step_index in reversed(range(STEPS)):
        step_mask, kept_values = kept_steps[step_index]
        grad_state, step_totals = backward_step(grad_state, step_mask, kept_values, tables, weights)
        totals = step_totals if totals is None else jax.tree.map(jnp.add, totals, step_totals)
    grad_spectral, grad_vectors, grad_w_in, grad_w_out = totals
    spectral_pad = jnp.zeros((spectral_whole.shape[1] - grad_spectral.size,), jnp.float32)
    spectral_pack = jnp.concatenate([grad_spectral.reshape(-1), spectral_pad]).reshape(1, -1)
    spectral_grad = lax.psum_scatter(
        spectral_pack.astype(jnp.bfloat16), "dp", scatter_dimension=1, tiled=True
    ).astype(jnp.float32)
    mlp_members = list(grad_vectors) + [grad_w_in.reshape(-1), grad_w_out.reshape(-1)]
    used_total = sum((member.size for member in mlp_members))
    mlp_pack = jnp.concatenate(
        mlp_members + [jnp.zeros((mlp_whole.shape[0] - used_total,), jnp.float32)]
    )
    mlp_grad = lax.psum_scatter(mlp_pack, ("dp", "lat"), scatter_dimension=0, tiled=True)
    return (output_fields, grad_state.astype(jnp.bfloat16), spectral_grad, mlp_grad)


def solution(mesh):
    return jax.shard_map(
        shards,
        mesh=mesh,
        in_specs=(
            P("dp", "lat", None, None),
            P("dp", None, "lat", None),
            P("dp"),
            P("lat", "dp"),
            P(("dp", "lat")),
            P("dp", "lat", None, None),
        ),
        out_specs=(
            P("dp", "lat", None, None),
            P("dp", "lat", None, None),
            P("lat", "dp"),
            P(("dp", "lat")),
        ),
        check_vma=False,
    )
```

profile of v0, /device:TPU:1, one launch (start us, length us, event | category | flops | bytes accessed | tf_op | source)
XLA Modules:
  0.0 2957.7 jit_solution(8117630416735941478)
XLA Ops:
  15.2 69.6 %all-gather.6.cloned.1.call-done = bf16[32,1,51584]{2,1,0:T(2,128)(2,1)} async-done(((bf16[1,1,51584]{2,1,0:T(2,128)(2,1)}), bf16[32,1,51584]{2,1,0:T(2,128)(2,1)}) %all-gather.6.cloned.1.call-update) | async-done | bytes 3301392 | tf_op jit(solution)/shard_map/all_gather | solution.py:266
  84.8 21.9 reduce.30
  106.7 7.3 reshape.582
  117.3 6.6 convert_bitcast_fusion.15
  126.0 14.0 all-to-all-start
  140.0 30.5 %all-to-all-done = bf16[1,24,72,649]{3,1,0,2:T(8,128)(2,1)S(1)} async-done(((bf16[1,24,72,649]{3,1,0,2:T(8,128)(2,1)}), bf16[1,24,72,649]{3,1,0,2:T(8,128)(2,1)S(1)}, u32[]{:S(2)}, u32[]{:S(2)}) %all-to-all-start) | async-done | bytes 2242976 | tf_op jit(solution)/shard_map/all_to_all | solution.py:118
  180.7 33.1 %all-to-all-done.1 = bf16[1,48,36,649]{3,2,0,1:T(8,128)(2,1)S(1)} async-done(((bf16[1,48,36,649]{3,2,0,1:T(8,128)(2,1)}), bf16[1,48,36,649]{3,2,0,1:T(8,128)(2,1)S(1)}, u32[]{:S(2)}, u32[]{:S(2)}) %all-to-all-start.1) | async-done | bytes 2242976 | tf_op jit(solution)/shard_map/all_to_all | solution.py:124
  216.0 67.1 %all-gather.4.cloned.1.call-done = bf16[1,9986048]{1,0:T(2,128)(2,1)} async-done(((bf16[1,624128]{1,0:T(2,128)(2,1)}), bf16[1,9986048]{1,0:T(2,128)(2,1)}) %all-gather.4.cloned.1.call-update) | async-done | bytes 19972112 | tf_op jit(solution)/shard_map/all_gather | solution.py:265
  283.1 421.6 %slice_reduce_fusion = bf16[9984216]{0:T(1024)(128)(2,1)} fusion(bf16[1,9986048]{1,0:T(2,128)(2,1)} %all-gather.4.cloned.1.call-done), kind=kLoop, calls=%fused_computation.1 | loop fusion | bytes 39936864 | tf_op jit(solution)/shard_map/slice | solution.py:97
  704.7 128.4 %while.3 = (u32[]{:T(128)}, bf16[9984216]{0:T(1024)(128)(2,1)}, bf16[24,649,641]{2,1,0:T(8,128)(2,1)}, u32[]{}, u32[]{}, /*index=5*/u32[]{}, u32[]{}, u32[]{}) while((u32[]{:T(128)}, bf16[9984216]{0:T(1024)(128)(2,1)}, bf16[24,649,641]{2,1,0:T(8,128)(2,1)}, u32[]{}, u32[]{}, /*index=5*/u32[]{}, u32[]{}, u32[]{}) %tuple.67), condition=%wide.cond, body=%wide.body.sunk | while | flops 9 | bytes 10335601
  833.1 12.7 convert_bitcast_fusion.13
  853.9 28.7 all-to-all-done.2
  897.4 6.5 reshape.555
  909.9 17.2 all-to-all-done.3
  935.9 7.6 convert_reduce_fusion.3
  943.6 23.3 multiply_convert_fusion.1
  974.8 6.6 convert_bitcast_fusion.11
  982.0 31.7 %all_to_all.246 = bf16[1,24,72,649]{3,1,0,2:T(8,128)(2,1)S(1)} all-to-all(bf16[1,24,72,649]{3,1,0,2:T(8,128)(2,1)S(1)} %copy.169), channel_id=1, replica_groups=mesh['dp'=16,'lat'=2] {'lat'}, dimensions={2} | all-to-all | bytes 4485888 | tf_op jit(solution)/shard_map/all_to_all | solution.py:118
  1017.2 33.7 %all_to_all.247 = bf16[1,48,36,649]{3,2,0,1:T(8,128)(2,1)S(1)} all-to-all(bf16[1,48,36,649]{3,2,0,1:T(8,128)(2,1)S(1)} %copy.171), channel_id=1, replica_groups=mesh['dp'=16,'lat'=2] {'lat'}, dimensions={1} | all-to-all | bytes 4485888 | tf_op jit(solution)/shard_map/all_to_all | solution.py:124
  1051.6 12.9 convert_bitcast_fusion.9
  1065.0 29.7 %all_to_all.248 = bf16[1,24,72,641]{3,1,0,2:T(8,128)(2,1)S(1)} all-to-all(bf16[1,24,72,641]{3,1,0,2:T(8,128)(2,1)S(1)} %copy.176), channel_id=1, replica_groups=mesh['dp'=16,'lat'=2] {'lat'}, dimensions={2} | all-to-all | bytes 4430592 | tf_op jit(solution)/shard_map/all_to_all | solution.py:128
  1103.9 29.2 all-to-all-done.7
  1142.5 7.6 convert_reduce_fusion.1
  1150.1 23.5 multiply_convert_fusion
  1173.7 13.1 convert_reduce_fusion.5
  1186.8 7.7 fusion.34
  1196.2 7.8 convert_bitcast_fusion.7
  1204.5 28.0 all_to_all.249
  1236.1 30.0 %all_to_all.250 = bf16[1,48,36,641]{3,2,0,1:T(8,128)(2,1)S(1)} all-to-all(bf16[1,48,36,641]{3,2,0,1:T(8,128)(2,1)S(1)} %copy.188), channel_id=1, replica_groups=mesh['dp'=16,'lat'=2] {'lat'}, dimensions={1} | all-to-all | bytes 4430592 | tf_op jit(solution)/shard_map/all_to_all | solution.py:205
  1266.8 12.9 convert_bitcast_fusion.5
  1288.5 23.4 all-to-all-done.10
  1324.6 10.1 fusion.108
  1334.7 8.1 fusion.56
  1342.8 7.4 all-to-all-done.11
  1352.9 9.0 fusion.35
  1362.1 6.5 convert_reduce_fusion.7
  1368.6 14.9 convert_reduce_fusion.4
  1383.6 7.2 fusion.33
  1408.3 20.2 fusion.72
  1440.9 11.0 bitcast_add_fusion.4
  1460.1 9.9 bitcast_add_fusion.3
  1481.5 13.2 convert_bitcast_fusion.1
  1503.7 25.9 add_convert_fusion
  1542.1 433.5 %while.4 = (u32[]{:T(128)}, bf16[24,649,641]{1,2,0:T(8,128)(2,1)}, bf16[9984216]{0:T(1024)(128)(2,1)}, u32[]{}, u32[]{}, /*index=5*/u32[]{}, u32[]{}, u32[]{}) while((u32[]{:T(128)}, bf16[24,649,641]{1,2,0:T(8,128)(2,1)}, bf16[9984216]{0:T(1024)(128)(2,1)}, u32[]{}, u32[]{}, /*index=5*/u32[]{}, u32[]{}, u32[]{}) %tuple.70), condition=%wide.cond.1, body=%wide.body.1.sunk | while | flops 9 | bytes 13312477
  1552.3 26.0 dynamic-update-slice.8
  1588.3 26.1 dynamic-update-slice.8
  1624.4 26.1 dynamic-update-slice.8
  1660.6 26.1 dynamic-update-slice.8
  1696.7 26.1 dynamic-update-slice.8
  1732.8 26.0 dynamic-update-slice.8
  1768.9 26.1 dynamic-update-slice.8
  1805.0 26.2 dynamic-update-slice.8
  1841.2 26.1 dynamic-update-slice.8
  1877.3 26.0 dynamic-update-slice.8
  1913.3 26.1 dynamic-update-slice.8
  1949.4 26.2 dynamic-update-slice.8
  1975.6 19.2 concatenate.14
  1997.5 7.5 fusion.24
  2008.5 53.2 %concatenate.15 = f32[1650688]{0:T(1024)} concatenate(f32[641]{0:T(1024)S(1)} %add.179, f32[641]{0:T(1024)S(1)} %add.180, f32[641]{0:T(1024)S(1)} %add.181, f32[641]{0:T(1024)S(1)} %add.182, f32[1282]{0:T(1024)S(1)} %add.183, f32[641]{0:T(1024)S(1)} %add.184, f32[821762]{0:T(1024)} %reshape.575, f32[821762]{0:T(1024)S(1)} %copy-done.14, f32[2677]{0:T(1024)S(1)} %broadcast_in_dim.2), dimensions={0} | concatenate | bytes 13205504 | tf_op jit(solution)/shard_map/concatenate | solution.py:294
  2061.8 207.4 %while.2 = (u32[]{:T(128)}, bf16[9986048]{0:T(1024)(128)(2,1)}, bf16[1,1,9986048]{2,1,0:T(2,128)(2,1)}) while((u32[]{:T(128)}, bf16[9986048]{0:T(1024)(128)(2,1)}, bf16[1,1,9986048]{2,1,0:T(2,128)(2,1)}) %tuple.73), condition=%cond.2, body=%body.2 | while | flops 9 | bytes 79888528
  2062.0 16.9 dynamic-slice.6
  2078.9 190.3 %reshape_dynamic-update-slice_fusion = bf16[1,1,9986048]{2,1,0:T(2,128)(2,1)} fusion(bf16[1,1,9986048]{2,1,0:T(2,128)(2,1)} %get-tuple-element.184, u32[]{:T(128)S(6)} %multiply.108, u32[]{:T(128)S(6)} %multiply.109, bf16[9986048]{0:T(1024)(128)(2,1)} %dynamic-slice.6), kind=kLoop, calls=%fused_computation.223 | loop fusion | bytes 39944200
  2271.2 9.9 fusion.45
  2286.1 659.0 %all-reduce.6.cloned.1.call-done = bf16[1,9986048]{1,0:T(2,128)(2,1)} async-done(((bf16[1,9986048]{1,0:T(2,128)(2,1)}), bf16[1,9986048]{1,0:T(2,128)(2,1)}) %all-reduce.6.cloned.1.call-update) | async-done | bytes 19972112
  (357 shorter events, 461.8 us)
Async XLA Ops:
  7.2 5.8 copy-start.2
  7.2 77.6 %all-gather.6.cloned.1.call-start = ((), (), s32[]{:S(2)}) async-start(), calls=%async_computation.17 | async-start | bytes 6809088 | tf_op jit(solution)/shard_map/all_gather | solution.py:266
  9.1 274.0 %all-gather.4.cloned.1.call-start = ((), (), s32[]{:S(2)}) async-start(), calls=%async_computation.16 | async-start | bytes 42440704 | tf_op jit(solution)/shard_map/all_gather | solution.py:265
  13.5 101.9 %copy-start.41 = (f32[24,72]{1,0:T(8,128)}, f32[24,72]{1,0:T(8,128)S(1)}, u32[]{:S(2)}) copy-start(f32[24,72]{1,0:T(8,128)S(1)} %broadcast_multiply_fusion.11) | copy-start | bytes 20740
  126.0 44.5 %all-to-all-start = ((bf16[1,24,72,649]{3,1,0,2:T(8,128)(2,1)}), bf16[1,24,72,649]{3,1,0,2:T(8,128)(2,1)S(1)}, u32[]{:S(2)}, u32[]{:S(2)}) async-start(bf16[1,24,72,649]{3,1,0,2:T(8,128)(2,1)} %copy.154), calls=%async_computation | async-start | bytes 5308416 | tf_op jit(solution)/shard_map/all_to_all | solution.py:118
  176.8 37.0 %all-to-all-start.1 = ((bf16[1,48,36,649]{3,2,0,1:T(8,128)(2,1)}), bf16[1,48,36,649]{3,2,0,1:T(8,128)(2,1)S(1)}, u32[]{:S(2)}, u32[]{:S(2)}) async-start(bf16[1,48,36,649]{3,2,0,1:T(8,128)(2,1)} %copy.156), calls=%async_computation.1 | async-start | bytes 5898240 | tf_op jit(solution)/shard_map/all_to_all | solution.py:124
  845.9 6.7 copy-start.36
  847.9 34.7 %all-to-all-start.2 = ((bf16[1,24,72,641]{3,1,0,2:T(8,128)(2,1)}), bf16[1,24,72,641]{3,1,0,2:T(8,128)(2,1)S(1)}, u32[]{:S(2)}, u32[]{:S(2)}) async-start(bf16[1,24,72,641]{3,1,0,2:T(8,128)(2,1)} %copy.161), calls=%async_computation.2 | async-start | bytes 5308416 | tf_op jit(solution)/shard_map/all_to_all | solution.py:128
  886.4 7.7 copy-start.13
  889.0 38.2 %all-to-all-start.3 = ((bf16[1,48,36,641]{3,2,0,1:T(8,128)(2,1)}), bf16[1,48,36,641]{3,2,0,1:T(8,128)(2,1)}, u32[]{:S(2)}, u32[]{:S(2)}) async-start(bf16[1,48,36,641]{3,2,0,1:T(8,128)(2,1)} %copy.163), calls=%async_computation.3 | async-start | bytes 5898240 | tf_op jit(solution)/shard_map/all_to_all | solution.py:132
  909.9 19.8 copy-start.3
  909.9 19.8 copy-start.37
  933.1 33.8 %copy-start.7 = (f32[1,24,72,641]{3,2,1,0:T(8,128)}, f32[1,24,72,641]{3,2,1,0:T(8,128)S(1)}, u32[]{:S(2)}) copy-start(f32[1,24,72,641]{3,2,1,0:T(8,128)S(1)} %get-tuple-element.73) | copy-start | bytes 13291780
  933.1 10.4 copy-start.48
  934.0 9.6 copy-start.52
  943.5 23.4 copy-start.18
  943.6 23.4 copy-start.30
  943.6 23.4 copy-start.61
  966.9 5.2 copy-start.28
  982.0 31.9 %copy-start.21 = (f32[48,48,72]{0,1,2:T(8,128)S(1)}, f32[48,48,72]{0,1,2:T(8,128)}, u32[]{:S(2)}) copy-start(f32[48,48,72]{0,1,2:T(8,128)} %constant.111.clone) | copy-start | bytes 1990660
  1051.6 12.9 copy-start.11
  1065.0 29.9 %copy-start.25 = (f32[48,48,72]{1,0,2:T(8,128)S(1)}, f32[48,48,72]{1,0,2:T(8,128)}, u32[]{:S(2)}) copy-start(f32[48,48,72]{1,0,2:T(8,128)} %constant.112.clone) | copy-start | bytes 1990660
  1099.8 33.3 %all-to-all-start.7 = ((bf16[1,48,36,641]{3,2,0,1:T(8,128)(2,1)}), bf16[1,48,36,641]{3,2,0,1:T(8,128)(2,1)S(1)}, u32[]{:S(2)}, u32[]{:S(2)}) async-start(bf16[1,48,36,641]{3,2,0,1:T(8,128)(2,1)} %copy.178), calls=%async_computation.7 | async-start | bytes 5898240 | tf_op jit(solution)/shard_map/all_to_all | solution.py:132
  1139.7 56.5 %copy-start.1 = (f32[1,24,72,641]{3,2,1,0:T(8,128)}, f32[1,24,72,641]{3,2,1,0:T(8,128)S(1)}, u32[]{:S(2)}) copy-start(f32[1,24,72,641]{3,2,1,0:T(8,128)S(1)} %get-tuple-element.78) | copy-start | bytes 13291780
  1150.1 23.6 copy-start.19
  1150.1 23.5 copy-start.15
  1150.1 23.5 copy-start.31
  1194.5 9.5 copy-start.6
  1204.5 28.2 copy-start.26
  1283.4 28.5 all-to-all-start.10
  1319.2 31.0 %all-to-all-start.11 = ((bf16[1,48,36,649]{3,2,0,1:T(8,128)(2,1)}), bf16[1,48,36,649]{3,2,0,1:T(8,128)(2,1)}, u32[]{:S(2)}, u32[]{:S(2)}) async-start(bf16[1,48,36,649]{3,2,0,1:T(8,128)(2,1)} %copy.196), calls=%async_computation.11 | async-start | bytes 5898240 | tf_op jit(solution)/shard_map/all_to_all | solution.py:216
  1324.6 10.1 copy-start.16
  1350.2 11.8 slice-start.4
  1352.7 9.3 slice-start
  1352.7 9.3 slice-start.2
  1352.9 9.1 slice-start.1
  1352.9 9.1 slice-start.3
  1352.9 9.1 slice-start.5
  1352.9 9.1 copy-start.17
  1362.0 6.6 copy-start.8
  1362.1 21.5 slice-start.6
  1368.6 15.0 slice-start.7
  1368.6 15.0 copy-start.35
  1368.6 15.0 copy-start.49
  1368.6 15.0 copy-start.53
  1383.6 8.0 slice-start.8
  1383.6 8.0 slice-start.9
  1403.3 26.5 all-to-all-start.12
  1436.8 44.0 %all-to-all-start.13 = ((bf16[1,48,36,641]{3,2,0,1:T(8,128)(2,1)}), bf16[1,48,36,641]{3,2,0,1:T(8,128)(2,1)S(1)}, u32[]{:S(2)}, u32[]{:S(2)}) async-start(bf16[1,48,36,641]{3,2,0,1:T(8,128)(2,1)} %copy.206), calls=%async_computation.13 | async-start | bytes 5898240 | tf_op jit(solution)/shard_map/all_to_all | solution.py:205
  1475.0 5.7 copy-start.60
  1475.0 5.7 copy-start.64
  1475.1 5.7 copy-start.57
  1498.6 30.9 %all-to-all-start.14 = ((bf16[1,24,72,649]{3,1,0,2:T(8,128)(2,1)}), bf16[1,24,72,649]{3,1,0,2:T(8,128)(2,1)}, u32[]{:S(2)}, u32[]{:S(2)}) async-start(bf16[1,24,72,649]{3,1,0,2:T(8,128)(2,1)} %copy.211), calls=%async_computation.14 | async-start | bytes 5308416 | tf_op jit(solution)/shard_map/all_to_all | solution.py:212
  1536.8 458.0 %all-to-all-start.15 = ((bf16[1,48,36,649]{3,2,0,1:T(8,128)(2,1)}), bf16[1,48,36,649]{3,2,0,1:T(8,128)(2,1)}, u32[]{:S(2)}, u32[]{:S(2)}) async-start(bf16[1,48,36,649]{3,2,0,1:T(8,128)(2,1)} %copy.214), calls=%async_computation.15 | async-start | bytes 5898240 | tf_op jit(solution)/shard_map/all_to_all | solution.py:216
  1542.0 742.3 %all-reduce.8.cloned.1.call-start = ((), (), s32[]{:S(2)}) async-start(), calls=%async_computation.19 | async-start | bytes 13205504
  2061.8 883.4 %all-reduce.6.cloned.1.call-start = ((), (), s32[]{:S(2)}) async-start(), calls=%async_computation.18 | async-start | bytes 79888384
  2271.1 10.0 copy-start.59
  2271.1 10.0 copy-start.58
  2271.1 10.0 copy-start.5
  2271.1 10.0 copy-start.10
  2271.1 10.0 copy-start.12
  2271.1 10.0 copy-start.43
  2271.1 10.0 copy-start.47
  2271.1 10.0 copy-start.51
  (27 other events, 61.0 us)
Sparse Core Ops, SparseCore 0:
  11.4 73.3 all-gather.5
  86.4 196.6 all-gather.3
  2061.9 169.9 all-reduce.7
  2269.3 675.7 all-reduce.5
where the time goes:
time: 3010 us; the launch traced here: 2960 us
  local copies, waits for them, and re-layouts  1370 us (46%)
  waiting for transfers between devices  967 us (32%)
  matrix products  281 us (9%)
  blocking collectives  153 us (5%)
  other arithmetic  104 us (3%)
  starting transfers between devices  61.2 us (2%)
    unnamed x244, local copies, waits for them, and re-layouts  794 us
    unnamed x6, waiting for transfers between devices  660 us
    slice x1, local copies, waits for them, and re-layouts, build_weights(): spectral = spectral_whole[0, :count_all].reshape(degrees_here, D + NOISE, D)  422 us
    all_gather x1, waiting for transfers between devices, shards(): mlp_whole = lax.all_gather(mlp_flat, ('dp', 'lat'), axis=0, tiled=True)  69.6 us
    all_gather x1, waiting for transfers between devices, shards(): spectral_whole = lax.all_gather(spectral_flat, 'dp', axis=1, tiled=True)  67.1 us
  transfers between devices with their start and end apart: 15, of which 11 were waited for; matrix products, arithmetic and copies ran while one was open for 29% of the time, Pallas kernels for 0%

commit v1 on v0

--- a/solution.py
+++ b/solution.py
@@ -5,6 +5,8 @@
 import jax.numpy as jnp
 import numpy as np
 from jax import lax
+from jax.experimental import pallas as pl
+from jax.experimental.pallas import tpu as pltpu
 from jax.sharding import PartitionSpec as P
 
 D = 641
@@ -15,7 +17,7 @@
 LDEG = 48
 ORDERS = 36
 STEPS = 2
-
+CIN = D + NOISE
 
 HIGHEST = lax.Precision.HIGHEST
 
@@ -234,7 +236,7 @@
     return (grad_middle + grad_norm_one, (grad_spectral, vectors_grad, grad_w_in, grad_w_out))
 
 
-def shards(fields, noise_fields, step_counts, spectral_flat, mlp_flat, cotangent):
+def shards_general(fields, noise_fields, step_counts, spectral_flat, mlp_flat, cotangent):
     lat_count = lax.axis_size("lat")
     lat_index = lax.axis_index("lat")
     dates_here = fields.shape[0]
@@ -298,9 +300,1007 @@
     return (output_fields, grad_state.astype(jnp.bfloat16), spectral_grad, mlp_grad)
 
 
+ROWS = NLAT // 2
+DEGS = LDEG // 2
+CELLS = ROWS * NLON
+DP = 768
+HP = 1408
+KP = 80
+GROUPS = 5
+GK = 16
+WROWS = 672
+BLK = 4
+BC = BLK * NLON
+WIN = 992
+MAIN = 944
+HEAD = 480
+BF = jnp.bfloat16
+F32 = jnp.float32
+MB = 2**20
+
+
+def params(limit=60, **more):
+    return pltpu.CompilerParams(vmem_limit_bytes=limit * MB, **more)
+
+
+def vspec():
+    return pl.BlockSpec(memory_space=pltpu.VMEM)
+
+
+def dot(a, b):
+    return jnp.dot(a, b, preferred_element_type=F32)
+
+
+def split_table(table):
+    high = table.astype(BF).astype(np.float32)
+    return np.concatenate([high, table - high, high], axis=1).astype(BF)
+
+
+def split_dot(table, value):
+    high = value.astype(BF).astype(F32)
+    return dot(table, jnp.concatenate([high, high, value - high], axis=0).astype(BF))
+
+
+def dot_nt(a, b):
+    return lax.dot_general(a, b, (((1,), (1,)), ((), ())), preferred_element_type=F32)
+
+
+def dot_tn(a, b):
+    return lax.dot_general(a, b, (((0,), (0,)), ((), ())), preferred_element_type=F32)
+
+
+def column_order():
+    places = -np.ones(KP, np.int64)
+    for group in range(GROUPS):
+        for i in range(8):
+            order = 8 * group + i
+            if order < ORDERS:
+                places[GK * group + i] = order
+                places[GK * group + 8 + i] = ORDERS + order
+    return places
+
+
+def plan_tables():
+    fourier, inverse, analysis, synthesis = spectral_tables(NLAT, NLON, LDEG, ORDERS)
+    places = column_order()
+    held = places >= 0
+    take = np.where(held, places, 0)
+    fourier = fourier[:, take] * held
+    inverse = inverse[take, :] * held[:, None]
+    analysis = analysis[:, :, take] * held
+    synthesis = synthesis[:, :, take] * held
+    eye = np.eye(GK, dtype=np.float32)
+
+    def blocks(table):
+        out = np.zeros((2, 2, GROUPS, 384, 384), np.float32)
+        for own in range(2):
+            for which in range(2):
+                half = own if which == 0 else 1 - own
+                for group in range(GROUPS):
+                    part = table[24 * own : 24 * own + 24, 24 * half : 24 * half + 24]
+                    part = part[:, :, GK * group : GK * group + GK]
+                    full = np.einsum("pqi,ij->piqj", part, eye)
+                    out[own, which, group] = full.reshape(384, 384)
+        return out.astype(BF)
+
+    by_degree = np.transpose
+    return dict(
+        fourier_t=split_table(fourier.T),
+        fourier=split_table(fourier),
+        inverse_t=split_table(inverse.T),
+        inverse=split_table(inverse),
+        analyse=blocks(by_degree(analysis, (1, 0, 2))),
+        synthesize=blocks(synthesis),
+        analyse_back=blocks(analysis),
+        synthesize_back=blocks(by_degree(synthesis, (1, 0, 2))),
+    )
+
+
+def rows_out(flat_ref, start, offset, step, wide, tiles, tail, put, count, unroll=4):
+    lane = lax.broadcasted_iota(jnp.int32, (8, 128), 1)
+
+    def one(t, carry):
+        shift = offset + step * t
+        jump = shift // 128
+        shift = shift - 128 * jump
+        amount = (128 - shift) % 128
+        low = lane + shift < 128
+        pieces = [
+            pltpu.roll(flat_ref[pl.ds(start + wide * t + jump + m, 8, stride=641), :], amount, 1)
+            for m in range(tiles + 1)
+        ]
+        for m in range(tiles):
+            piece = jnp.where(low, pieces[m], pieces[m + 1])
+            if m == tiles - 1:
+                piece = jnp.where(lane < tail, piece, 0.0)
+            put(m, t, piece)
+        return carry
+
+    lax.fori_loop(0, count, one, 0, unroll=unroll)
+
+
+def rows_in(flat_ref, start, offset, step, wide, tiles, get, count, unroll=2):
+    lane = lax.broadcasted_iota(jnp.int32, (8, 128), 1)
+
+    def one(t, carry):
+        shift = offset + step * t
+        jump = shift // 128
+        shift = shift - 128 * jump
+        high = lane >= shift
+        pieces = [pltpu.roll(get(m, t), shift, 1) for m in range(tiles)]
+        last = tiles + (1 if step > 1 else 0)
+        for m in range(last):
+            here = pieces[m] if m < tiles else jnp.zeros((8, 128), F32)
+            before = pieces[m - 1] if m > 0 else jnp.zeros((8, 128), F32)
+            piece = jnp.where(high, here, before)
+            where = pl.ds(start + wide * t + jump + m, 8, stride=641)
+            if m == 0 or m >= tiles - 1:
+                flat_ref[where, :] = flat_ref[where, :] + piece
+            else:
+                flat_ref[where, :] = piece
+        return carry
+
+    lax.fori_loop(0, count, one, 0, unroll=unroll)
+
+
+def shard_place(shard, length):
+    first = (shard * length) // D
+    base = (first // 16) * 16
+    start = D * base - length * shard + 128 * 88
+    return base, start // 128, start % 128
+
+
+def window_kernel(length, shard_ref, flat_ref, main_ref, side_ref, flat, tiles, extra):
+    chunks = length // 128
+    base, start, offset = shard_place(shard_ref[0], length)
+    flat[0:88, :] = jnp.zeros((88, 128), F32)
+    flat[88 + chunks :, :] = jnp.zeros((flat.shape[0] - 88 - chunks, 128), F32)
+
+    def load(i, carry):
+        piece = flat_ref[:, pl.ds(pl.multiple_of(1024 * i, 1024), 1024)]
+        flat[pl.ds(pl.multiple_of(88 + 8 * i, 8), 8), :] = piece.astype(F32).reshape(8, 128)
+        return carry
+
+    lax.fori_loop(0, chunks // 8, load, 0, unroll=7)
+    rest = chunks % 8
+    if rest:
+        piece = flat_ref[:, 128 * (chunks - rest) :].astype(F32).reshape(rest, 128)
+        flat[88 + chunks - rest : 88 + chunks, :] = piece
+    lane = lax.broadcasted_iota(jnp.int32, (8, 128), 1)
+    extra[...] = jnp.zeros_like(extra)
+
+    def put(m, t, piece):
+        if m < 5:
+            tiles[m, pl.ds(t, 8, stride=128), :] = piece
+        else:
+            extra[...] = jnp.where(lane == t, piece[:, 0:1], extra[...])
+
+    rows_out(flat, start, offset, 1, 5, 6, 1, put, 128)
+    side_ref[48:64, :] = jnp.zeros((16, 640), BF)
+    side_ref[48:64, 0:128] = jnp.concatenate([extra[...], jnp.zeros((8, 128), F32)], axis=0).astype(BF)
+    for m in range(5):
+        at = slice(128 * m, 128 * m + 128)
+        main_ref[:, at] = tiles[m, 16 : 16 + MAIN, :].astype(BF)
+        side_ref[0:16, at] = tiles[m, 0:16, :].astype(BF)
+        side_ref[16:48, at] = tiles[m, 16 + MAIN : WIN, :].astype(BF)
+
+
+def spectral_window(shard, flat):
+    length = flat.shape[1]
+    return pl.pallas_call(
+        partial(window_kernel, length),
+        out_shape=(jax.ShapeDtypeStruct((MAIN, 640), BF), jax.ShapeDtypeStruct((64, 640), BF)),
+        in_specs=[pl.BlockSpec(memory_space=pltpu.SMEM), vspec()],
+        out_specs=(vspec(), vspec()),
+        scratch_shapes=[
+            pltpu.VMEM((5256, 128), F32),
+            pltpu.VMEM((5, 1024, 128), F32),
+            pltpu.VMEM((8, 128), F32),
+        ],
+        compiler_params=params(),
+    )(shard, flat)
+
+
+VECTORS = ((0, D), (D, D), (2 * D, D), (3 * D, D), (4 * D, HID), (4 * D + HID, D))
+IN_AT = 5 * D + HID
+OUT_AT = IN_AT + D * HID
+
+
+def mlp_kernel(flat_ref, in_ref, out_ref, vec_ref, flat, tin, tout):
+    count = flat_ref.shape[0]
+    flat[0:count, :] = flat_ref[...].astype(F32)
+    lane = lax.broadcasted_iota(jnp.int32, (1, 128), 1)
+    vec_ref[...] = jnp.zeros_like(vec_ref)
+    for row, (place, length) in enumerate(VECTORS):
+        first, shift = place // 128, place % 128
+        for m in range(-(-length // 128)):
+            one = flat[first + m : first + m + 1, :]
+            two = flat[first + m + 1 : first + m + 2, :]
+            if shift:
+                one = pltpu.roll(one, 128 - shift, 1)
+                two = pltpu.roll(two, 128 - shift, 1)
+            piece = jnp.where(lane + shift < 128, one, two)
+            piece = jnp.where(lane + 128 * m < length, piece, 0.0)
+            vec_ref[row : row + 1, 128 * m : 128 * m + 128] = piece
+    for part in range(2):
+
+        def put_in(m, t, piece, part=part):
+            tin[m, pl.ds(t + 512 * part, 8, stride=64), :] = piece
+
+        rows_out(flat, IN_AT // 128 + 641 * 8 * part, IN_AT % 128, 2, 10, 11, 2, put_in, 64, 2)
+
+        def put_out(m, t, piece, part=part):
+            tout[m, pl.ds(t + 1024 * part, 8, stride=128), :] = piece
+
+        rows_out(flat, OUT_AT // 128 + 641 * 8 * part, OUT_AT % 128, 1, 5, 6, 1, put_out, 128, 4)
+    keep = lax.broadcasted_iota(jnp.int32, (DP, 128), 0) < D
+    for m in range(11):
+        in_ref[:, 128 * m : 128 * m + 128] = jnp.where(keep, tin[m, :DP, :], 0.0).astype(BF)
+    keep = lax.broadcasted_iota(jnp.int32, (HP, 128), 0) < HID
+    for m in range(6):
+        out_ref[:, 128 * m : 128 * m + 128] = jnp.where(keep, tout[m, :HP, :], 0.0).astype(BF)
+
+
+def mlp_weights(flat):
+    return pl.pallas_call(
+        mlp_kernel,
+        out_shape=(
+            jax.ShapeDtypeStruct((DP, HP), BF),
+            jax.ShapeDtypeStruct((HP, DP), BF),
+            jax.ShapeDtypeStruct((8, HP), F32),
+        ),
+        in_specs=[vspec()],
+        out_specs=(vspec(), vspec(), vspec()),
+        scratch_shapes=[
+            pltpu.VMEM((16776, 128), F32),
+            pltpu.VMEM((11, 1024, 128), F32),
+            pltpu.VMEM((6, 2048, 128), F32),
+        ],
+        compiler_params=params(),
+    )(flat)
+
+
+ALL_ROWS = 15584
+CHIPS = 8
+
+
+def cuts(length, count):
+    return [((s * length) // D) // 16 * 16 for s in range(count)] + [ALL_ROWS]
+
+
+def gather_kernel(length, main_ref, side_ref, w_ref, column_ref, sides, edges, line, ring, over, arrive, local):
+    dp = lax.axis_index("dp")
+    lat = lax.axis_index("lat")
+    core = dp % 2
+    chip = dp // 2
+    z = chip // 2
+    x = chip % 2
+    place = z + x * (7 - 2 * z)
+    home = lat == core
+    count = 2 * CHIPS
+
+    def chip_at(p):
+        p = (p + CHIPS) % CHIPS
+        back = p // 4
+        return ((1 - back) * p + back * (7 - p)) * 2 + back
+
+    def device(p, which):
+        return (chip_at(p) * 2 + which, lat)
+
+    def shard(p, which):
+        return chip_at(p) * 2 + which
+
+    across = (dp, 1 - lat)
+    partner = (dp + 1 - 2 * core, lat)
+    barrier = pltpu.get_barrier_semaphore()
+    for who in (device(place + 1, core), device(place - 1, core), across, partner):
+        pl.semaphore_signal(barrier, inc=1, device_id=who, device_id_type=pl.DeviceIdType.MESH)
+    pl.semaphore_wait(barrier, 4)
+
+    def rows_of(s, first, size):
+        start = ((s * length) // D) // 16 * 16 + 16 + first
+        return w_ref.at[pl.ds(pl.multiple_of(start, 16), size)]
+
+    def remote(src, dst, send, recv, who):
+        return pltpu.make_async_remote_copy(
+            src_ref=src, dst_ref=dst, send_sem=send, recv_sem=recv, device_id=who,
+            device_id_type=pl.DeviceIdType.MESH,
+        )
+
+    first = core
+    second = 1 - core
+    hops = {1: [(0, 0), (0, 1), (1, 0), (1, 1), (2, 0), (2, 1), (3, 0)],
+            -1: [(0, 0), (0, 1), (1, 0), (1, 1), (2, 0), (2, 1), (3, 1)]}
+    coming = [(way, d, w) for d in (1, 2, 3) for w in (0, 1) for way in (1, -1)] + [(1, 4, 0), (-1, 4, 1)]
+
+    def named(way, d, w):
+        which = first if w == 0 else second
+        return shard(place - way * d, which)
+
+    def wait_part(kind, s, size):
+        remote(rows_of(s, 0, size), rows_of(s, 0, size), local.at[0], arrive.at[kind, s], across).wait_recv()
+
+    def wait_side(s):
+        remote(sides.at[s], sides.at[s], local.at[0], arrive.at[2, s], across).wait_recv()
+
+    own = dp
+
+    @pl.when(home)
+    def _():
+        keep = pltpu.make_async_copy(main_ref, rows_of(own, 0, MAIN), local.at[0])
+        keep.start()
+        keep_side = pltpu.make_async_copy(side_ref, sides.at[own], local.at[1])
+        keep_side.start()
+        sent = []
+
+        def send(way, hop, s, main, side):
+            to = device(place + way, core)
+            lane = 0 if way == 1 else 1
+            copies = (
+                remote(main, rows_of(s, 0, MAIN), ring.at[lane, hop], arrive.at[0, s], to),
+                remote(side, sides.at[s], ring.at[lane + 2, hop], arrive.at[2, s], to),
+            )
+            for copy in copies:
+                copy.start()
+                sent.append(copy)
+
+        def cross(index, s, main, side):
+            copies = [remote(main(0, HEAD), rows_of(s, 0, HEAD), over.at[0, index], arrive.at[1, s], across)]
+            copies.append(remote(side, sides.at[s], over.at[1, index], arrive.at[2, s], across))
+            if index < 2:
+                copies.insert(
+                    0,
+                    remote(
+                        main(HEAD, MAIN - HEAD), rows_of(s, HEAD, MAIN - HEAD), over.at[2, index],
+                        arrive.at[0, s], across,
+                    ),
+                )
+            for copy in copies:
+                copy.start()
+                sent.append(copy)
+
+        send(1, 0, own, main_ref, side_ref)
+        send(-1, 0, own, main_ref, side_ref)
+        cross(0, own, lambda at, size: main_ref.at[pl.ds(at, size)], side_ref)
+        mate = dp + 1 - 2 * core
+        wait_part(0, mate, MAIN)
+        wait_side(mate)
+        held = lambda s: (lambda at, size: rows_of(s, at, size))
+        send(1, 1, mate, rows_of(mate, 0, MAIN), sides.at[mate])
+        send(-1, 1, mate, rows_of(mate, 0, MAIN), sides.at[mate])
+        cross(1, mate, held(mate), sides.at[mate])
+        for index, (way, d, w) in enumerate(coming):
+            s = named(way, d, w)
+            wait_part(0, s, MAIN)
+            wait_side(s)
+            if (d, w) in hops[way]:
+                send(way, hops[way].index((d, w)), s, rows_of(s, 0, MAIN), sides.at[s])
+            cross(2 + index, s, held(s), sides.at[s])
+        for copy in sent:
+            copy.wait_send()
+        keep.wait()
+        keep_side.wait()
+
+    @pl.when(jnp.logical_not(home))
+    def _():
+        sent = [
+            remote(main_ref, rows_of(own, 0, MAIN), ring.at[4, 0], arrive.at[0, own], partner),
+            remote(side_ref, sides.at[own], ring.at[4, 1], arrive.at[2, own], partner),
+        ]
+        for copy in sent:
+            copy.start()
+        size = MAIN - HEAD
+
+        def send(way, hop, s):
+            lane = 0 if way == 1 else 1
+            copy = remote(
+                rows_of(s, HEAD, size), rows_of(s, HEAD, size), ring.at[lane, hop], arrive.at[0, s],
+                device(place + way, core),
+            )
+            copy.start()
+            sent.append(copy)
+
+        mate = dp + 1 - 2 * core
+        wait_part(0, own, size)
+        send(1, 0, own)
+        send(-1, 0, own)
+        wait_part(0, mate, size)
+        send(1, 1, mate)
+        send(-1, 1, mate)
+        for way, d, w in coming:
+            s = named(way, d, w)
+            wait_part(0, s, size)
+            if (d, w) in hops[way]:
+                send(way, hops[way].index((d, w)), s)
+        for s in [own, mate] + [named(*one) for one in coming]:
+            wait_part(1, s, HEAD)
+            wait_side(s)
+        for copy in sent:
+            copy.wait_send()
+
+    places = cuts(length, count)
+    copies = []
+    for s in range(count):
+        span = places[s + 1] - places[s]
+        edge = sides[s, 0:16, :]
+        if s:
+            before = places[s] - places[s - 1] - 16 - MAIN
+            edge = edge + sides[s - 1, 16 + before : 32 + before, :]
+        edges[s] = edge
+        copies.append(pltpu.make_async_copy(edges.at[s], w_ref.at[pl.ds(places[s], 16)], local.at[2 + s]))
+        left = span - 16 - MAIN
+        if left:
+            copies.append(
+                pltpu.make_async_copy(
+                    sides.at[s, pl.ds(16, left)], w_ref.at[pl.ds(places[s] + 16 + MAIN, left)],
+                    local.at[2 + count + s],
+                )
+            )
+    for copy in copies:
+        copy.start()
+    lane = lax.broadcasted_iota(jnp.int32, (8, 128), 1)
+    line[...] = jnp.zeros_like(line)
+    for s in range(count):
+        a, b = places[s] // 128, places[s] % 128
+        piece = sides[s, 48:64, 0:128].astype(F32)[:8]
+        if b:
+            piece = pltpu.roll(piece, b, 1)
+        line[a : a + 8, :] += jnp.where(lane >= b, piece, 0.0)
+        line[a + 1 : a + 9, :] += jnp.where(lane < b, piece, 0.0)
+    lane = lax.broadcasted_iota(jnp.int32, (1, 128), 1)
+    for degree in range(DEGS):
+        a, b = CIN * degree // 128, CIN * degree % 128
+        piece = line[a : a + 8, :]
+        if b:
+            piece = pltpu.roll(piece, 128 - b, 1)
+        for m in range(6):
+            one = jnp.where(lane + b < 128, piece[m : m + 1], piece[m + 1 : m + 2])
+            one = jnp.where(lane + 128 * m < CIN, one, 0.0)
+            column_ref[degree : degree + 1, 128 * m : 128 * m + 128] = one
+    for copy in copies:
+        copy.wait()
+
+
+def gather_rows(length, main, side):
+    count = 2 * CHIPS
+    return pl.pallas_call(
+        partial(gather_kernel, length),
+        out_shape=(jax.ShapeDtypeStruct((ALL_ROWS, 640), BF), jax.ShapeDtypeStruct((DEGS, DP), F32)),
+        in_specs=[vspec(), vspec()],
+        out_specs=(pl.BlockSpec(memory_space=pl.ANY), vspec()),
+        scratch_shapes=[
+            pltpu.VMEM((count, 64, 640), BF),
+            pltpu.VMEM((count, 16, 640), BF),
+            pltpu.VMEM((136, 128), F32),
+            pltpu.SemaphoreType.DMA((5, 7)),
+            pltpu.SemaphoreType.DMA((3, count)),
+            pltpu.SemaphoreType.DMA((3, count)),
+            pltpu.SemaphoreType.DMA((2 + 2 * count,)),
+        ],
+        compiler_params=params(30, collective_id=0, has_side_effects=True),
+    )(main, side)
+
+
+def lane_mask():
+    return (lax.broadcasted_iota(jnp.int32, (1, DP), 1) < D).astype(F32)
+
+
+def unit_of(values, mask):
+    mean = jnp.sum(values, axis=-1, keepdims=True) * (1.0 / D)
+    centred = (values - mean) * mask
+    square = jnp.sum(centred * centred, axis=-1, keepdims=True) * (1.0 / D)
+    scale = lax.rsqrt(square + 1e-06)
+    return centred * scale, scale
+
+
+def norm_back(upstream, unit, scale, gain):
+    scaled = upstream * gain
+    mean_one = jnp.sum(scaled, axis=-1, keepdims=True) * (1.0 / D)
+    mean_two = jnp.sum(scaled * unit, axis=-1, keepdims=True) * (1.0 / D)
+    return scale * (scaled - mean_one * lane_mask() - unit * mean_two)
+
+
+def modes_kernel(state_ref, noise_ref, vec_ref, table_ref, out_ref):
+    unit, scale = unit_of(state_ref[...].astype(F32), lane_mask())
+    normed = unit * vec_ref[0:1, :DP] + vec_ref[1:2, :DP]
+    joined = jnp.concatenate(
+        [normed[:, :640], normed[:, 640:] + noise_ref[...].astype(F32)], axis=1
+    )
+    for j in range(BLK):
+        piece = joined[NLON * j : NLON * j + NLON, :]
+        out_ref[j] = split_dot(table_ref[...], piece).astype(BF)
+
+
+def modes(state, noise, vectors, table):
+    return pl.pallas_call(
+        modes_kernel,
+        grid=(ROWS // BLK,),
+        out_shape=jax.ShapeDtypeStruct((ROWS, KP, DP), BF),
+        in_specs=[
+            pl.BlockSpec((BC, DP), lambda i: (i, 0)),
+            pl.BlockSpec((BC, 128), lambda i: (i, 0)),
+            pl.BlockSpec((8, HP), lambda i: (0, 0)),
+            pl.BlockSpec((KP, 3 * NLON), lambda i: (0, 0)),
+        ],
+        out_specs=pl.BlockSpec((BLK, KP, DP), lambda i: (i, 0, 0)),
+        compiler_params=params(),
+    )(state, noise, vectors, table)
+
+
+def legendre(table_ref, own_ref, other_ref, out_ref):
+    for group in range(GROUPS):
+        at = slice(GK * group, GK * group + GK)
+        total = dot(table_ref[0, 0, group], own_ref[:, at, :].reshape(384, DP))
+        total = total + dot(table_ref[0, 1, group], other_ref[:, at, :].reshape(384, DP))
+        out_ref[:, at, :] = total.astype(out_ref.dtype).reshape(24, GK, DP)
+
+
+def fetch(w_ref, w_buf, sem, degree, slot):
+    first = pl.multiple_of((CIN * degree) // 16 * 16, 16)
+    return pltpu.make_async_copy(w_ref.at[pl.ds(first, WROWS)], w_buf.at[slot], sem.at[slot])
+
+
+def mix_kernel(half_ref, own_ref, other_ref, table_ref, column_ref, w_ref, coeff_ref, mixed_ref, w_buf, sem):
+    fetch(w_ref, w_buf, sem, 0, 0).start()
+    legendre(table_ref, own_ref, other_ref, coeff_ref)
+    lane = lax.broadcasted_iota(jnp.int32, (KP, 128), 1)
+
+    def one(degree, carry):
+        slot = degree % 2
+
+        @pl.when(degree + 1 < DEGS)
+        def _():
+            fetch(w_ref, w_buf, sem, degree + 1, 1 - slot).start()
+
+        fetch(w_ref, w_buf, sem, degree, slot).wait()
+        coeffs = coeff_ref[degree].astype(F32)
+        moved = pltpu.roll(coeffs, (CIN * degree) % 16, 1)
+        mixed = dot(moved[:, :WROWS].astype(BF), w_buf[slot])
+        mixed_ref[degree, :, :640] = mixed.astype(BF)
+        last = jnp.sum(coeffs * column_ref[pl.ds(degree, 1), :], axis=1, keepdims=True)
+        mixed_ref[degree, :, 640:] = jnp.where(lane < 1, last, 0.0).astype(BF)
+        return carry
+
+    lax.fori_loop(0, DEGS, one, 0)
+
+
+def mix_back_kernel(half_ref, own_ref, other_ref, table_ref, column_ref, w_ref, grad_ref, out_ref, w_buf, wide, sem):
+    fetch(w_ref, w_buf, sem, 0, 0).start()
+    legendre(table_ref, own_ref, other_ref, grad_ref)
+    keep = lax.broadcasted_iota(jnp.int32, (KP, DP), 1) < CIN
+    wide[...] = jnp.zeros_like(wide)
+
+    def one(degree, carry):
+        slot = degree % 2
+
+        @pl.when(degree + 1 < DEGS)
+        def _():
+            fetch(w_ref, w_buf, sem, degree + 1, 1 - slot).start()
+
+        fetch(w_ref, w_buf, sem, degree, slot).wait()
+        wide[:, :WROWS] = dot_nt(grad_ref[degree, :, :640], w_buf[slot])
+        back = pltpu.roll(wide[...], DP - (CIN * degree) % 16, 1)
+        last = grad_ref[degree, :, 640:].astype(F32)[:, 0:1]
+        back = back + last * column_ref[pl.ds(degree, 1), :]
+        out_ref[degree] = jnp.where(keep, back, 0.0).astype(BF)
+        return carry
+
+    lax.fori_loop(0, DEGS, one, 0)
+
+
+def mix(half, own, other, table, weights, column, back):
+    whole = pl.BlockSpec((24, KP, DP), lambda i, h: (0, 0, 0))
+    scratch = [pltpu.VMEM((2, WROWS, 640), BF)]
+    if back:
+        scratch.append(pltpu.VMEM((KP, DP), F32))
+    scratch.append(pltpu.SemaphoreType.DMA((2,)))
+    return pl.pallas_call(
+        mix_back_kernel if back else mix_kernel,
+        grid_spec=pltpu.PrefetchScalarGridSpec(
+            num_scalar_prefetch=1,
+            grid=(1,),
+            in_specs=[
+                whole,
+                whole,
+                pl.BlockSpec((1, 2, GROUPS, 384, 384), lambda i, h: (h[0], 0, 0, 0, 0)),
+                pl.BlockSpec((DEGS, DP), lambda i, h: (0, 0)),
+                pl.BlockSpec(memory_space=pl.ANY),
+            ],
+            out_specs=(whole, whole),
+            scratch_shapes=scratch,
+        ),
+        out_shape=(jax.ShapeDtypeStruct((24, KP, DP), BF),) * 2,
+        compiler_params=params(),
+    )(half, own, other, table, column, weights)
+
+
+HID_PARTS = ((0, 256), (256, 256), (512, 256), (768, 256), (1024, 256), (1280, 128))
+
+
+def feed_kernel(
+    half_ref, mask_ref, own_ref, other_ref, table_ref, inverse_ref, state_ref, vec_ref, in_ref, out_ref,
+    next_ref, middle_ref, hidden_ref, active_ref, slope_ref, lat,
+):
+    i = pl.program_id(0)
+
+    @pl.when(i == 0)
+    def _():
+        legendre(table_ref, own_ref, other_ref, lat)
+
+    mask = mask_ref[0]
+    parts = [split_dot(inverse_ref[...], lat[BLK * i + j]) for j in range(BLK)]
+    middle = state_ref[...].astype(F32) + mask * jnp.concatenate(parts, axis=0)
+    middle_ref[...] = middle
+    unit, scale = unit_of(middle, lane_mask())
+    hidden = (unit * vec_ref[2:3, :DP] + vec_ref[3:4, :DP]).astype(BF)
+    hidden_ref[...] = hidden
+    for first, width in HID_PARTS:
+        at = slice(first, first + width)
+        pre = dot(hidden, in_ref[:, at]) + vec_ref[4:5, at]
+        bell = 0.5 * (1.0 + lax.erf(pre * (1.0 / math.sqrt(2.0))))
+        active_ref[:, at] = (pre * bell).astype(BF)
+        slope = bell + pre * (jnp.exp(-0.5 * pre * pre) * (1.0 / math.sqrt(2.0 * math.pi)))
+        slope_ref[:, at] = slope.astype(BF)
+    result = dot(active_ref[...], out_ref[...]) + vec_ref[5:6, :DP]
+    next_ref[...] = (middle + mask * result).astype(next_ref.dtype)
+
+
+def cell_spec(width):
+    return pl.BlockSpec((BC, width), lambda i, *h: (i, 0))
+
+
+def fixed(*shape):
+    return pl.BlockSpec(shape, lambda i, *h: (0,) * len(shape))
+
+
+def table_spec():
+    return pl.BlockSpec((1, 2, GROUPS, 384, 384), lambda i, h, *m: (h[0], 0, 0, 0, 0))
+
+
+def feed(half, mask, own, other, table, inverse_t, state, vectors, w_in, w_out, last):
+    cells = lambda width, kind: jax.ShapeDtypeStruct((CELLS, width), kind)
+    return pl.pallas_call(
+        feed_kernel,
+        grid_spec=pltpu.PrefetchScalarGridSpec(
+            num_scalar_prefetch=2,
+            grid=(ROWS // BLK,),
+            in_specs=[
+                fixed(24, KP, DP), fixed(24, KP, DP), table_spec(), fixed(NLON, 3 * KP), cell_spec(DP),
+                fixed(8, HP), fixed(DP, HP), fixed(HP, DP),
+            ],
+            out_specs=(cell_spec(DP), cell_spec(DP), cell_spec(DP), cell_spec(HP), cell_spec(HP)),
+            scratch_shapes=[pltpu.VMEM((24, KP, DP), F32)],
+        ),
+        out_shape=(
+            cells(DP, BF if last else F32), cells(DP, F32), cells(DP, BF), cells(HP, BF), cells(HP, BF),
+        ),
+        compiler_params=params(),
+    )(half, mask, own, other, table, inverse_t, state, vectors, w_in, w_out)
+
+
+def feed_back_kernel(
+    mask_ref, grad_ref, slope_ref, middle_ref, vec_ref, in_ref, out_ref, inverse_ref,
+    result_ref, pre_ref, gm_ref, modes_ref, sums_ref,
+):
+    i = pl.program_id(0)
+
+    @pl.when(i == 0)
+    def _():
+        sums_ref[...] = jnp.zeros_like(sums_ref)
+
+    mask = mask_ref[0]
+    grad = grad_ref[...].astype(F32)
+    result = (mask * grad).astype(BF)
+    result_ref[...] = result
+    sums_ref[5:6, :DP] += jnp.sum(result.astype(F32), axis=0, keepdims=True)
+    for first, width in HID_PARTS:
+        at = slice(first, first + width)
+        active = dot_nt(result, out_ref[at, :])
+        pre = (active * slope_ref[:, at].astype(F32)).astype(BF)
+        pre_ref[:, at] = pre
+        sums_ref[4:5, at] += jnp.sum(pre.astype(F32), axis=0, keepdims=True)
+    upstream = dot_nt(pre_ref[...], in_ref[...])
+    unit, scale = unit_of(middle_ref[...], lane_mask())
+    sums_ref[2:3, :DP] += jnp.sum(upstream * unit, axis=0, keepdims=True)
+    sums_ref[3:4, :DP] += jnp.sum(upstream, axis=0, keepdims=True)
+    total = grad + norm_back(upstream, unit, scale, vec_ref[2:3, :DP])
+    gm_ref[...] = total
+    total = mask * total
+    for j in range(BLK):
+        piece = total[NLON * j : NLON * j + NLON, :]
+        modes_ref[j] = split_dot(inverse_ref[...], piece).astype(BF)
+
+
+def feed_back(mask, grad, slope, middle, vectors, w_in, w_out, inverse):
+    cells = lambda width, kind: jax.ShapeDtypeStruct((CELLS, width), kind)
+    return pl.pallas_call(
+        feed_back_kernel,
+        grid_spec=pltpu.PrefetchScalarGridSpec(
+            num_scalar_prefetch=1,
+            grid=(ROWS // BLK,),
+            in_specs=[
+                cell_spec(DP), cell_spec(HP), cell_spec(DP), fixed(8, HP), fixed(DP, HP), fixed(HP, DP),
+                fixed(KP, 3 * NLON),
+            ],
+            out_specs=(
+                cell_spec(DP), cell_spec(HP), cell_spec(DP),
+                pl.BlockSpec((BLK, KP, DP), lambda i, *h: (i, 0, 0)), fixed(8, HP),
+            ),
+        ),
+        out_shape=(
+            cells(DP, BF), cells(HP, BF), cells(DP, F32), jax.ShapeDtypeStruct((ROWS, KP, DP), BF),
+            jax.ShapeDtypeStruct((8, HP), F32),
+        ),
+        compiler_params=params(),
+    )(mask, grad, slope, middle, vectors, w_in, w_out, inverse)
+
+
+def first_back_kernel(
+    half_ref, own_ref, other_ref, table_ref, fourier_ref, state_ref, gm_ref, vec_ref, out_ref, sums_ref, lat,
+):
+    i = pl.program_id(0)
+
+    @pl.when(i == 0)
+    def _():
+        legendre(table_ref, own_ref, other_ref, lat)
+        sums_ref[...] = jnp.zeros_like(sums_ref)
+
+    parts = [split_dot(fourier_ref[...], lat[BLK * i + j]) for j in range(BLK)]
+    upstream = jnp.concatenate(parts, axis=0)
+    unit, scale = unit_of(state_ref[...].astype(F32), lane_mask())
+    sums_ref[0:1, :] += jnp.sum(upstream * unit, axis=0, keepdims=True)
+    sums_ref[1:2, :] += jnp.sum(upstream, axis=0, keepdims=True)
+    total = gm_ref[...] + norm_back(upstream, unit, scale, vec_ref[0:1, :DP])
+    out_ref[...] = total.astype(out_ref.dtype)
+
+
+def first_back(half, own, other, table, fourier, state, gm, vectors, last):
+    return pl.pallas_call(
+        first_back_kernel,
+        grid_spec=pltpu.PrefetchScalarGridSpec(
+            num_scalar_prefetch=1,
+            grid=(ROWS // BLK,),
+            in_specs=[
+                fixed(24, KP, DP), fixed(24, KP, DP), table_spec(), fixed(NLON, 3 * KP), cell_spec(DP),
+                cell_spec(DP), fixed(8, HP),
+            ],
+            out_specs=(cell_spec(DP), fixed(8, DP)),
+            scratch_shapes=[pltpu.VMEM((24, KP, DP), F32)],
+        ),
+        out_shape=(
+            jax.ShapeDtypeStruct((CELLS, DP), BF if last else F32), jax.ShapeDtypeStruct((8, DP), F32),
+        ),
+        compiler_params=params(),
+    )(half, own, other, table, fourier, state, gm, vectors)
+
+
+def mlp_grad_kernel(h0, h1, p0, p1, a0, a1, r0, r1, tin, tout, turned):
+    for step, ref in enumerate((h0, h1)):
+        turned[:, CELLS * step : CELLS * step + CELLS] = ref[...].T
+    for first, width in HID_PARTS:
+        at = slice(first, first + width)
+        part = dot(turned[:, :CELLS], p0[:, at]) + dot(turned[:, CELLS:], p1[:, at])
+        for m in range(width // 128):
+            tin[first // 128 + m] = part[:, 128 * m : 128 * m + 128]
+        part = dot_tn(a0[:, at], r0[...]) + dot_tn(a1[:, at], r1[...])
+        for m in range(6):
+            tout[m, at, :] = part[:, 128 * m : 128 * m + 128]
+
+
+def mlp_flat_kernel(gin, gout, feed_sums, first_sums, flat_ref, tin, tout):
+    tin[:, :DP, :] = gin[...]
+    tout[:, :HP, :] = gout[...]
+    tin[:, DP:, :] = jnp.zeros((11, 1024 - DP, 128), F32)
+    tout[:, HP:, :] = jnp.zeros((6, 2048 - HP, 128), F32)
+    flat_ref[...] = jnp.zeros_like(flat_ref)
+    lane = lax.broadcasted_iota(jnp.int32, (1, 128), 1)
+    sums = feed_sums[...]
+    for row, (place, length) in enumerate(VECTORS):
+        first, shift = place // 128, place % 128
+        for m in range(-(-length // 128)):
+            at = slice(128 * m, 128 * m + 128)
+            piece = first_sums[row : row + 1, at] if row < 2 else sums[row : row + 1, at]
+            piece = jnp.where(lane + 128 * m < length, piece, 0.0)
+            if shift:
+                piece = pltpu.roll(piece, shift, 1)
+            flat_ref[first + m : first + m + 1, :] += jnp.where(lane >= shift, piece, 0.0)
+            flat_ref[first + m + 1 : first + m + 2, :] += jnp.where(lane < shift, piece, 0.0)
+    for part in range(2):
+
+        def get_in(m, t, part=part):
+            return tin[m, pl.ds(t + 512 * part, 8, stride=64), :]
+
+        rows_in(flat_ref, IN_AT // 128 + 641 * 8 * part, IN_AT % 128, 2, 10, 11, get_in, 64, 1)
+
+    for part in range(2):
+
+        def get_out(m, t, part=part):
+            return tout[m, pl.ds(t + 1024 * part, 8, stride=128), :]
+
+        rows_in(flat_ref, OUT_AT // 128 + 641 * 8 * part, OUT_AT % 128, 1, 5, 6, get_out, 128, 2)
+
+
+FLAT_ROWS = 16784
+
+
+def mlp_grads(hidden, pre, active, result, feed_sums, first_sums):
+    gin, gout = pl.pallas_call(
+        mlp_grad_kernel,
+        out_shape=(jax.ShapeDtypeStruct((11, DP, 128), F32), jax.ShapeDtypeStruct((6, HP, 128), F32)),
+        in_specs=[vspec()] * 8,
+        out_specs=(vspec(), vspec()),
+        scratch_shapes=[pltpu.VMEM((DP, 2 * CELLS), BF)],
+        compiler_params=params(62),
+    )(*hidden, *pre, *active, *result)
+    return pl.pallas_call(
+        mlp_flat_kernel,
+        out_shape=jax.ShapeDtypeStruct((FLAT_ROWS, 128), F32),
+        in_specs=[vspec()] * 4,
+        out_specs=vspec(),
+        scratch_shapes=[pltpu.VMEM((11, 1024, 128), F32), pltpu.VMEM((6, 2048, 128), F32)],
+        compiler_params=params(62),
+    )(gin, gout, feed_sums, first_sums)
+
+
+def spectral_grad_kernel(c0, c1, g0, g1, tiles_ref, head_ref):
+    rows = 16 * KP
+    tiles_ref[:, 0:16, :] = jnp.zeros((6, 16, 128), F32)
+    for e in range(2):
+        total = dot_tn(c0[:, e].reshape(rows, DP), g0[:, e].reshape(rows, DP))
+        total = total + dot_tn(c1[:, e].reshape(rows, DP), g1[:, e].reshape(rows, DP))
+        if e == 0:
+            head_ref[...] = total[0:8, :]
+        for m in range(6):
+            tiles_ref[m, 16 + CIN * e : 16 + CIN * e + CIN, :] = total[:CIN, 128 * m : 128 * m + 128]
+    tiles_ref[:, 16 + 2 * CIN :, :] = jnp.zeros((6, 1384 - 16 - 2 * CIN, 128), F32)
+
+
+def spectral_grads(coeffs, grads):
+    return pl.pallas_call(
+        spectral_grad_kernel,
+        out_shape=(jax.ShapeDtypeStruct((6, 1384, 128), F32), jax.ShapeDtypeStruct((8, DP), F32)),
+        in_specs=[vspec()] * 4,
+        out_specs=(vspec(), vspec()),
+        compiler_params=params(),
+    )(*coeffs, *grads)
+
+
+def flatten_kernel(length, shard_ref, tiles_ref, next_ref, out_ref, tiles, flat):
+    chunks = length // 128
+    shard = shard_ref[0]
+    base, start, offset = shard_place(shard, length)
+    move = base - CIN * ((3 * shard) // 2) + 16
+    tiles[...] = tiles_ref[...]
+    for m in range(6):
+        tiles[m, 16 + 2 * CIN : 24 + 2 * CIN, :] = next_ref[:, 128 * m : 128 * m + 128]
+    flat[...] = jnp.zeros_like(flat)
+
+    def get(m, t):
+        return tiles[m, pl.ds(t + move, 8, stride=128), :]
+
+    rows_in(flat, start, offset, 1, 5, 6, get, 128)
+
+    def save(i, carry):
+        piece = flat[pl.ds(pl.multiple_of(88 + 8 * i, 8), 8), :].reshape(1, 1024)
+        out_ref[:, pl.ds(pl.multiple_of(1024 * i, 1024), 1024)] = piece
+        return carry
+
+    lax.fori_loop(0, chunks // 8, save, 0, unroll=7)
+    rest = chunks % 8
+    if rest:
+        piece = flat[88 + chunks - rest : 88 + chunks, :].reshape(1, 128 * rest)
+        out_ref[:, 128 * (chunks - rest) :] = piece
+
+
+def flatten(shard, tiles, after, length):
+    return pl.pallas_call(
+        partial(flatten_kernel, length),
+        out_shape=jax.ShapeDtypeStruct((1, length), F32),
+        in_specs=[pl.BlockSpec(memory_space=pltpu.SMEM), vspec(), vspec()],
+        out_specs=vspec(),
+        scratch_shapes=[pltpu.VMEM((6, 1384, 128), F32), pltpu.VMEM((5256, 128), F32)],
+        compiler_params=params(),
+    )(shard, tiles, after)
+
+
+def wide(block):
+    flat = block.reshape(CELLS, D)
+    return jnp.pad(flat, ((0, 0), (0, DP - D)))
+
+
+def shards_paired(fields, noise_fields, step_counts, spectral_flat, mlp_flat, cotangent):
+    axes = ("dp", "lat")
+    dp_count = lax.axis_size("dp")
+    dp_index = lax.axis_index("dp")
+    core = dp_index % 2
+    lat_index = lax.axis_index("lat")
+    length = spectral_flat.shape[1]
+    places = [(d, y) for d in range(dp_count) for y in range(2)]
+    number = lambda d, y: 2 * d + y
+    mirror = [(number(d, y), number(d - d % 2 + y, d % 2)) for d, y in places]
+    other_core = [(number(d, y), number(d + 1 - 2 * (d % 2), y)) for d, y in places]
+    same_core = [[number(d, y) for d, y in places if d % 2 == c] for c in range(2)]
+    mirrored = lambda a: lax.ppermute(a, axes, mirror)
+    swapped = lambda a: lax.ppermute(a, axes, other_core)
+    half = core.astype(jnp.int32).reshape(1)
+    tables = {name: jnp.asarray(value) for name, value in plan_tables().items()}
+
+    main, side = spectral_window(dp_index.astype(jnp.int32).reshape(1), spectral_flat)
+    weights, column = gather_rows(length, main, side)
+    mlp_whole = lax.all_gather(mlp_flat, axes, axis=0, tiled=True)
+    state = mirrored(wide(fields))
+    noise = jnp.pad(
+        noise_fields.reshape(STEPS, CELLS, NOISE), ((0, 0), (0, 0), (1, 128 - 1 - NOISE))
+    )
+    noise = mirrored(noise)
+    counts = mirrored(step_counts)
+    grad = mirrored(wide(cotangent))
+    w_in, w_out, vectors = mlp_weights(mlp_whole.reshape(-1, 128))
+
+    kept = []
+    for step in range(STEPS):
+        mask = (step < counts).astype(F32)
+        lon_modes = modes(state, noise[step], vectors, tables["fourier_t"])
+        coeffs, mixed = mix(half, lon_modes, swapped(lon_modes), tables["analyse"], weights, column, False)
+        following, middle, hidden, active, slope = feed(
+            half, mask, mixed, swapped(mixed), tables["synthesize"], tables["inverse_t"], state, vectors,
+            w_in, w_out, step == STEPS - 1,
+        )
+        kept.append((mask, state, coeffs, middle, hidden, active, slope))
+        state = following
+    output = mirrored(state)
+
+    owners = dp_count
+    pairs = np.array([[(3 * s) // 2, (3 * s) // 2 + 1] for s in range(owners)])
+
+    def to_owners(block):
+        parts = jnp.concatenate([block[a : b + 1] for a, b in pairs], axis=0)
+        parts = parts.reshape(owners, 2, KP, DP)
+        return lax.all_to_all(
+            parts, axes, split_axis=0, concat_axis=0, tiled=True, axis_index_groups=same_core
+        )
+
+    coeff_parts = [to_owners(kept[step][2]) for step in range(STEPS)]
+    grad_parts = [None] * STEPS
+    results = [None] * STEPS
+    pres = [None] * STEPS
+    feed_sums = first_sums = 0.0
+    for step in reversed(range(STEPS)):
+        mask, state, coeffs, middle, hidden, active, slope = kept[step]
+        results[step], pres[step], gm, grad_modes, sums = feed_back(
+            mask, grad, slope, middle, vectors, w_in, w_out, tables["inverse"]
+        )
+        feed_sums = feed_sums + sums
+        grad_mixed, grad_coeffs = mix(
+            half, grad_modes, swapped(grad_modes), tables["synthesize_back"], weights, column, True
+        )
+        grad_parts[step] = to_owners(grad_mixed)
+        grad, sums = first_back(
+            half, grad_coeffs, swapped(grad_coeffs), tables["analyse_back"], tables["fourier"], state, gm,
+            vectors, step == 0,
+        )
+        first_sums = first_sums + sums
+    fields_grad = mirrored(grad)
+    mlp_pack = mlp_grads(
+        [k[4] for k in kept], pres, [k[5] for k in kept], results, feed_sums, first_sums
+    )
+    mlp_pack = mlp_pack[: mlp_whole.shape[0] // 128].reshape(-1)
+    mlp_grad = lax.psum_scatter(mlp_pack, axes, scatter_dimension=0, tiled=True)
+
+    owner = (dp_index - core + lat_index).astype(jnp.int32).reshape(1)
+    tiles, head = spectral_grads(coeff_parts, grad_parts)
+    spot = lambda s, c: number(s - s % 2 + c, s % 2)
+    earlier = [(spot(s, c), spot(s - 1, c)) for s in range(1, owners) for c in range(2)]
+    after = lax.ppermute(head, axes, earlier)
+    spectral_grad = mirrored(flatten(owner, tiles, after, length))
+    narrow = lambda a: a[:, :D].reshape(1, ROWS, NLON, D)
+    return narrow(output), narrow(fields_grad), spectral_grad, mlp_grad
+
+
 def solution(mesh):
+    paired = mesh.shape["lat"] == 2 and mesh.shape["dp"] == 16
     return jax.shard_map(
-        shards,
+        shards_paired if paired else shards_general,
         mesh=mesh,
         in_specs=(
             P("dp", "lat", None, None),

time: 3010 us -> 1050 us (0.35); the launches traced: 2960 us -> 1040 us
  local copies, waits for them, and re-layouts: 1370 us -> 97.4 us
  waiting for transfers between devices: 967 us -> 264 us
  Pallas kernels: 0 us -> 547 us
  matrix products: 281 us -> 0 us
  blocking collectives: 153 us -> 0 us
  other arithmetic: 104 us -> 24 us
    unnamed x244 -> x81, local copies, waits for them, and re-layouts: 794 us -> 74 us
    unnamed x6 -> x3, waiting for transfers between devices: 660 us -> 97.6 us
    pallas_call x0 -> x19, Pallas kernels: none -> 547 us  [the longest x1 168 us: gather_rows(): pl.pallas_call(partial(gather_kernel, length), out_shape=(jax.ShapeDtypeS...]
    slice x3 -> x0, local copies, waits for them, and re-layouts: 426 us -> none  [the longest x1 422 us: build_weights(): spectral = spectral_whole[0, :count_all].reshape(degrees_here, D + NOISE, D)]
    dot_general x34 -> x0, matrix products: 281 us -> none  [the longest x2 46.1 us: backward_step(): jnp.einsum('blkc,blkd->lcd', by_degree, grad_degree, preferred_element_ty...]
    all_to_all x5 -> x0, blocking collectives: 153 us -> none  [the longest x1 33.7 us: forward_step(): lax.all_to_all(coeffs, 'lat', split_axis=1, concat_axis=2, tiled=True)]
    all_gather x2 -> x1, waiting for transfers between devices: 137 us -> 23.3 us  [shards_paired(): mlp_whole = lax.all_gather(mlp_flat, axes, axis=0, tiled=True)]
    all_to_all x11 -> x4, waiting for transfers between devices: 171 us -> 83.6 us  [to_owners(): lax.all_to_all(parts, axes, split_axis=0, concat_axis=0, tiled=True, axis...]
  transfers between devices with their start and end apart: 15 -> 22, of which waited for: 11 -> 9; matrix products, arithmetic and copies ran while one was open for 29% -> 8% of each run, Pallas kernels for 0% -> 49%
where the time goes in v1:
time: 1050 us; the launch traced here: 1040 us
  Pallas kernels  547 us (52%)
  waiting for transfers between devices  264 us (25%)
  local copies, waits for them, and re-layouts  97.4 us (9%)
  starting transfers between devices  87.6 us (8%)
  other arithmetic  24 us (2%)
  between operations  16.2 us (2%)
    pallas_call x1, Pallas kernels, gather_rows(): pl.pallas_call(partial(gather_kernel, length), out_shape=(jax.ShapeDtypeS...  168 us
    pallas_call x4, Pallas kernels, mix(): pl.pallas_call(mix_back_kernel if back else mix_kernel, grid_spec=pltpu.P...  114 us
    unnamed x3, waiting for transfers between devices  97.6 us
    all_to_all x4, waiting for transfers between devices, to_owners(): lax.all_to_all(parts, axes, split_axis=0, concat_axis=0, tiled=True, axis...  83.6 us
    unnamed x81, local copies, waits for them, and re-layouts  74 us
    pallas_call x2, Pallas kernels, feed(): pl.pallas_call(feed_kernel, grid_spec=pltpu.PrefetchScalarGridSpec(num_sc...  49.9 us
    ppermute x7, waiting for transfers between devices, shards_paired(): mirrored = lambda a: lax.ppermute(a, axes, mirror)  44.7 us
    pallas_call x2, Pallas kernels, feed_back(): pl.pallas_call(feed_back_kernel, grid_spec=pltpu.PrefetchScalarGridSpec(n...  40.3 us
  transfers between devices with their start and end apart: 22, of which 9 were waited for; matrix products, arithmetic and copies ran while one was open for 8% of the time, Pallas kernels for 49%

profile of v1, /device:TPU:1, one launch (start us, length us, event | category | flops | bytes accessed | tf_op | source)
XLA Modules:
  0.0 1036.4 jit_solution(16536459761459086994)
XLA Ops:
  7.2 1.7 reshape.64
  8.9 3.5 pad.11
  12.4 4.5 collective-permute-start.1
  18.8 1.9 collective-permute-start.2
  20.7 40.1 %collective-permute-done.2 = bf16[2,1728,128]{2,1,0:T(8,128)(2,1)S(1)} collective-permute-done((bf16[2,1728,128]{2,1,0:T(8,128)(2,1)S(1)}, bf16[2,1728,128]{2,1,0:T(8,128)(2,1)S(1)}, u32[]{:S(2)}, u32[]{:S(2)}) %collective-permute-start.2) | collective-permute-done | bytes 884768 | tf_op jit(solution)/shard_map/ppermute | solution.py:1223
  61.7 23.3 %all-gather.3.cloned.1.call-done = bf16[32,1,51584]{2,1,0:T(2,128)(2,1)} async-done(((bf16[1,1,51584]{2,1,0:T(2,128)(2,1)}), bf16[32,1,51584]{2,1,0:T(2,128)(2,1)}) %all-gather.3.cloned.1.call-update) | async-done | bytes 3301392 | tf_op jit(solution)/shard_map/all_gather | solution.py:1230
  85.0 22.0 %reduce = bf16[32,51584]{1,0:T(8,128)(2,1)} reduce(bf16[32,1,51584]{2,1,0:T(2,128)(2,1)} %all-gather.3.cloned.1.call-done, bf16[]{:T(256)} %constant.66), dimensions={1}, to_apply=%all-gather.reduce_sub_computation | reduce | bytes 6602754 | tf_op jit(solution)/shard_map/all_gather | solution.py:1230
  107.0 7.3 reshape.53.flat_ref
  114.4 26.1 %shard_map.165 = (bf16[768,1408]{1,0:T(8,128)(2,1)}, bf16[1408,768]{1,0:T(8,128)(2,1)}, f32[8,1408]{1,0:T(8,128)}) custom-call(bf16[12896,128]{1,0:T(8,128)(2,1)} %reshape.53.flat_ref), custom_call_target="tpu_custom_call" | custom-call | tf_op jit(solution)/shard_map/pallas_call | solution.py:545
  141.9 7.2 shard_map.166.own_ref
  149.3 10.0 shard_map.167
  161.5 168.1 %shard_map.168 = (bf16[15584,640]{1,0:T(8,128)(2,1)S(1)}, f32[24,768]{1,0:T(8,128)S(1)}) custom-call(bf16[944,640]{1,0:T(8,128)(2,1)S(1)} %copy-done.1, bf16[64,640]{1,0:T(8,128)(2,1)S(1)} %copy-done.3), custom_call_target="tpu_custom_call" | custom-call | tf_op jit(solution)/shard_map/pallas_call | solution.py:766
  329.6 6.6 copy-done
  336.9 1.6 copy-done.12
  338.6 27.6 %shard_map.169 = (bf16[24,80,768]{2,1,0:T(8,128)(2,1)}, bf16[24,80,768]{2,1,0:T(8,128)(2,1)}) custom-call(s32[1]{0:T(128)} %bitcast.half_ref, bf16[24,80,768]{2,1,0:T(8,128)(2,1)} %shard_map.166.own_ref, bf16[24,80,768]{2,1,0:T(8,128)(2,1)} %copy-done.12, bf16[2,2,5,384,384]{4,3,2,1,0:T(8,128)(2,1)} %constant.48.clone.table_ref, f32[24,768]{1,0:T(8,128)} %copy-done.2, ...), custom_call_target="tpu_custom_call" | custom-call | tf_op jit(solution)/shard_map/pallas_call | solution.py:897
  372.4 1.9 copy-done.9
  374.3 4.7 all-to-all-start
  378.9 3.8 collective-permute-start
  382.8 4.7 collective-permute-done
  389.7 24.9 %shard_map.170 = (f32[1728,768]{1,0:T(8,128)}, f32[1728,768]{1,0:T(8,128)}, bf16[1728,768]{1,0:T(8,128)(2,1)}, bf16[1728,1408]{1,0:T(8,128)(2,1)}, bf16[1728,1408]{1,0:T(8,128)(2,1)}) custom-call(s32[1]{0:T(128)} %bitcast.half_ref, f32[1]{0:T(128)S(6)} %convert_element_type.12.mask_ref, bf16[24,80,768]{2,1,0:T(8,128)(2,1)} %get-tuple-element.52.own_ref, ...), custom_call_target="tpu_custom_call" | custom-call | tf_op jit(solution)/shard_map/pallas_call | solution.py:962
  414.6 7.6 shard_map.171.own_ref
  422.2 3.5 pad.13
  425.7 1.9 collective-permute-start.8
  429.4 27.6 %shard_map.172 = (bf16[24,80,768]{2,1,0:T(8,128)(2,1)}, bf16[24,80,768]{2,1,0:T(8,128)(2,1)}) custom-call(s32[1]{0:T(128)} %bitcast.half_ref, bf16[24,80,768]{2,1,0:T(8,128)(2,1)} %shard_map.171.own_ref, bf16[24,80,768]{2,1,0:T(8,128)(2,1)} %copy-done.15, bf16[2,2,5,384,384]{4,3,2,1,0:T(8,128)(2,1)} %constant.48.clone.table_ref, f32[24,768]{1,0:T(8,128)} %copy-done.2, ...), custom_call_target="tpu_custom_call" | custom-call | tf_op jit(solution)/shard_map/pallas_call | solution.py:897
  457.0 20.0 %collective-permute-start.6 = (bf16[24,80,768]{2,1,0:T(8,128)(2,1)}, bf16[24,80,768]{2,1,0:T(8,128)(2,1)S(1)}, u32[]{:S(2)}, u32[]{:S(2)}) collective-permute-start(bf16[24,80,768]{2,1,0:T(8,128)(2,1)} %get-tuple-element.56.own_ref), channel_id=1, source_target_pairs={{0,2},{1,3},{2,0},{3,1},{4,6},{5,7},{6,4},{7,5},{8,10},{9,11},{10,... | collective-permute-start | bytes 8847368 | tf_op jit(solution)/shard_map/ppermute | solution.py:1224
  477.0 1.7 slice_dynamic-update-slice_fusion.33
  478.7 1.8 slice_dynamic-update-slice_fusion.20
  480.5 1.9 slice_dynamic-update-slice_fusion.19
  482.4 1.9 slice_dynamic-update-slice_fusion.18
  484.2 1.9 slice_dynamic-update-slice_fusion.17
  489.3 10.5 %all-to-all-start.1 = ((bf16[16,2,80,768]{3,2,1,0:T(8,128)(2,1)}), bf16[16,2,80,768]{3,2,1,0:T(8,128)(2,1)}, u32[]{:S(2)}, u32[]{:S(2)}) async-start(bf16[16,2,80,768]{3,2,1,0:T(8,128)(2,1)} %bitcast.10), calls=%async_computation.1 | async-start | bytes 7864320 | tf_op jit(solution)/shard_map/all_to_all | solution.py:1259
  502.1 25.0 %shard_map.173 = (bf16[1728,768]{1,0:T(8,128)(2,1)}, f32[1728,768]{1,0:T(8,128)}, bf16[1728,768]{1,0:T(8,128)(2,1)}, bf16[1728,1408]{1,0:T(8,128)(2,1)}, bf16[1728,1408]{1,0:T(8,128)(2,1)}) custom-call(s32[1]{0:T(128)} %bitcast.half_ref, f32[1]{0:T(128)S(6)} %convert_element_type.11.mask_ref, bf16[24,80,768]{2,1,0:T(8,128)(2,1)} %get-tuple-element.56.own_ref, ...), custom_call_target="tpu_custom_call" | custom-call | tf_op jit(solution)/shard_map/pallas_call | solution.py:962
  527.1 20.1 %shard_map.174 = (bf16[1728,768]{1,0:T(8,128)(2,1)}, bf16[1728,1408]{1,0:T(8,128)(2,1)}, f32[1728,768]{1,0:T(8,128)}, bf16[24,80,768]{2,1,0:T(8,128)(2,1)}, f32[8,1408]{1,0:T(8,128)}) custom-call(f32[1]{0:T(128)S(6)} %convert_element_type.11.mask_ref, bf16[1728,768]{1,0:T(8,128)(2,1)} %collective-permute-done.8.grad_ref, ...), custom_call_target="tpu_custom_call" | custom-call | tf_op jit(solution)/shard_map/pallas_call | solution.py:1016
  547.6 5.2 collective-permute-done.9.other_ref
  552.9 1.7 copy-done.17
  554.6 29.5 %shard_map.175 = (bf16[24,80,768]{2,1,0:T(8,128)(2,1)}, bf16[24,80,768]{2,1,0:T(8,128)(2,1)}) custom-call(s32[1]{0:T(128)} %bitcast.half_ref, bf16[24,80,768]{2,1,0:T(8,128)(2,1)} %get-tuple-element.60.own_ref, bf16[24,80,768]{2,1,0:T(8,128)(2,1)} %copy-done.17, bf16[2,2,5,384,384]{4,3,2,1,0:T(8,128)(2,1)} %constant.51.clone.table_ref, f32[24,768]{1,0:T(8,128)} %copy-done.2, ...), custom_call_target="tpu_custom_call" | custom-call | tf_op jit(solution)/shard_map/pallas_call | solution.py:897
  584.5 1.9 slice_dynamic-update-slice_fusion.29
  586.4 1.9 slice_dynamic-update-slice_fusion.6
  588.2 1.8 slice_dynamic-update-slice_fusion.5
  590.1 1.8 slice_dynamic-update-slice_fusion.4
  591.9 1.8 slice_dynamic-update-slice_fusion.3
  596.9 7.2 all-to-all-start.3
  605.7 15.3 %shard_map.176 = (f32[1728,768]{1,0:T(8,128)}, f32[8,768]{1,0:T(8,128)}) custom-call(s32[1]{0:T(128)} %bitcast.half_ref, bf16[24,80,768]{2,1,0:T(8,128)(2,1)} %get-tuple-element.61.own_ref, bf16[24,80,768]{2,1,0:T(8,128)(2,1)} %copy-done.14, bf16[2,2,5,384,384]{4,3,2,1,0:T(8,128)(2,1)} %constant.50.clone.table_ref, ...), custom_call_target="tpu_custom_call" | custom-call | tf_op jit(solution)/shard_map/pallas_call | solution.py:1058
  621.0 20.2 %shard_map.177 = (bf16[1728,768]{1,0:T(8,128)(2,1)}, bf16[1728,1408]{1,0:T(8,128)(2,1)}, f32[1728,768]{1,0:T(8,128)}, bf16[24,80,768]{2,1,0:T(8,128)(2,1)}, f32[8,1408]{1,0:T(8,128)}) custom-call(f32[1]{0:T(128)S(6)} %convert_element_type.12.mask_ref, f32[1728,768]{1,0:T(8,128)} %get-tuple-element.63.grad_ref, ...), custom_call_target="tpu_custom_call" | custom-call | tf_op jit(solution)/shard_map/pallas_call | solution.py:1016
  641.6 5.2 collective-permute-done.11.other_ref
  646.8 1.6 copy-done.16
  648.4 29.5 %shard_map.178 = (bf16[24,80,768]{2,1,0:T(8,128)(2,1)}, bf16[24,80,768]{2,1,0:T(8,128)(2,1)}) custom-call(s32[1]{0:T(128)} %bitcast.half_ref, bf16[24,80,768]{2,1,0:T(8,128)(2,1)} %get-tuple-element.66.own_ref, bf16[24,80,768]{2,1,0:T(8,128)(2,1)} %copy-done.16, bf16[2,2,5,384,384]{4,3,2,1,0:T(8,128)(2,1)} %constant.51.clone.table_ref, f32[24,768]{1,0:T(8,128)} %copy-done.2, ...), custom_call_target="tpu_custom_call" | custom-call | tf_op jit(solution)/shard_map/pallas_call | solution.py:897
  679.0 31.5 %shard_map.182 = (f32[11,768,128]{2,1,0:T(8,128)}, f32[6,1408,128]{2,1,0:T(8,128)}) custom-call(bf16[1728,768]{1,0:T(8,128)(2,1)} %get-tuple-element.76.h0, bf16[1728,768]{1,0:T(8,128)(2,1)} %get-tuple-element.77.h1, bf16[1728,1408]{1,0:T(8,128)(2,1)} %get-tuple-element.78.p0, bf16[1728,1408]{1,0:T(8,128)(2,1)} %get-tuple-element.79.p1, ...), custom_call_target="tpu_custom_call" | custom-call | tf_op jit(solution)/shard_map/pallas_call | solution.py:1127
  716.0 1.9 copy-done.10
  717.9 14.5 %shard_map.179 = (bf16[1728,768]{1,0:T(8,128)(2,1)}, f32[8,768]{1,0:T(8,128)}) custom-call(s32[1]{0:T(128)} %bitcast.half_ref, bf16[24,80,768]{2,1,0:T(8,128)(2,1)} %get-tuple-element.67.own_ref, bf16[24,80,768]{2,1,0:T(8,128)(2,1)} %collective-permute-done.12.other_ref, bf16[2,2,5,384,384]{4,3,2,1,0:T(8,128)(2,1)} %constant.50.clone.table_ref, ...), custom_call_target="tpu_custom_call" | custom-call | tf_op jit(solution)/shard_map/pallas_call | solution.py:1058
  733.8 36.9 %shard_map.183 = f32[16784,128]{1,0:T(8,128)} custom-call(f32[11,768,128]{2,1,0:T(8,128)} %get-tuple-element.84.gin, f32[6,1408,128]{2,1,0:T(8,128)} %get-tuple-element.85.gout, f32[8,1408]{1,0:T(8,128)} %add.23.feed_sums, f32[8,768]{1,0:T(8,128)} %add.24.first_sums), custom_call_target="tpu_custom_call" | custom-call | tf_op jit(solution)/shard_map/pallas_call | solution.py:1135
  770.8 6.8 all-to-all-start.2
  777.6 4.9 slice_bitcast_fusion
  782.5 3.8 collective-permute-start.7
  786.3 2.2 collective-permute-start.13
  788.5 83.6 %all-to-all-done.2.g0 = bf16[16,2,80,768]{3,2,1,0:T(8,128)(2,1)} async-done(((bf16[16,2,80,768]{3,2,1,0:T(8,128)(2,1)}), bf16[16,2,80,768]{3,2,1,0:T(8,128)(2,1)}, u32[]{:S(2)}, u32[]{:S(2)}) %all-to-all-start.2) | async-done | bytes 3932192 | tf_op jit(solution)/shard_map/all_to_all | solution.py:1259
  872.0 14.0 %shard_map.180 = (f32[6,1384,128]{2,1,0:T(8,128)}, f32[8,768]{1,0:T(8,128)}) custom-call(bf16[16,2,80,768]{3,2,1,0:T(8,128)(2,1)} %all-to-all-done.c0, bf16[16,2,80,768]{3,2,1,0:T(8,128)(2,1)} %all-to-all-done.1.c1, bf16[16,2,80,768]{3,2,1,0:T(8,128)(2,1)} %all-to-all-done.2.g0, bf16[16,2,80,768]{3,2,1,0:T(8,128)(2,1)} %all-to-all-done.3.g1), custom_call_target="tpu_custom_call" | custom-call | tf_op jit(solution)/shard_map/pallas_call | solution.py:1159
  887.3 4.2 collective-permute-done.14.next_ref
  892.1 11.6 %shard_map.181 = f32[1,624128]{1,0:T(1,128)} custom-call(s32[1]{0:T(128)} %bitcast.8.shard_ref, f32[6,1384,128]{2,1,0:T(8,128)} %get-tuple-element.74.tiles_ref, f32[8,768]{1,0:T(8,128)} %copy-done.20), custom_call_target="tpu_custom_call" | custom-call | tf_op jit(solution)/shard_map/pallas_call | solution.py:1196
  903.8 16.4 %collective-permute-start.15 = (f32[1,624128]{1,0:T(1,128)}, f32[1,624128]{1,0:T(1,128)}, u32[]{:S(2)}, u32[]{:S(2)}) collective-permute-start(f32[1,624128]{1,0:T(1,128)} %shard_map.181), channel_id=1, source_target_pairs={{0,0},{1,2},{2,1},{3,3},{4,4},{5,6},{6,5},{7,7},{8,8},{9,10},{10,9... | collective-permute-start | bytes 7489544 | tf_op jit(solution)/shard_map/ppermute | solution.py:1223
  920.2 97.6 %all-reduce.6.cloned.1.call-done = f32[1650688]{0:T(1024)} async-done(((f32[1650688]{0:T(1024)}), f32[1650688]{0:T(1024)}) %all-reduce.6.cloned.1.call-update) | async-done | bytes 6602768
  1017.8 1.7 dynamic-slice
  1021.1 3.4 copy.55
  1024.5 4.6 copy.56
  (96 shorter events, 39.1 us)
Async XLA Ops:
  7.2 77.9 %all-gather.3.cloned.1.call-start = ((), (), s32[]{:S(2)}) async-start(), calls=%async_computation.4 | async-start | bytes 6809088 | tf_op jit(solution)/shard_map/all_gather | solution.py:1230
  12.4 128.0 %collective-permute-start.1 = (bf16[1728,768]{1,0:T(8,128)(2,1)}, bf16[1728,768]{1,0:T(8,128)(2,1)S(1)}, u32[]{:S(2)}, u32[]{:S(2)}) collective-permute-start(bf16[1728,768]{1,0:T(8,128)(2,1)} %pad.11), channel_id=1, source_target_pairs={{0,0},{1,2},{2,1},{3,3},{4,4},{5,6},{6,5},{7,7},{8,8},{9,10},{10,9... | collective-permute-start | bytes 7962632 | tf_op jit(solution)/shard_map/ppermute | solution.py:1223
  18.8 42.0 %collective-permute-start.2 = (bf16[2,1728,128]{2,1,0:T(8,128)(2,1)S(1)}, bf16[2,1728,128]{2,1,0:T(8,128)(2,1)S(1)}, u32[]{:S(2)}, u32[]{:S(2)}) collective-permute-start(bf16[2,1728,128]{2,1,0:T(8,128)(2,1)S(1)} %pad.12), channel_id=1, source_target_pairs={{0,0},{1,2},{2,1},{3,3},{4,4},{5,6},{6,5},{7,7},{8,8},{9,10},{10,9... | collective-permute-start | bytes 2654216 | tf_op jit(solution)/shard_map/ppermute | solution.py:1223
  140.4 1.5 copy-start.4
  149.1 187.8 %collective-permute-start.3 = (bf16[24,80,768]{2,1,0:T(8,128)(2,1)}, bf16[24,80,768]{2,1,0:T(8,128)(2,1)S(1)}, u32[]{:S(2)}, u32[]{:S(2)}) collective-permute-start(bf16[24,80,768]{2,1,0:T(8,128)(2,1)} %shard_map.166.own_ref), channel_id=1, source_target_pairs={{0,2},{1,3},{2,0},{3,1},{4,6},{5,7},{6,4},{7,5},{8,10},{9,11},{10,... | collective-permute-start | bytes 8847368 | tf_op jit(solution)/shard_map/ppermute | solution.py:1224
  159.3 1.3 copy-start.1
  160.6 0.9 copy-start.3
  329.6 6.6 copy-start
  336.3 0.6 copy-start.2
  336.9 1.7 copy-start.12
  366.2 6.1 copy-start.7
  366.2 21.9 %collective-permute-start.4 = (bf16[24,80,768]{2,1,0:T(8,128)(2,1)}, bf16[24,80,768]{2,1,0:T(8,128)(2,1)S(1)}, u32[]{:S(2)}, u32[]{:S(2)}) collective-permute-start(bf16[24,80,768]{2,1,0:T(8,128)(2,1)} %get-tuple-element.52.own_ref), channel_id=1, source_target_pairs={{0,2},{1,3},{2,0},{3,1},{4,6},{5,7},{6,4},{7,5},{8,10},{9,11},{10,... | collective-permute-start | bytes 8847368 | tf_op jit(solution)/shard_map/ppermute | solution.py:1224
  372.4 1.9 copy-start.9
  374.3 115.0 %all-to-all-start = ((bf16[16,2,80,768]{3,2,1,0:T(8,128)(2,1)}), bf16[16,2,80,768]{3,2,1,0:T(8,128)(2,1)}, u32[]{:S(2)}, u32[]{:S(2)}) async-start(bf16[16,2,80,768]{3,2,1,0:T(8,128)(2,1)} %bitcast.21), calls=%async_computation | async-start | bytes 7864320 | tf_op jit(solution)/shard_map/all_to_all | solution.py:1259
  378.9 8.5 collective-permute-start
  388.1 1.6 copy-start.13
  422.2 5.6 collective-permute-start.5
  425.7 101.4 %collective-permute-start.8 = (bf16[1728,768]{1,0:T(8,128)(2,1)}, bf16[1728,768]{1,0:T(8,128)(2,1)}, u32[]{:S(2)}, u32[]{:S(2)}) collective-permute-start(bf16[1728,768]{1,0:T(8,128)(2,1)} %pad.13), channel_id=1, source_target_pairs={{0,0},{1,2},{2,1},{3,3},{4,4},{5,6},{6,5},{7,7},{8,8},{9,10},{10,9... | collective-permute-start | bytes 7962632 | tf_op jit(solution)/shard_map/ppermute | solution.py:1223
  427.8 1.6 copy-start.15
  457.0 29.1 %copy-start.6 = (bf16[24,80,768]{2,1,0:T(8,128)(2,1)S(1)}, bf16[24,80,768]{2,1,0:T(8,128)(2,1)}, u32[]{:S(2)}) copy-start(bf16[24,80,768]{2,1,0:T(8,128)(2,1)} %get-tuple-element.71) | copy-start | bytes 8847364
  457.0 43.5 %collective-permute-start.6 = (bf16[24,80,768]{2,1,0:T(8,128)(2,1)}, bf16[24,80,768]{2,1,0:T(8,128)(2,1)S(1)}, u32[]{:S(2)}, u32[]{:S(2)}) collective-permute-start(bf16[24,80,768]{2,1,0:T(8,128)(2,1)} %get-tuple-element.56.own_ref), channel_id=1, source_target_pairs={{0,2},{1,3},{2,0},{3,1},{4,6},{5,7},{6,4},{7,5},{8,10},{9,11},{10,... | collective-permute-start | bytes 8847368 | tf_op jit(solution)/shard_map/ppermute | solution.py:1224
  489.3 107.6 %all-to-all-start.1 = ((bf16[16,2,80,768]{3,2,1,0:T(8,128)(2,1)}), bf16[16,2,80,768]{3,2,1,0:T(8,128)(2,1)}, u32[]{:S(2)}, u32[]{:S(2)}) async-start(bf16[16,2,80,768]{3,2,1,0:T(8,128)(2,1)} %bitcast.10), calls=%async_computation.1 | async-start | bytes 7864320 | tf_op jit(solution)/shard_map/all_to_all | solution.py:1259
  500.5 1.6 copy-start.11
  547.2 5.7 collective-permute-start.9
  552.9 1.7 copy-start.17
  584.0 9.7 copy-start.8
  584.0 20.1 %collective-permute-start.10 = (bf16[24,80,768]{2,1,0:T(8,128)(2,1)}, bf16[24,80,768]{2,1,0:T(8,128)(2,1)S(1)}, u32[]{:S(2)}, u32[]{:S(2)}) collective-permute-start(bf16[24,80,768]{2,1,0:T(8,128)(2,1)} %get-tuple-element.61.own_ref), channel_id=1, source_target_pairs={{0,2},{1,3},{2,0},{3,1},{4,6},{5,7},{6,4},{7,5},{8,10},{9,11},{10,... | collective-permute-start | bytes 8847368 | tf_op jit(solution)/shard_map/ppermute | solution.py:1224
  596.9 173.8 %all-to-all-start.3 = ((bf16[16,2,80,768]{3,2,1,0:T(8,128)(2,1)}), bf16[16,2,80,768]{3,2,1,0:T(8,128)(2,1)}, u32[]{:S(2)}, u32[]{:S(2)}) async-start(bf16[16,2,80,768]{3,2,1,0:T(8,128)(2,1)} %bitcast.12), calls=%async_computation.3 | async-start | bytes 7864320 | tf_op jit(solution)/shard_map/all_to_all | solution.py:1259
  604.1 1.6 copy-start.14
  641.1 37.2 %copy-start.18 = (f32[8,1408]{1,0:T(8,128)S(1)}, f32[8,1408]{1,0:T(8,128)}, u32[]{:S(2)}) copy-start(f32[8,1408]{1,0:T(8,128)} %get-tuple-element.86) | copy-start | bytes 135172
  641.2 37.2 %copy-start.19 = (f32[8,1408]{1,0:T(8,128)S(1)}, f32[8,1408]{1,0:T(8,128)}, u32[]{:S(2)}) copy-start(f32[8,1408]{1,0:T(8,128)} %get-tuple-element.87) | copy-start | bytes 135172
  641.2 5.7 collective-permute-start.11
  646.8 1.6 copy-start.16
  677.9 40.0 %collective-permute-start.12 = (bf16[24,80,768]{2,1,0:T(8,128)(2,1)}, bf16[24,80,768]{2,1,0:T(8,128)(2,1)}, u32[]{:S(2)}, u32[]{:S(2)}) collective-permute-start(bf16[24,80,768]{2,1,0:T(8,128)(2,1)} %get-tuple-element.67.own_ref), channel_id=1, source_target_pairs={{0,2},{1,3},{2,0},{3,1},{4,6},{5,7},{6,4},{7,5},{8,10},{9,11},{10,... | collective-permute-start | bytes 8847368 | tf_op jit(solution)/shard_map/ppermute | solution.py:1224
  710.5 5.4 copy-start.5
  716.0 1.9 copy-start.10
  717.9 14.6 %copy-start.21 = (f32[8,768]{1,0:T(8,128)S(1)}, f32[8,768]{1,0:T(8,128)}, u32[]{:S(2)}) copy-start(f32[8,768]{1,0:T(8,128)} %get-tuple-element.88) | copy-start | bytes 73732
  770.8 101.3 %all-to-all-start.2 = ((bf16[16,2,80,768]{3,2,1,0:T(8,128)(2,1)}), bf16[16,2,80,768]{3,2,1,0:T(8,128)(2,1)}, u32[]{:S(2)}, u32[]{:S(2)}) async-start(bf16[16,2,80,768]{3,2,1,0:T(8,128)(2,1)} %bitcast.22), calls=%async_computation.2 | async-start | bytes 7864320 | tf_op jit(solution)/shard_map/all_to_all | solution.py:1259
  777.5 240.3 %all-reduce.6.cloned.1.call-start = ((), (), s32[]{:S(2)}) async-start(), calls=%async_computation.5 | async-start | bytes 13205504
  782.5 137.8 %collective-permute-start.7 = (bf16[1728,768]{1,0:T(8,128)(2,1)}, bf16[1728,768]{1,0:T(8,128)(2,1)S(1)}, u32[]{:S(2)}, u32[]{:S(2)}) collective-permute-start(bf16[1728,768]{1,0:T(8,128)(2,1)} %get-tuple-element.57), channel_id=1, source_target_pairs={{0,0},{1,2},{2,1},{3,3},{4,4},{5,6},{6,5},{7,7},{8,8},{9,10},{10,9... | collective-permute-start | bytes 7962632 | tf_op jit(solution)/shard_map/ppermute | solution.py:1223
  786.3 133.9 %collective-permute-start.13 = (bf16[1728,768]{1,0:T(8,128)(2,1)}, bf16[1728,768]{1,0:T(8,128)(2,1)}, u32[]{:S(2)}, u32[]{:S(2)}) collective-permute-start(bf16[1728,768]{1,0:T(8,128)(2,1)} %get-tuple-element.69), channel_id=1, source_target_pairs={{0,0},{1,2},{2,1},{3,3},{4,4},{5,6},{6,5},{7,7},{8,8},{9,10},{10,9... | collective-permute-start | bytes 7962632 | tf_op jit(solution)/shard_map/ppermute | solution.py:1223
  886.0 5.5 collective-permute-start.14
  891.5 0.6 copy-start.20
  903.8 115.8 %collective-permute-start.15 = (f32[1,624128]{1,0:T(1,128)}, f32[1,624128]{1,0:T(1,128)}, u32[]{:S(2)}, u32[]{:S(2)}) collective-permute-start(f32[1,624128]{1,0:T(1,128)} %shard_map.181), channel_id=1, source_target_pairs={{0,0},{1,2},{2,1},{3,3},{4,4},{5,6},{6,5},{7,7},{8,8},{9,10},{10,9... | collective-permute-start | bytes 7489544 | tf_op jit(solution)/shard_map/ppermute | solution.py:1223
Sparse Core Ops, SparseCore 0:
  11.4 73.5 all-gather.2
  784.2 233.6 all-reduce.5

commit v2 on v1

--- a/solution.py
+++ b/solution.py
@@ -305,15 +305,16 @@
 CELLS = ROWS * NLON
 DP = 768
 HP = 1408
-KP = 80
-GROUPS = 5
-GK = 16
+KP = 72
+GROUPS = 9
+GK = 8
+DEPTH = 8
 WROWS = 672
 BLK = 4
 BC = BLK * NLON
 WIN = 992
 MAIN = 944
-HEAD = 480
+HEAD = 416
 BF = jnp.bfloat16
 F32 = jnp.float32
 MB = 2**20
@@ -323,6 +324,9 @@
     return pltpu.CompilerParams(vmem_limit_bytes=limit * MB, **more)
 
 
+LIGHT = pl.CostEstimate(flops=1, bytes_accessed=1, transcendentals=0)
+
+
 def vspec():
     return pl.BlockSpec(memory_space=pltpu.VMEM)
 
@@ -350,29 +354,25 @@
 
 
 def column_order():
-    places = -np.ones(KP, np.int64)
+    places = np.zeros(KP, np.int64)
     for group in range(GROUPS):
-        for i in range(8):
-            order = 8 * group + i
-            if order < ORDERS:
-                places[GK * group + i] = order
-                places[GK * group + 8 + i] = ORDERS + order
+        for i in range(4):
+            places[GK * group + i] = 4 * group + i
+            places[GK * group + 4 + i] = ORDERS + 4 * group + i
     return places
 
 
 def plan_tables():
     fourier, inverse, analysis, synthesis = spectral_tables(NLAT, NLON, LDEG, ORDERS)
-    places = column_order()
-    held = places >= 0
-    take = np.where(held, places, 0)
-    fourier = fourier[:, take] * held
-    inverse = inverse[take, :] * held[:, None]
-    analysis = analysis[:, :, take] * held
-    synthesis = synthesis[:, :, take] * held
+    take = column_order()
+    fourier = fourier[:, take]
+    inverse = inverse[take, :]
+    analysis = analysis[:, :, take]
+    synthesis = synthesis[:, :, take]
     eye = np.eye(GK, dtype=np.float32)
 
     def blocks(table):
-        out = np.zeros((2, 2, GROUPS, 384, 384), np.float32)
+        out = np.zeros((2, GROUPS, 192, 384), np.float32)
         for own in range(2):
             for which in range(2):
                 half = own if which == 0 else 1 - own
@@ -380,7 +380,7 @@
                     part = table[24 * own : 24 * own + 24, 24 * half : 24 * half + 24]
                     part = part[:, :, GK * group : GK * group + GK]
                     full = np.einsum("pqi,ij->piqj", part, eye)
-                    out[own, which, group] = full.reshape(384, 384)
+                    out[own, group, :, 192 * which : 192 * which + 192] = full.reshape(192, 192)
         return out.astype(BF)
 
     by_degree = np.transpose
@@ -497,6 +497,7 @@
             pltpu.VMEM((5, 1024, 128), F32),
             pltpu.VMEM((8, 128), F32),
         ],
+        cost_estimate=LIGHT,
         compiler_params=params(),
     )(shard, flat)
 
@@ -507,8 +508,9 @@
 
 
 def mlp_kernel(flat_ref, in_ref, out_ref, vec_ref, flat, tin, tout):
-    count = flat_ref.shape[0]
-    flat[0:count, :] = flat_ref[...].astype(F32)
+    count, rows, _ = flat_ref.shape
+    for k in range(count):
+        flat[rows * k : rows * k + rows, :] = flat_ref[k].astype(F32)
     lane = lax.broadcasted_iota(jnp.int32, (1, 128), 1)
     vec_ref[...] = jnp.zeros_like(vec_ref)
     for row, (place, length) in enumerate(VECTORS):
@@ -556,6 +558,7 @@
             pltpu.VMEM((11, 1024, 128), F32),
             pltpu.VMEM((6, 2048, 128), F32),
         ],
+        cost_estimate=LIGHT,
         compiler_params=params(),
     )(flat)
 
@@ -777,6 +780,7 @@
             pltpu.SemaphoreType.DMA((3, count)),
             pltpu.SemaphoreType.DMA((2 + 2 * count,)),
         ],
+        cost_estimate=LIGHT,
         compiler_params=params(30, collective_id=0, has_side_effects=True),
     )(main, side)
 
@@ -808,92 +812,133 @@
     )
     for j in range(BLK):
         piece = joined[NLON * j : NLON * j + NLON, :]
-        out_ref[j] = split_dot(table_ref[...], piece).astype(BF)
+        out_ref[j] = split_dot(table_ref[...], piece).astype(BF).reshape(GROUPS, GK, DP)
 
 
 def modes(state, noise, vectors, table):
     return pl.pallas_call(
         modes_kernel,
         grid=(ROWS // BLK,),
-        out_shape=jax.ShapeDtypeStruct((ROWS, KP, DP), BF),
+        out_shape=jax.ShapeDtypeStruct((ROWS, GROUPS, GK, DP), BF),
         in_specs=[
             pl.BlockSpec((BC, DP), lambda i: (i, 0)),
             pl.BlockSpec((BC, 128), lambda i: (i, 0)),
             pl.BlockSpec((8, HP), lambda i: (0, 0)),
             pl.BlockSpec((KP, 3 * NLON), lambda i: (0, 0)),
         ],
-        out_specs=pl.BlockSpec((BLK, KP, DP), lambda i: (i, 0, 0)),
+        out_specs=pl.BlockSpec((BLK, GROUPS, GK, DP), lambda i: (i, 0, 0, 0)),
+        cost_estimate=LIGHT,
         compiler_params=params(),
     )(state, noise, vectors, table)
 
 
 def legendre(table_ref, own_ref, other_ref, out_ref):
     for group in range(GROUPS):
-        at = slice(GK * group, GK * group + GK)
-        total = dot(table_ref[0, 0, group], own_ref[:, at, :].reshape(384, DP))
-        total = total + dot(table_ref[0, 1, group], other_ref[:, at, :].reshape(384, DP))
-        out_ref[:, at, :] = total.astype(out_ref.dtype).reshape(24, GK, DP)
-
-
-def fetch(w_ref, w_buf, sem, degree, slot):
+        both = jnp.concatenate(
+            [own_ref[:, group].reshape(192, DP), other_ref[:, group].reshape(192, DP)], axis=0
+        )
+        total = dot(table_ref[0, group], both)
+        out_ref[:, group] = total.astype(out_ref.dtype).reshape(24, GK, DP)
+
+
+def fetch(w_ref, w_buf, sem, degree):
+    slot = degree % DEPTH
     first = pl.multiple_of((CIN * degree) // 16 * 16, 16)
     return pltpu.make_async_copy(w_ref.at[pl.ds(first, WROWS)], w_buf.at[slot], sem.at[slot])
 
 
-def mix_kernel(half_ref, own_ref, other_ref, table_ref, column_ref, w_ref, coeff_ref, mixed_ref, w_buf, sem):
-    fetch(w_ref, w_buf, sem, 0, 0).start()
+def fetch_next(w_ref, w_buf, sem, degree):
+    fetch(w_ref, w_buf, sem, degree).wait()
+
+
+def fetch_ahead(w_ref, w_buf, sem, degree):
+    @pl.when(degree + DEPTH < DEGS)
+    def _():
+        fetch(w_ref, w_buf, sem, degree + DEPTH).start()
+
+
+C_TILES = 9
+G_TILES = 11
+OWNERS = 16
+
+
+def owner_degrees(owner):
+    first = 3 * (owner // 2)
+    return first + 2 * (owner % 2), first + 1
+
+
+def pack_tiles(block_ref, parts_ref, middle_tiles):
+    lane = lax.broadcasted_iota(jnp.int32, (KP, 128), 1)
+    for owner in range(OWNERS):
+        own, middle = owner_degrees(owner)
+        for m in range(5):
+            at = slice(128 * m, 128 * m + 128)
+            parts_ref[owner, m] = block_ref[own, :, :, at].reshape(KP, 128)
+        for n, m in enumerate(middle_tiles[owner % 2]):
+            at = slice(128 * m, 128 * m + 128)
+            parts_ref[owner, 5 + n] = block_ref[middle, :, :, at].reshape(KP, 128)
+        one = block_ref[own, :, :, 640:].reshape(KP, 128).astype(F32)
+        two = block_ref[middle, :, :, 640:].reshape(KP, 128).astype(F32)
+        two = pltpu.roll(two, 16, 1)
+        last = parts_ref.shape[1] - 1
+        parts_ref[owner, last] = jnp.where(lane < 16, one, two).astype(BF)
+
+
+def mix_kernel(
+    half_ref, own_ref, other_ref, table_ref, column_ref, w_ref, parts_ref, mixed_ref, coeff_ref, w_buf, sem,
+):
+    for degree in range(DEPTH):
+        fetch(w_ref, w_buf, sem, degree).start()
     legendre(table_ref, own_ref, other_ref, coeff_ref)
+    pack_tiles(coeff_ref, parts_ref, ((0, 1, 2), (2, 3, 4)))
     lane = lax.broadcasted_iota(jnp.int32, (KP, 128), 1)
 
     def one(degree, carry):
-        slot = degree % 2
-
-        @pl.when(degree + 1 < DEGS)
-        def _():
-            fetch(w_ref, w_buf, sem, degree + 1, 1 - slot).start()
-
-        fetch(w_ref, w_buf, sem, degree, slot).wait()
-        coeffs = coeff_ref[degree].astype(F32)
+        fetch_next(w_ref, w_buf, sem, degree)
+        coeffs = coeff_ref[degree].reshape(KP, DP).astype(F32)
         moved = pltpu.roll(coeffs, (CIN * degree) % 16, 1)
-        mixed = dot(moved[:, :WROWS].astype(BF), w_buf[slot])
-        mixed_ref[degree, :, :640] = mixed.astype(BF)
+        mixed = dot(moved[:, :WROWS].astype(BF), w_buf[degree % DEPTH])
         last = jnp.sum(coeffs * column_ref[pl.ds(degree, 1), :], axis=1, keepdims=True)
-        mixed_ref[degree, :, 640:] = jnp.where(lane < 1, last, 0.0).astype(BF)
+        mixed = jnp.concatenate([mixed, jnp.where(lane < 1, last, 0.0)], axis=1)
+        mixed_ref[degree] = mixed.astype(BF).reshape(GROUPS, GK, DP)
+        fetch_ahead(w_ref, w_buf, sem, degree)
         return carry
 
     lax.fori_loop(0, DEGS, one, 0)
 
 
-def mix_back_kernel(half_ref, own_ref, other_ref, table_ref, column_ref, w_ref, grad_ref, out_ref, w_buf, wide, sem):
-    fetch(w_ref, w_buf, sem, 0, 0).start()
+def mix_back_kernel(
+    half_ref, own_ref, other_ref, table_ref, column_ref, w_ref, parts_ref, out_ref, grad_ref, w_buf, wide, sem,
+):
+    for degree in range(DEPTH):
+        fetch(w_ref, w_buf, sem, degree).start()
     legendre(table_ref, own_ref, other_ref, grad_ref)
+    every = (0, 1, 2, 3, 4)
+    pack_tiles(grad_ref, parts_ref, (every, every))
     keep = lax.broadcasted_iota(jnp.int32, (KP, DP), 1) < CIN
     wide[...] = jnp.zeros_like(wide)
 
     def one(degree, carry):
-        slot = degree % 2
-
-        @pl.when(degree + 1 < DEGS)
-        def _():
-            fetch(w_ref, w_buf, sem, degree + 1, 1 - slot).start()
-
-        fetch(w_ref, w_buf, sem, degree, slot).wait()
-        wide[:, :WROWS] = dot_nt(grad_ref[degree, :, :640], w_buf[slot])
+        fetch_next(w_ref, w_buf, sem, degree)
+        grad = grad_ref[degree].reshape(KP, DP)
+        wide[:, :WROWS] = dot_nt(grad[:, :640], w_buf[degree % DEPTH])
         back = pltpu.roll(wide[...], DP - (CIN * degree) % 16, 1)
-        last = grad_ref[degree, :, 640:].astype(F32)[:, 0:1]
+        last = grad[:, 640:].astype(F32)[:, 0:1]
         back = back + last * column_ref[pl.ds(degree, 1), :]
-        out_ref[degree] = jnp.where(keep, back, 0.0).astype(BF)
+        out_ref[degree] = jnp.where(keep, back, 0.0).astype(BF).reshape(GROUPS, GK, DP)
+        fetch_ahead(w_ref, w_buf, sem, degree)
         return carry
 
     lax.fori_loop(0, DEGS, one, 0)
 
 
 def mix(half, own, other, table, weights, column, back):
-    whole = pl.BlockSpec((24, KP, DP), lambda i, h: (0, 0, 0))
-    scratch = [pltpu.VMEM((2, WROWS, 640), BF)]
+    whole = fixed(24, GROUPS, GK, DP)
+    tiles = G_TILES if back else C_TILES
+    scratch = [pltpu.VMEM((24, GROUPS, GK, DP), BF), pltpu.VMEM((DEPTH, WROWS, 640), BF)]
     if back:
         scratch.append(pltpu.VMEM((KP, DP), F32))
-    scratch.append(pltpu.SemaphoreType.DMA((2,)))
+    scratch.append(pltpu.SemaphoreType.DMA((DEPTH,)))
     return pl.pallas_call(
         mix_back_kernel if back else mix_kernel,
         grid_spec=pltpu.PrefetchScalarGridSpec(
@@ -902,14 +947,18 @@
             in_specs=[
                 whole,
                 whole,
-                pl.BlockSpec((1, 2, GROUPS, 384, 384), lambda i, h: (h[0], 0, 0, 0, 0)),
-                pl.BlockSpec((DEGS, DP), lambda i, h: (0, 0)),
+                table_spec(),
+                fixed(DEGS, DP),
                 pl.BlockSpec(memory_space=pl.ANY),
             ],
-            out_specs=(whole, whole),
+            out_specs=(fixed(OWNERS, tiles, KP, 128), whole),
             scratch_shapes=scratch,
         ),
-        out_shape=(jax.ShapeDtypeStruct((24, KP, DP), BF),) * 2,
+        out_shape=(
+            jax.ShapeDtypeStruct((OWNERS, tiles, KP, 128), BF),
+            jax.ShapeDtypeStruct((24, GROUPS, GK, DP), BF),
+        ),
+        cost_estimate=LIGHT,
         compiler_params=params(),
     )(half, own, other, table, column, weights)
 
@@ -928,7 +977,7 @@
         legendre(table_ref, own_ref, other_ref, lat)
 
     mask = mask_ref[0]
-    parts = [split_dot(inverse_ref[...], lat[BLK * i + j]) for j in range(BLK)]
+    parts = [split_dot(inverse_ref[...], lat[BLK * i + j].reshape(KP, DP)) for j in range(BLK)]
     middle = state_ref[...].astype(F32) + mask * jnp.concatenate(parts, axis=0)
     middle_ref[...] = middle
     unit, scale = unit_of(middle, lane_mask())
@@ -954,7 +1003,7 @@
 
 
 def table_spec():
-    return pl.BlockSpec((1, 2, GROUPS, 384, 384), lambda i, h, *m: (h[0], 0, 0, 0, 0))
+    return pl.BlockSpec((1, GROUPS, 192, 384), lambda i, h, *m: (h[0], 0, 0, 0))
 
 
 def feed(half, mask, own, other, table, inverse_t, state, vectors, w_in, w_out, last):
@@ -965,15 +1014,16 @@
             num_scalar_prefetch=2,
             grid=(ROWS // BLK,),
             in_specs=[
-                fixed(24, KP, DP), fixed(24, KP, DP), table_spec(), fixed(NLON, 3 * KP), cell_spec(DP),
+                fixed(24, GROUPS, GK, DP), fixed(24, GROUPS, GK, DP), table_spec(), fixed(NLON, 3 * KP), cell_spec(DP),
                 fixed(8, HP), fixed(DP, HP), fixed(HP, DP),
             ],
             out_specs=(cell_spec(DP), cell_spec(DP), cell_spec(DP), cell_spec(HP), cell_spec(HP)),
-            scratch_shapes=[pltpu.VMEM((24, KP, DP), F32)],
+            scratch_shapes=[pltpu.VMEM((24, GROUPS, GK, DP), F32)],
         ),
         out_shape=(
             cells(DP, BF if last else F32), cells(DP, F32), cells(DP, BF), cells(HP, BF), cells(HP, BF),
         ),
+        cost_estimate=LIGHT,
         compiler_params=params(),
     )(half, mask, own, other, table, inverse_t, state, vectors, w_in, w_out)
 
@@ -1008,7 +1058,7 @@
     total = mask * total
     for j in range(BLK):
         piece = total[NLON * j : NLON * j + NLON, :]
-        modes_ref[j] = split_dot(inverse_ref[...], piece).astype(BF)
+        modes_ref[j] = split_dot(inverse_ref[...], piece).astype(BF).reshape(GROUPS, GK, DP)
 
 
 def feed_back(mask, grad, slope, middle, vectors, w_in, w_out, inverse):
@@ -1024,13 +1074,14 @@
             ],
             out_specs=(
                 cell_spec(DP), cell_spec(HP), cell_spec(DP),
-                pl.BlockSpec((BLK, KP, DP), lambda i, *h: (i, 0, 0)), fixed(8, HP),
+                pl.BlockSpec((BLK, GROUPS, GK, DP), lambda i, *h: (i, 0, 0, 0)), fixed(8, HP),
             ),
         ),
         out_shape=(
-            cells(DP, BF), cells(HP, BF), cells(DP, F32), jax.ShapeDtypeStruct((ROWS, KP, DP), BF),
+            cells(DP, BF), cells(HP, BF), cells(DP, F32), jax.ShapeDtypeStruct((ROWS, GROUPS, GK, DP), BF),
             jax.ShapeDtypeStruct((8, HP), F32),
         ),
+        cost_estimate=LIGHT,
         compiler_params=params(),
     )(mask, grad, slope, middle, vectors, w_in, w_out, inverse)
 
@@ -1045,7 +1096,7 @@
         legendre(table_ref, own_ref, other_ref, lat)
         sums_ref[...] = jnp.zeros_like(sums_ref)
 
-    parts = [split_dot(fourier_ref[...], lat[BLK * i + j]) for j in range(BLK)]
+    parts = [split_dot(fourier_ref[...], lat[BLK * i + j].reshape(KP, DP)) for j in range(BLK)]
     upstream = jnp.concatenate(parts, axis=0)
     unit, scale = unit_of(state_ref[...].astype(F32), lane_mask())
     sums_ref[0:1, :] += jnp.sum(upstream * unit, axis=0, keepdims=True)
@@ -1061,15 +1112,16 @@
             num_scalar_prefetch=1,
             grid=(ROWS // BLK,),
             in_specs=[
-                fixed(24, KP, DP), fixed(24, KP, DP), table_spec(), fixed(NLON, 3 * KP), cell_spec(DP),
+                fixed(24, GROUPS, GK, DP), fixed(24, GROUPS, GK, DP), table_spec(), fixed(NLON, 3 * KP), cell_spec(DP),
                 cell_spec(DP), fixed(8, HP),
             ],
             out_specs=(cell_spec(DP), fixed(8, DP)),
-            scratch_shapes=[pltpu.VMEM((24, KP, DP), F32)],
+            scratch_shapes=[pltpu.VMEM((24, GROUPS, GK, DP), F32)],
         ),
         out_shape=(
             jax.ShapeDtypeStruct((CELLS, DP), BF if last else F32), jax.ShapeDtypeStruct((8, DP), F32),
         ),
+        cost_estimate=LIGHT,
         compiler_params=params(),
     )(half, own, other, table, fourier, state, gm, vectors)
 
@@ -1087,7 +1139,7 @@
             tout[m, at, :] = part[:, 128 * m : 128 * m + 128]
 
 
-def mlp_flat_kernel(gin, gout, feed_sums, first_sums, flat_ref, tin, tout):
+def mlp_flat_kernel(gin, gout, feed_sums, first_sums, pack_ref, tin, tout, flat_ref):
     tin[:, :DP, :] = gin[...]
     tout[:, :HP, :] = gout[...]
     tin[:, DP:, :] = jnp.zeros((11, 1024 - DP, 128), F32)
@@ -1118,9 +1170,14 @@
             return tout[m, pl.ds(t + 1024 * part, 8, stride=128), :]
 
         rows_in(flat_ref, OUT_AT // 128 + 641 * 8 * part, OUT_AT % 128, 1, 5, 6, get_out, 128, 2)
+    for k in range(32):
+        piece = flat_ref[SHARD_ROWS * k : SHARD_ROWS * k + SHARD_ROWS, :]
+        piece = jnp.concatenate([piece, jnp.zeros((416 - SHARD_ROWS, 128), F32)], axis=0)
+        pack_ref[(k // 2) % 2, (k // 4) * 2 + k % 2] = piece.astype(BF)
 
 
 FLAT_ROWS = 16784
+SHARD_ROWS = 403
 
 
 def mlp_grads(hidden, pre, active, result, feed_sums, first_sums):
@@ -1130,39 +1187,76 @@
         in_specs=[vspec()] * 8,
         out_specs=(vspec(), vspec()),
         scratch_shapes=[pltpu.VMEM((DP, 2 * CELLS), BF)],
+        cost_estimate=LIGHT,
         compiler_params=params(62),
     )(*hidden, *pre, *active, *result)
     return pl.pallas_call(
         mlp_flat_kernel,
-        out_shape=jax.ShapeDtypeStruct((FLAT_ROWS, 128), F32),
+        out_shape=jax.ShapeDtypeStruct((2, 16, 416, 128), BF),
         in_specs=[vspec()] * 4,
         out_specs=vspec(),
-        scratch_shapes=[pltpu.VMEM((11, 1024, 128), F32), pltpu.VMEM((6, 2048, 128), F32)],
+        scratch_shapes=[
+            pltpu.VMEM((11, 1024, 128), F32),
+            pltpu.VMEM((6, 2048, 128), F32),
+            pltpu.VMEM((FLAT_ROWS, 128), F32),
+        ],
+        cost_estimate=LIGHT,
         compiler_params=params(62),
     )(gin, gout, feed_sums, first_sums)
 
 
-def spectral_grad_kernel(c0, c1, g0, g1, tiles_ref, head_ref):
-    rows = 16 * KP
+def spectral_grad_kernel(odd_ref, c0, c1, g0, g1, tiles_ref, head_ref):
+    rows = OWNERS * KP
+    lane = lax.broadcasted_iota(jnp.int32, (DP, 128), 1)
     tiles_ref[:, 0:16, :] = jnp.zeros((6, 16, 128), F32)
-    for e in range(2):
-        total = dot_tn(c0[:, e].reshape(rows, DP), g0[:, e].reshape(rows, DP))
-        total = total + dot_tn(c1[:, e].reshape(rows, DP), g1[:, e].reshape(rows, DP))
-        if e == 0:
-            head_ref[...] = total[0:8, :]
+    tiles_ref[:, 16 + 2 * CIN :, :] = jnp.zeros((6, 1384 - 16 - 2 * CIN, 128), F32)
+
+    def side(ref, first, count):
+        take = [ref[:, m].reshape(rows, 128) for m in list(range(first, first + count)) + [ref.shape[1] - 1]]
+        return jnp.concatenate(take, axis=1)
+
+    def product(c_first, c_count, g_first):
+        total = dot_tn(side(c0, c_first, c_count), side(g0, g_first, 5))
+        return total + dot_tn(side(c1, c_first, c_count), side(g1, g_first, 5))
+
+    def save(start, part, first, count, column):
         for m in range(6):
-            tiles_ref[m, 16 + CIN * e : 16 + CIN * e + CIN, :] = total[:CIN, 128 * m : 128 * m + 128]
-    tiles_ref[:, 16 + 2 * CIN :, :] = jnp.zeros((6, 1384 - 16 - 2 * CIN, 128), F32)
-
-
-def spectral_grads(coeffs, grads):
+            piece = part[first : first + count, 128 * m : 128 * m + 128]
+            if m == 5:
+                if column:
+                    piece = pltpu.roll(piece, 128 - column, 1)
+                piece = jnp.where(lane[:count] < 1, piece, 0.0)
+            tiles_ref[m, start : start + count, :] = piece
+
+    own = product(0, 5, 0)
+    head_ref[...] = jnp.concatenate(
+        [own[0:8, :640], jnp.where(lane[:8] < 1, own[0:8, 640:], 0.0)], axis=1
+    )
+    middle = product(5, 3, 5)
+
+    @pl.when(odd_ref[0] == 0)
+    def _():
+        save(16, own, 0, CIN, 0)
+        save(16 + CIN, middle, 0, 384, 16)
+        tiles_ref[:, 16 + CIN + 384 : 16 + 2 * CIN, :] = jnp.zeros((6, CIN - 384, 128), F32)
+
+    @pl.when(odd_ref[0] == 1)
+    def _():
+        tiles_ref[:, 16 : 16 + 256, :] = jnp.zeros((6, 256, 128), F32)
+        save(16 + 256, middle, 0, 384, 16)
+        save(16 + 640, middle, 400, 9, 16)
+        save(16 + CIN, own, 0, CIN, 0)
+
+
+def spectral_grads(odd, coeffs, grads):
     return pl.pallas_call(
         spectral_grad_kernel,
         out_shape=(jax.ShapeDtypeStruct((6, 1384, 128), F32), jax.ShapeDtypeStruct((8, DP), F32)),
-        in_specs=[vspec()] * 4,
+        in_specs=[pl.BlockSpec(memory_space=pltpu.SMEM)] + [vspec()] * 4,
         out_specs=(vspec(), vspec()),
+        cost_estimate=LIGHT,
         compiler_params=params(),
-    )(*coeffs, *grads)
+    )(odd, *coeffs, *grads)
 
 
 def flatten_kernel(length, shard_ref, tiles_ref, next_ref, out_ref, tiles, flat):
@@ -1199,6 +1293,7 @@
         in_specs=[pl.BlockSpec(memory_space=pltpu.SMEM), vspec(), vspec()],
         out_specs=vspec(),
         scratch_shapes=[pltpu.VMEM((6, 1384, 128), F32), pltpu.VMEM((5256, 128), F32)],
+        cost_estimate=LIGHT,
         compiler_params=params(),
     )(shard, tiles, after)
 
@@ -1220,42 +1315,42 @@
     mirror = [(number(d, y), number(d - d % 2 + y, d % 2)) for d, y in places]
     other_core = [(number(d, y), number(d + 1 - 2 * (d % 2), y)) for d, y in places]
     same_core = [[number(d, y) for d, y in places if d % 2 == c] for c in range(2)]
-    mirrored = lambda a: lax.ppermute(a, axes, mirror)
+    stays = core == lat_index
+
+    def mirrored(block):
+        moved = lax.ppermute(block, axes, [pair for pair in mirror if pair[0] != pair[1]])
+        return jnp.where(stays, block, moved)
+
     swapped = lambda a: lax.ppermute(a, axes, other_core)
     half = core.astype(jnp.int32).reshape(1)
     tables = {name: jnp.asarray(value) for name, value in plan_tables().items()}
 
     main, side = spectral_window(dp_index.astype(jnp.int32).reshape(1), spectral_flat)
     weights, column = gather_rows(length, main, side)
-    mlp_whole = lax.all_gather(mlp_flat, axes, axis=0, tiled=True)
+    mlp_whole = lax.all_gather(mlp_flat.reshape(-1, 128), axes, axis=0, tiled=False)
+    mlp_whole, weights = lax.optimization_barrier((mlp_whole, weights))
     state = mirrored(wide(fields))
-    noise = jnp.pad(
-        noise_fields.reshape(STEPS, CELLS, NOISE), ((0, 0), (0, 0), (1, 128 - 1 - NOISE))
-    )
-    noise = mirrored(noise)
+    noise = mirrored(noise_fields).reshape(STEPS, CELLS, NOISE)
+    noise = jnp.pad(noise, ((0, 0), (0, 0), (1, 128 - 1 - NOISE)))
     counts = mirrored(step_counts)
-    grad = mirrored(wide(cotangent))
-    w_in, w_out, vectors = mlp_weights(mlp_whole.reshape(-1, 128))
+    later, weights = lax.optimization_barrier((cotangent, weights))
+    grad = mirrored(wide(later))
+    w_in, w_out, vectors = mlp_weights(mlp_whole)
 
     kept = []
     for step in range(STEPS):
         mask = (step < counts).astype(F32)
         lon_modes = modes(state, noise[step], vectors, tables["fourier_t"])
-        coeffs, mixed = mix(half, lon_modes, swapped(lon_modes), tables["analyse"], weights, column, False)
+        parts, mixed = mix(half, lon_modes, swapped(lon_modes), tables["analyse"], weights, column, False)
         following, middle, hidden, active, slope = feed(
             half, mask, mixed, swapped(mixed), tables["synthesize"], tables["inverse_t"], state, vectors,
             w_in, w_out, step == STEPS - 1,
         )
-        kept.append((mask, state, coeffs, middle, hidden, active, slope))
+        kept.append((mask, state, parts, middle, hidden, active, slope))
         state = following
     output = mirrored(state)
 
-    owners = dp_count
-    pairs = np.array([[(3 * s) // 2, (3 * s) // 2 + 1] for s in range(owners)])
-
-    def to_owners(block):
-        parts = jnp.concatenate([block[a : b + 1] for a, b in pairs], axis=0)
-        parts = parts.reshape(owners, 2, KP, DP)
+    def to_owners(parts):
         return lax.all_to_all(
             parts, axes, split_axis=0, concat_axis=0, tiled=True, axis_index_groups=same_core
         )
@@ -1266,15 +1361,15 @@
     pres = [None] * STEPS
     feed_sums = first_sums = 0.0
     for step in reversed(range(STEPS)):
-        mask, state, coeffs, middle, hidden, active, slope = kept[step]
+        mask, state, parts, middle, hidden, active, slope = kept[step]
         results[step], pres[step], gm, grad_modes, sums = feed_back(
             mask, grad, slope, middle, vectors, w_in, w_out, tables["inverse"]
         )
         feed_sums = feed_sums + sums
-        grad_mixed, grad_coeffs = mix(
+        parts, grad_coeffs = mix(
             half, grad_modes, swapped(grad_modes), tables["synthesize_back"], weights, column, True
         )
-        grad_parts[step] = to_owners(grad_mixed)
+        grad_parts[step] = to_owners(parts)
         grad, sums = first_back(
             half, grad_coeffs, swapped(grad_coeffs), tables["analyse_back"], tables["fourier"], state, gm,
             vectors, step == 0,
@@ -1284,13 +1379,19 @@
     mlp_pack = mlp_grads(
         [k[4] for k in kept], pres, [k[5] for k in kept], results, feed_sums, first_sums
     )
-    mlp_pack = mlp_pack[: mlp_whole.shape[0] // 128].reshape(-1)
-    mlp_grad = lax.psum_scatter(mlp_pack, axes, scatter_dimension=0, tiled=True)
+    own = lax.dynamic_index_in_dim(mlp_pack, core, 0, keepdims=False)
+    give = lax.dynamic_index_in_dim(mlp_pack, 1 - core, 0, keepdims=False)
+    pair = (own.astype(F32) + swapped(give).astype(F32)).astype(BF)
+    pair = lax.all_to_all(
+        pair, axes, split_axis=0, concat_axis=0, tiled=True, axis_index_groups=same_core
+    )
+    mlp_grad = jnp.sum(pair.astype(F32), axis=0)[: mlp_flat.shape[0] // 128].reshape(-1)
 
     owner = (dp_index - core + lat_index).astype(jnp.int32).reshape(1)
-    tiles, head = spectral_grads(coeff_parts, grad_parts)
+    odd = lat_index.astype(jnp.int32).reshape(1)
+    tiles, head = spectral_grads(odd, coeff_parts, grad_parts)
     spot = lambda s, c: number(s - s % 2 + c, s % 2)
-    earlier = [(spot(s, c), spot(s - 1, c)) for s in range(1, owners) for c in range(2)]
+    earlier = [(spot(s, c), spot(s - 1, c)) for s in range(1, dp_count) for c in range(2)]
     after = lax.ppermute(head, axes, earlier)
     spectral_grad = mirrored(flatten(owner, tiles, after, length))
     narrow = lambda a: a[:, :D].reshape(1, ROWS, NLON, D)

time: 1050 us -> 778 us (0.74)
  waiting for transfers between devices: 264 us -> 67.5 us
  local copies, waits for them, and re-layouts: 97.4 us -> 28 us
  Pallas kernels: 547 us -> 500 us
  starting transfers between devices: 87.6 us -> 130 us
    unnamed x3 -> x1, waiting for transfers between devices: 97.6 us -> 0.68 us
    all_to_all x4, waiting for transfers between devices: 83.6 us -> 0.01 us  [to_owners(): lax.all_to_all(parts, axes, split_axis=0, concat_axis=0, tiled=True, axis...]
    unnamed x81 -> x38, local copies, waits for them, and re-layouts: 74 us -> 16.4 us
    pallas_call x4, Pallas kernels: 114 us -> 69.1 us  [mix(): pl.pallas_call(mix_back_kernel if back else mix_kernel, grid_spec=pltpu.P...]
    ppermute x7, starting transfers between devices: 34.6 us -> 66.5 us  [mirrored(): lax.ppermute(block, axes, [pair for pair in mirror if pair[0] != pair[1]])]
    all_to_all x4, starting transfers between devices: 29.1 us -> 53.3 us  [to_owners(): lax.all_to_all(parts, axes, split_axis=0, concat_axis=0, tiled=True, axis...]
    all_gather x1, waiting for transfers between devices: 23.3 us -> 0.01 us  [shards_paired(): lax.all_gather(mlp_flat.reshape(-1, 128), axes, axis=0, tiled=False)]
    all_gather x1 -> x0, other arithmetic: 22 us -> none  [shards_paired(): mlp_whole = lax.all_gather(mlp_flat, axes, axis=0, tiled=True)]
  transfers between devices with their start and end apart: 22 -> 23, of which waited for: 9 -> 9; matrix products, arithmetic and copies ran while one was open for 8% -> 4% of each run, Pallas kernels for 49% -> 59%
where the time goes in v2:
time: 778 us; the launch traced here: 770 us
  Pallas kernels  500 us (64%)
  starting transfers between devices  130 us (17%)
  waiting for transfers between devices  67.5 us (9%)
  other arithmetic  28.3 us (4%)
  local copies, waits for them, and re-layouts  28 us (4%)
  between operations  16.1 us (2%)
    pallas_call x1, Pallas kernels, gather_rows(): pl.pallas_call(partial(gather_kernel, length), out_shape=(jax.ShapeDtypeS...  178 us
    pallas_call x4, Pallas kernels, mix(): pl.pallas_call(mix_back_kernel if back else mix_kernel, grid_spec=pltpu.P...  69.1 us
    ppermute x7, starting transfers between devices, mirrored(): lax.ppermute(block, axes, [pair for pair in mirror if pair[0] != pair[1]])  66.5 us
    all_to_all x4, starting transfers between devices, to_owners(): lax.all_to_all(parts, axes, split_axis=0, concat_axis=0, tiled=True, axis...  53.3 us
    pallas_call x2, Pallas kernels, feed(): pl.pallas_call(feed_kernel, grid_spec=pltpu.PrefetchScalarGridSpec(num_sc...  45 us
    pallas_call x2, Pallas kernels, feed_back(): pl.pallas_call(feed_back_kernel, grid_spec=pltpu.PrefetchScalarGridSpec(n...  40 us
    ppermute x7, waiting for transfers between devices, mirrored(): lax.ppermute(block, axes, [pair for pair in mirror if pair[0] != pair[1]])  38.6 us
    pallas_call x1, Pallas kernels, mlp_grads(): pl.pallas_call(mlp_flat_kernel, out_shape=jax.ShapeDtypeStruct((2, 16, 41...  35.7 us
  transfers between devices with their start and end apart: 23, of which 9 were waited for; matrix products, arithmetic and copies ran while one was open for 4% of the time, Pallas kernels for 59%

profile of v2, /device:TPU:1, one launch (start us, length us, event | category | flops | bytes accessed | tf_op | source)
XLA Modules:
  0.0 770.2 jit_solution(1650111960096003218)
XLA Ops:
  7.2 0.7 all-gather.2.cloned.1.call-update
  7.9 3.5 pad.11
  11.4 4.5 collective-permute-start.1
  16.0 1.9 collective-permute-start.2
  17.9 10.0 %shard_map.165 = (bf16[944,640]{1,0:T(8,128)(2,1)}, bf16[64,640]{1,0:T(8,128)(2,1)}) custom-call(s32[1]{0:T(128)} %bitcast.5.shard_ref, bf16[1,624128]{1,0:T(2,128)(2,1)} %flat_ref.1), custom_call_target="tpu_custom_call" | custom-call | flops 1 | bytes 1 | tf_op jit(solution)/shard_map/pallas_call | solution.py:490
  27.9 1.3 copy-done.1
  29.2 0.9 copy-done.3
  30.1 178.5 %shard_map.166 = (bf16[15584,640]{1,0:T(8,128)(2,1)S(1)}, f32[24,768]{1,0:T(8,128)S(1)}) custom-call(bf16[944,640]{1,0:T(8,128)(2,1)S(1)} %copy-done.1, bf16[64,640]{1,0:T(8,128)(2,1)S(1)} %copy-done.3), custom_call_target="tpu_custom_call" | custom-call | flops 1 | bytes 1 | tf_op jit(solution)/shard_map/pallas_call | solution.py:769
  208.6 6.7 copy-done
  216.5 1.5 reshape.43
  218.0 1.3 fusion.2
  219.3 3.9 broadcast_select_fusion.2.state_ref
  223.2 26.1 %shard_map.167 = (bf16[768,1408]{1,0:T(8,128)(2,1)}, bf16[1408,768]{1,0:T(8,128)(2,1)}, f32[8,1408]{1,0:T(8,128)}) custom-call(bf16[32,403,128]{2,1,0:T(8,128)(2,1)} %all-gather.2.cloned.1.call-done.flat_ref), custom_call_target="tpu_custom_call" | custom-call | flops 1 | bytes 1 | tf_op jit(solution)/shard_map/pallas_call | solution.py:547
  249.2 7.1 shard_map.168.own_ref
  256.4 5.2 collective-permute-done.3.other_ref
  261.5 1.5 copy-done.9
  263.1 15.3 %shard_map.169 = (bf16[16,9,72,128]{3,2,1,0:T(8,128)(2,1)}, bf16[24,9,8,768]{3,2,1,0:T(8,128)(2,1)}) custom-call(s32[1]{0:T(128)} %bitcast.half_ref, bf16[24,9,8,768]{3,2,1,0:T(8,128)(2,1)} %shard_map.168.own_ref, bf16[24,9,8,768]{3,2,1,0:T(8,128)(2,1)} %copy-done.9, bf16[2,9,192,384]{3,2,1,0:T(8,128)(2,1)} %constant.59.clone.table_ref, ...), custom_call_target="tpu_custom_call" | custom-call | flops 1 | bytes 1 | tf_op jit(solution)/shard_map/pallas_call | solution.py:942
  278.6 11.5 %all-to-all-start = ((bf16[16,9,72,128]{3,2,1,0:T(8,128)(2,1)}), bf16[16,9,72,128]{3,2,1,0:T(8,128)(2,1)}, u32[]{:S(2)}, u32[]{:S(2)}) async-start(bf16[16,9,72,128]{3,2,1,0:T(8,128)(2,1)} %get-tuple-element.78), calls=%async_computation | async-start | bytes 5308416 | tf_op jit(solution)/shard_map/all_to_all | solution.py:1354
  290.1 4.0 collective-permute-start
  294.8 1.7 collective-permute-done
  297.2 1.5 copy-done.13
  298.7 22.5 %shard_map.170 = (f32[1728,768]{1,0:T(8,128)}, f32[1728,768]{1,0:T(8,128)}, bf16[1728,768]{1,0:T(8,128)(2,1)}, bf16[1728,1408]{1,0:T(8,128)(2,1)}, bf16[1728,1408]{1,0:T(8,128)(2,1)}) custom-call(s32[1]{0:T(128)} %bitcast.half_ref, f32[1]{0:T(128)S(6)} %convert_element_type.27.mask_ref, bf16[24,9,8,768]{3,2,1,0:T(8,128)(2,1)} %get-tuple-element.59.own_ref, ...), custom_call_target="tpu_custom_call" | custom-call | flops 1 | bytes 1 | tf_op jit(solution)/shard_map/pallas_call | solution.py:1011
  321.2 7.7 shard_map.171.own_ref
  328.9 1.8 pad.13
  330.7 2.3 collective-permute-start.8
  333.0 1.1 collective-permute-done.5.other_ref
  334.2 15.5 %shard_map.172 = (bf16[16,9,72,128]{3,2,1,0:T(8,128)(2,1)}, bf16[24,9,8,768]{3,2,1,0:T(8,128)(2,1)}) custom-call(s32[1]{0:T(128)} %bitcast.half_ref, bf16[24,9,8,768]{3,2,1,0:T(8,128)(2,1)} %shard_map.171.own_ref, bf16[24,9,8,768]{3,2,1,0:T(8,128)(2,1)} %collective-permute-done.5.other_ref, bf16[2,9,192,384]{3,2,1,0:T(8,128)(2,1)} %constant.59.clone.table_ref, ...), custom_call_target="tpu_custom_call" | custom-call | flops 1 | bytes 1 | tf_op jit(solution)/shard_map/pallas_call | solution.py:942
  349.8 8.9 %all-to-all-start.1 = ((bf16[16,9,72,128]{3,2,1,0:T(8,128)(2,1)}), bf16[16,9,72,128]{3,2,1,0:T(8,128)(2,1)}, u32[]{:S(2)}, u32[]{:S(2)}) async-start(bf16[16,9,72,128]{3,2,1,0:T(8,128)(2,1)} %get-tuple-element.79), calls=%async_computation.1 | async-start | bytes 5308416 | tf_op jit(solution)/shard_map/all_to_all | solution.py:1354
  358.7 18.2 %collective-permute-done.8 = bf16[1728,768]{1,0:T(8,128)(2,1)} collective-permute-done((bf16[1728,768]{1,0:T(8,128)(2,1)}, bf16[1728,768]{1,0:T(8,128)(2,1)}, u32[]{:S(2)}, u32[]{:S(2)}) %collective-permute-start.8) | collective-permute-done | bytes 2654240 | tf_op jit(solution)/shard_map/ppermute | solution.py:1321
  377.0 3.9 broadcast_select_fusion.1.grad_ref
  380.8 22.5 %shard_map.173 = (bf16[1728,768]{1,0:T(8,128)(2,1)}, f32[1728,768]{1,0:T(8,128)}, bf16[1728,768]{1,0:T(8,128)(2,1)}, bf16[1728,1408]{1,0:T(8,128)(2,1)}, bf16[1728,1408]{1,0:T(8,128)(2,1)}) custom-call(s32[1]{0:T(128)} %bitcast.half_ref, f32[1]{0:T(128)S(6)} %convert_element_type.26.mask_ref, bf16[24,9,8,768]{3,2,1,0:T(8,128)(2,1)} %get-tuple-element.63.own_ref, ...), custom_call_target="tpu_custom_call" | custom-call | flops 1 | bytes 1 | tf_op jit(solution)/shard_map/pallas_call | solution.py:1011
  403.4 20.1 %shard_map.174 = (bf16[1728,768]{1,0:T(8,128)(2,1)}, bf16[1728,1408]{1,0:T(8,128)(2,1)}, f32[1728,768]{1,0:T(8,128)}, bf16[24,9,8,768]{3,2,1,0:T(8,128)(2,1)}, f32[8,1408]{1,0:T(8,128)}) custom-call(f32[1]{0:T(128)S(6)} %convert_element_type.26.mask_ref, bf16[1728,768]{1,0:T(8,128)(2,1)} %broadcast_select_fusion.1.grad_ref, ...), custom_call_target="tpu_custom_call" | custom-call | flops 1 | bytes 1 | tf_op jit(solution)/shard_map/pallas_call | solution.py:1066
  423.5 5.2 collective-permute-done.9.other_ref
  428.6 1.5 copy-done.10
  430.1 19.2 %shard_map.175 = (bf16[16,11,72,128]{3,2,1,0:T(8,128)(2,1)}, bf16[24,9,8,768]{3,2,1,0:T(8,128)(2,1)}) custom-call(s32[1]{0:T(128)} %bitcast.half_ref, bf16[24,9,8,768]{3,2,1,0:T(8,128)(2,1)} %get-tuple-element.68.own_ref, bf16[24,9,8,768]{3,2,1,0:T(8,128)(2,1)} %copy-done.10, bf16[2,9,192,384]{3,2,1,0:T(8,128)(2,1)} %constant.62.clone.table_ref, ...), custom_call_target="tpu_custom_call" | custom-call | flops 1 | bytes 1 | tf_op jit(solution)/shard_map/pallas_call | solution.py:942
  449.4 15.1 %all-to-all-start.3 = ((bf16[16,11,72,128]{3,2,1,0:T(8,128)(2,1)}), bf16[16,11,72,128]{3,2,1,0:T(8,128)(2,1)S(1)}, u32[]{:S(2)}, u32[]{:S(2)}) async-start(bf16[16,11,72,128]{3,2,1,0:T(8,128)(2,1)} %get-tuple-element.81), calls=%async_computation.3 | async-start | bytes 6488064 | tf_op jit(solution)/shard_map/all_to_all | solution.py:1354
  464.9 4.9 collective-permute-done.10.other_ref
  469.9 13.0 %shard_map.176 = (f32[1728,768]{1,0:T(8,128)}, f32[8,768]{1,0:T(8,128)}) custom-call(s32[1]{0:T(128)} %bitcast.half_ref, bf16[24,9,8,768]{3,2,1,0:T(8,128)(2,1)} %get-tuple-element.69.own_ref, bf16[24,9,8,768]{3,2,1,0:T(8,128)(2,1)} %collective-permute-done.10.other_ref, bf16[2,9,192,384]{3,2,1,0:T(8,128)(2,1)} %constant.61.clone.table_ref, ...), custom_call_target="tpu_custom_call" | custom-call | flops 1 | bytes 1 | tf_op jit(solution)/shard_map/pallas_call | solution.py:1109
  482.9 19.9 %shard_map.177 = (bf16[1728,768]{1,0:T(8,128)(2,1)}, bf16[1728,1408]{1,0:T(8,128)(2,1)}, f32[1728,768]{1,0:T(8,128)}, bf16[24,9,8,768]{3,2,1,0:T(8,128)(2,1)}, f32[8,1408]{1,0:T(8,128)}) custom-call(f32[1]{0:T(128)S(6)} %convert_element_type.27.mask_ref, f32[1728,768]{1,0:T(8,128)} %get-tuple-element.71.grad_ref, ...), custom_call_target="tpu_custom_call" | custom-call | flops 1 | bytes 1 | tf_op jit(solution)/shard_map/pallas_call | solution.py:1066
  503.2 4.9 collective-permute-done.11.other_ref
  508.1 19.1 %shard_map.178 = (bf16[16,11,72,128]{3,2,1,0:T(8,128)(2,1)}, bf16[24,9,8,768]{3,2,1,0:T(8,128)(2,1)}) custom-call(s32[1]{0:T(128)} %bitcast.half_ref, bf16[24,9,8,768]{3,2,1,0:T(8,128)(2,1)} %get-tuple-element.74.own_ref, bf16[24,9,8,768]{3,2,1,0:T(8,128)(2,1)} %collective-permute-done.11.other_ref, bf16[2,9,192,384]{3,2,1,0:T(8,128)(2,1)} %constant.62.clone.table_ref, ...), custom_call_target="tpu_custom_call" | custom-call | flops 1 | bytes 1 | tf_op jit(solution)/shard_map/pallas_call | solution.py:942
  527.2 1.7 copy-done.5
  529.0 17.9 %all-to-all-start.2 = ((bf16[16,11,72,128]{3,2,1,0:T(8,128)(2,1)}), bf16[16,11,72,128]{3,2,1,0:T(8,128)(2,1)}, u32[]{:S(2)}, u32[]{:S(2)}) async-start(bf16[16,11,72,128]{3,2,1,0:T(8,128)(2,1)} %get-tuple-element.80), calls=%async_computation.2 | async-start | bytes 6488064 | tf_op jit(solution)/shard_map/all_to_all | solution.py:1354
  546.8 2.1 collective-permute-start.12
  549.0 31.5 %shard_map.182 = (f32[11,768,128]{2,1,0:T(8,128)}, f32[6,1408,128]{2,1,0:T(8,128)}) custom-call(bf16[1728,768]{1,0:T(8,128)(2,1)} %get-tuple-element.84.h0, bf16[1728,768]{1,0:T(8,128)(2,1)} %get-tuple-element.85.h1, bf16[1728,1408]{1,0:T(8,128)(2,1)} %get-tuple-element.86.p0, bf16[1728,1408]{1,0:T(8,128)(2,1)} %get-tuple-element.87.p1, ...), custom_call_target="tpu_custom_call" | custom-call | flops 1 | bytes 1 | tf_op jit(solution)/shard_map/pallas_call | solution.py:1184
  581.1 12.3 %shard_map.179 = (bf16[1728,768]{1,0:T(8,128)(2,1)}, f32[8,768]{1,0:T(8,128)}) custom-call(s32[1]{0:T(128)} %bitcast.half_ref, bf16[24,9,8,768]{3,2,1,0:T(8,128)(2,1)} %get-tuple-element.75.own_ref, bf16[24,9,8,768]{3,2,1,0:T(8,128)(2,1)} %collective-permute-done.12.other_ref, bf16[2,9,192,384]{3,2,1,0:T(8,128)(2,1)} %constant.61.clone.table_ref, ...), custom_call_target="tpu_custom_call" | custom-call | flops 1 | bytes 1 | tf_op jit(solution)/shard_map/pallas_call | solution.py:1109
  593.4 1.3 add.33.first_sums
  594.8 35.7 %shard_map.183 = bf16[2,16,416,128]{3,2,1,0:T(8,128)(2,1)} custom-call(f32[11,768,128]{2,1,0:T(8,128)} %get-tuple-element.92.gin, f32[6,1408,128]{2,1,0:T(8,128)} %get-tuple-element.93.gout, f32[8,1408]{1,0:T(8,128)} %add.32.feed_sums, f32[8,768]{1,0:T(8,128)} %add.33.first_sums), custom_call_target="tpu_custom_call" | custom-call | flops 1 | bytes 1 | tf_op jit(solution)/shard_map/pallas_call | solution.py:1193
  630.5 2.9 dynamic-slice_bitcast_fusion
  633.4 3.8 collective-permute-start.7
  637.2 1.9 collective-permute-start.13
  639.2 3.1 fusion
  642.3 5.8 all-to-all-start.4
  648.1 12.1 %shard_map.180 = (f32[6,1384,128]{2,1,0:T(8,128)}, f32[8,768]{1,0:T(8,128)}) custom-call(s32[1]{0:T(128)} %bitcast.11.odd_ref, bf16[16,9,72,128]{3,2,1,0:T(8,128)(2,1)} %all-to-all-done.c0, bf16[16,9,72,128]{3,2,1,0:T(8,128)(2,1)} %all-to-all-done.1.c1, bf16[16,11,72,128]{3,2,1,0:T(8,128)(2,1)} %all-to-all-done.2.g0, bf16[16,11,72,128]{3,2,1,0:T(8,128)(2,1)} %copy-done.5), custom_call_target="tpu_custom_call" | custom-call | flops 1 | bytes 1 | tf_op jit(solution)/shard_map/pallas_call | solution.py:1252
  660.2 1.3 collective-permute-start.14
  661.5 6.9 collective-permute-done.14.next_ref
  669.1 11.8 %shard_map.181 = f32[1,624128]{1,0:T(1,128)} custom-call(s32[1]{0:T(128)} %bitcast.10.shard_ref, f32[6,1384,128]{2,1,0:T(8,128)} %get-tuple-element.82.tiles_ref, f32[8,768]{1,0:T(8,128)} %copy-done.17), custom_call_target="tpu_custom_call" | custom-call | flops 1 | bytes 1 | tf_op jit(solution)/shard_map/pallas_call | solution.py:1290
  680.8 47.9 %collective-permute-start.15 = (f32[1,624128]{1,0:T(1,128)}, f32[1,624128]{1,0:T(1,128)}, u32[]{:S(2)}, u32[]{:S(2)}) collective-permute-start(f32[1,624128]{1,0:T(1,128)} %shard_map.181), channel_id=1, source_target_pairs={{1,2},{2,1},{5,6},{6,5},{9,10},{10,9},{13,14},{14,13},{17,18},{18,... | collective-permute-start | bytes 7489544 | tf_op jit(solution)/shard_map/ppermute | solution.py:1321
  728.8 3.5 slice_select_fusion.1
  732.3 3.8 slice_select_fusion
  736.0 1.7 convert_reduce_fusion
  737.8 0.7 slice_bitcast_fusion
  738.4 18.6 %collective-permute-done.15 = f32[1,624128]{1,0:T(1,128)} collective-permute-done((f32[1,624128]{1,0:T(1,128)}, f32[1,624128]{1,0:T(1,128)}, u32[]{:S(2)}, u32[]{:S(2)}) %collective-permute-start.15) | collective-permute-done | bytes 2496544 | tf_op jit(solution)/shard_map/ppermute | solution.py:1321
  757.0 5.9 broadcast_select_fusion
  (56 shorter events, 4.0 us)
Async XLA Ops:
  7.2 216.0 %all-gather.2.cloned.1.call-start = ((), (), s32[]{:S(2)}) async-start(), calls=%async_computation.5 | async-start | bytes 3446784 | tf_op jit(solution)/shard_map/all_gather | solution.py:1330
  7.9 8.1 %copy-start.14 = (bf16[1,2,24,576]{3,2,1,0:T(8,128)(2,1)S(1)}, bf16[1,2,24,576]{3,2,1,0:T(8,128)(2,1)}, u32[]{:S(2)}) copy-start(bf16[1,2,24,576]{3,2,1,0:T(8,128)(2,1)} %param.15) | copy-start | bytes 165892
  11.4 207.8 %collective-permute-start.1 = (bf16[1728,768]{1,0:T(8,128)(2,1)}, bf16[1728,768]{1,0:T(8,128)(2,1)}, u32[]{:S(2)}, u32[]{:S(2)}) collective-permute-start(bf16[1728,768]{1,0:T(8,128)(2,1)} %pad.11), channel_id=1, source_target_pairs={{1,2},{2,1},{5,6},{6,5},{9,10},{10,9},{13,14},{14,13},{17,18},{18,... | collective-permute-start | bytes 7962632 | tf_op jit(solution)/shard_map/ppermute | solution.py:1321
  16.0 199.9 %collective-permute-start.2 = (bf16[1,2,24,576]{3,2,1,0:T(8,128)(2,1)S(1)}, bf16[1,2,24,576]{3,2,1,0:T(8,128)(2,1)S(1)}, u32[]{:S(2)}, u32[]{:S(2)}) collective-permute-start(bf16[1,2,24,576]{3,2,1,0:T(8,128)(2,1)S(1)} %copy-done.14), channel_id=1, source_target_pairs={{1,2},{2,1},{5,6},{6,5},{9,10},{10,9},{13,14},{14,13},{17,18},{18,... | collective-permute-start | bytes 165896 | tf_op jit(solution)/shard_map/ppermute | solution.py:1321
  27.9 1.3 copy-start.1
  29.2 0.9 copy-start.3
  30.1 189.2 %copy-start.6 = (bf16[1,24,72,641]{3,2,1,0:T(8,128)(2,1)S(1)}, bf16[1,24,72,641]{3,2,1,0:T(8,128)(2,1)}, u32[]{:S(2)}) copy-start(bf16[1,24,72,641]{3,2,1,0:T(8,128)(2,1)} %param.14) | copy-start | bytes 6645892
  208.6 6.7 copy-start
  215.3 0.6 copy-start.2
  256.4 5.2 collective-permute-start.3
  261.5 1.5 copy-start.9
  278.4 18.7 %collective-permute-start.4 = (bf16[24,9,8,768]{3,2,1,0:T(8,128)(2,1)}, bf16[24,9,8,768]{3,2,1,0:T(8,128)(2,1)S(1)}, u32[]{:S(2)}, u32[]{:S(2)}) collective-permute-start(bf16[24,9,8,768]{3,2,1,0:T(8,128)(2,1)} %get-tuple-element.59.own_ref), channel_id=1, source_target_pairs={{0,2},{1,3},{2,0},{3,1},{4,6},{5,7},{6,4},{7,5},{8,10},{9,11},{10,... | collective-permute-start | bytes 7962632 | tf_op jit(solution)/shard_map/ppermute | solution.py:1324
  278.6 71.2 %all-to-all-start = ((bf16[16,9,72,128]{3,2,1,0:T(8,128)(2,1)}), bf16[16,9,72,128]{3,2,1,0:T(8,128)(2,1)}, u32[]{:S(2)}, u32[]{:S(2)}) async-start(bf16[16,9,72,128]{3,2,1,0:T(8,128)(2,1)} %get-tuple-element.78), calls=%async_computation | async-start | bytes 5308416 | tf_op jit(solution)/shard_map/all_to_all | solution.py:1354
  290.1 6.4 collective-permute-start
  297.2 1.5 copy-start.13
  321.2 7.7 %copy-start.7 = (bf16[1,24,72,641]{3,2,1,0:T(8,128)(2,1)S(1)}, bf16[1,24,72,641]{3,2,1,0:T(8,128)(2,1)}, u32[]{:S(2)}) copy-start(bf16[1,24,72,641]{3,2,1,0:T(8,128)(2,1)} %param.19) | copy-start | bytes 6645892
  328.9 5.3 collective-permute-start.5
  330.7 46.3 %collective-permute-start.8 = (bf16[1728,768]{1,0:T(8,128)(2,1)}, bf16[1728,768]{1,0:T(8,128)(2,1)}, u32[]{:S(2)}, u32[]{:S(2)}) collective-permute-start(bf16[1728,768]{1,0:T(8,128)(2,1)} %pad.13), channel_id=1, source_target_pairs={{1,2},{2,1},{5,6},{6,5},{9,10},{10,9},{13,14},{14,13},{17,18},{18,... | collective-permute-start | bytes 7962632 | tf_op jit(solution)/shard_map/ppermute | solution.py:1321
  349.6 31.2 %collective-permute-start.6 = (bf16[24,9,8,768]{3,2,1,0:T(8,128)(2,1)}, bf16[24,9,8,768]{3,2,1,0:T(8,128)(2,1)}, u32[]{:S(2)}, u32[]{:S(2)}) collective-permute-start(bf16[24,9,8,768]{3,2,1,0:T(8,128)(2,1)} %get-tuple-element.63.own_ref), channel_id=1, source_target_pairs={{0,2},{1,3},{2,0},{3,1},{4,6},{5,7},{6,4},{7,5},{8,10},{9,11},{10,... | collective-permute-start | bytes 7962632 | tf_op jit(solution)/shard_map/ppermute | solution.py:1324
  349.8 99.5 %all-to-all-start.1 = ((bf16[16,9,72,128]{3,2,1,0:T(8,128)(2,1)}), bf16[16,9,72,128]{3,2,1,0:T(8,128)(2,1)}, u32[]{:S(2)}, u32[]{:S(2)}) async-start(bf16[16,9,72,128]{3,2,1,0:T(8,128)(2,1)} %get-tuple-element.79), calls=%async_computation.1 | async-start | bytes 5308416 | tf_op jit(solution)/shard_map/all_to_all | solution.py:1354
  423.5 5.2 collective-permute-start.9
  428.6 1.5 copy-start.10
  449.4 77.8 %all-to-all-start.3 = ((bf16[16,11,72,128]{3,2,1,0:T(8,128)(2,1)}), bf16[16,11,72,128]{3,2,1,0:T(8,128)(2,1)S(1)}, u32[]{:S(2)}, u32[]{:S(2)}) async-start(bf16[16,11,72,128]{3,2,1,0:T(8,128)(2,1)} %get-tuple-element.81), calls=%async_computation.3 | async-start | bytes 6488064 | tf_op jit(solution)/shard_map/all_to_all | solution.py:1354
  464.5 5.4 collective-permute-start.10
  502.8 5.3 collective-permute-start.11
  527.2 1.8 copy-start.5
  529.0 113.4 %all-to-all-start.2 = ((bf16[16,11,72,128]{3,2,1,0:T(8,128)(2,1)}), bf16[16,11,72,128]{3,2,1,0:T(8,128)(2,1)}, u32[]{:S(2)}, u32[]{:S(2)}) async-start(bf16[16,11,72,128]{3,2,1,0:T(8,128)(2,1)} %get-tuple-element.80), calls=%async_computation.2 | async-start | bytes 6488064 | tf_op jit(solution)/shard_map/all_to_all | solution.py:1354
  546.8 34.3 %collective-permute-start.12 = (bf16[24,9,8,768]{3,2,1,0:T(8,128)(2,1)}, bf16[24,9,8,768]{3,2,1,0:T(8,128)(2,1)}, u32[]{:S(2)}, u32[]{:S(2)}) collective-permute-start(bf16[24,9,8,768]{3,2,1,0:T(8,128)(2,1)} %get-tuple-element.75.own_ref), channel_id=1, source_target_pairs={{0,2},{1,3},{2,0},{3,1},{4,6},{5,7},{6,4},{7,5},{8,10},{9,11},{10,... | collective-permute-start | bytes 7962632 | tf_op jit(solution)/shard_map/ppermute | solution.py:1324
  549.0 31.5 %copy-start.15 = (f32[8,1408]{1,0:T(8,128)S(1)}, f32[8,1408]{1,0:T(8,128)}, u32[]{:S(2)}) copy-start(f32[8,1408]{1,0:T(8,128)} %get-tuple-element.94) | copy-start | bytes 135172
  549.0 31.5 %copy-start.16 = (f32[8,1408]{1,0:T(8,128)S(1)}, f32[8,1408]{1,0:T(8,128)}, u32[]{:S(2)}) copy-start(f32[8,1408]{1,0:T(8,128)} %get-tuple-element.95) | copy-start | bytes 135172
  581.1 12.3 %copy-start.18 = (f32[8,768]{1,0:T(8,128)S(1)}, f32[8,768]{1,0:T(8,128)}, u32[]{:S(2)}) copy-start(f32[8,768]{1,0:T(8,128)} %get-tuple-element.96) | copy-start | bytes 73732
  630.5 8.7 %copy-start.4 = (bf16[2,16,416,128]{3,2,1,0:T(8,128)(2,1)S(1)}, bf16[2,16,416,128]{3,2,1,0:T(8,128)(2,1)}, u32[]{:S(2)}) copy-start(bf16[2,16,416,128]{3,2,1,0:T(8,128)(2,1)} %shard_map.183) | copy-start | bytes 10223620
  633.4 5.8 collective-permute-start.16
  633.4 95.3 %collective-permute-start.7 = (bf16[1728,768]{1,0:T(8,128)(2,1)}, bf16[1728,768]{1,0:T(8,128)(2,1)}, u32[]{:S(2)}, u32[]{:S(2)}) collective-permute-start(bf16[1728,768]{1,0:T(8,128)(2,1)} %get-tuple-element.64), channel_id=1, source_target_pairs={{1,2},{2,1},{5,6},{6,5},{9,10},{10,9},{13,14},{14,13},{17,18},{18,... | collective-permute-start | bytes 7962632 | tf_op jit(solution)/shard_map/ppermute | solution.py:1321
  637.2 95.0 %collective-permute-start.13 = (bf16[1728,768]{1,0:T(8,128)(2,1)}, bf16[1728,768]{1,0:T(8,128)(2,1)}, u32[]{:S(2)}, u32[]{:S(2)}) collective-permute-start(bf16[1728,768]{1,0:T(8,128)(2,1)} %get-tuple-element.77), channel_id=1, source_target_pairs={{1,2},{2,1},{5,6},{6,5},{9,10},{10,9},{13,14},{14,13},{17,18},{18,... | collective-permute-start | bytes 7962632 | tf_op jit(solution)/shard_map/ppermute | solution.py:1321
  642.3 93.7 %all-to-all-start.4 = ((bf16[16,416,128]{2,1,0:T(8,128)(2,1)}), bf16[16,416,128]{2,1,0:T(8,128)(2,1)}, u32[]{:S(2)}, u32[]{:S(2)}) async-start(bf16[16,416,128]{2,1,0:T(8,128)(2,1)} %fusion), calls=%async_computation.4 | async-start | bytes 3407872 | tf_op jit(solution)/shard_map/all_to_all | solution.py:1385
  660.2 8.2 %collective-permute-start.14 = (f32[8,768]{1,0:T(8,128)}, f32[8,768]{1,0:T(8,128)S(1)}, u32[]{:S(2)}, u32[]{:S(2)}) collective-permute-start(f32[8,768]{1,0:T(8,128)} %get-tuple-element.83), channel_id=1, source_target_pairs={{1,0},{3,2},{4,1},{6,3},{5,4},{7,6},{8,5},{10,7},{9,8},{11,10},{12... | collective-permute-start | bytes 73736 | tf_op jit(solution)/shard_map/ppermute | solution.py:1395
  668.5 0.6 copy-start.17
  669.1 59.7 %copy-start.11 = (bf16[1728,768]{1,0:T(8,128)(2,1)S(1)}, bf16[1728,768]{1,0:T(8,128)(2,1)}, u32[]{:S(2)}) copy-start(bf16[1728,768]{1,0:T(8,128)(2,1)} %get-tuple-element.64) | copy-start | bytes 7962628
  680.8 51.5 %copy-start.12 = (bf16[1728,768]{1,0:T(8,128)(2,1)S(1)}, bf16[1728,768]{1,0:T(8,128)(2,1)}, u32[]{:S(2)}) copy-start(bf16[1728,768]{1,0:T(8,128)(2,1)} %get-tuple-element.77) | copy-start | bytes 7962628
  680.8 76.2 %collective-permute-start.15 = (f32[1,624128]{1,0:T(1,128)}, f32[1,624128]{1,0:T(1,128)}, u32[]{:S(2)}, u32[]{:S(2)}) collective-permute-start(f32[1,624128]{1,0:T(1,128)} %shard_map.181), channel_id=1, source_target_pairs={{1,2},{2,1},{5,6},{6,5},{9,10},{10,9},{13,14},{14,13},{17,18},{18,... | collective-permute-start | bytes 7489544 | tf_op jit(solution)/shard_map/ppermute | solution.py:1321
  732.3 24.7 %copy-start.8 = (f32[1,624128]{1,0:T(1,128)S(1)}, f32[1,624128]{1,0:T(1,128)}, u32[]{:S(2)}) copy-start(f32[1,624128]{1,0:T(1,128)} %shard_map.181) | copy-start | bytes 7489540
Sparse Core Ops, SparseCore 0:
  10.9 68.5 all-gather.1

commit v3 on v2

--- a/solution.py
+++ b/solution.py
@@ -314,7 +314,8 @@
 BC = BLK * NLON
 WIN = 992
 MAIN = 944
-HEAD = 416
+TROWS = 1392
+HEAD = 352
 BF = jnp.bfloat16
 F32 = jnp.float32
 MB = 2**20
@@ -832,13 +833,56 @@
     )(state, noise, vectors, table)
 
 
-def legendre(table_ref, own_ref, other_ref, out_ref):
+class Swap:
+    def __init__(self, own_ref, other, table_ref, table, send, recv, sem):
+        dp = lax.axis_index("dp")
+        core = dp % 2
+        self.partner = (dp + 1 - 2 * core, lax.axis_index("lat"))
+        self.table = pltpu.make_async_copy(table_ref.at[core], table, sem)
+        self.copies = [
+            pltpu.make_async_remote_copy(
+                src_ref=own_ref.at[:, group], dst_ref=other.at[:, group], send_sem=send.at[group],
+                recv_sem=recv.at[group], device_id=self.partner, device_id_type=pl.DeviceIdType.MESH,
+            )
+            for group in range(GROUPS)
+        ]
+
+    def start(self):
+        self.table.start()
+        barrier = pltpu.get_barrier_semaphore()
+        pl.semaphore_signal(barrier, inc=1, device_id=self.partner, device_id_type=pl.DeviceIdType.MESH)
+        pl.semaphore_wait(barrier, 1)
+        for copy in self.copies:
+            copy.start()
+
+    def finish(self):
+        for copy in self.copies:
+            copy.wait_send()
+
+
+def swap_scratch():
+    return [
+        pltpu.VMEM((24, GROUPS, GK, DP), BF),
+        pltpu.VMEM((GROUPS, 192, 384), BF),
+        pltpu.SemaphoreType.DMA((GROUPS,)),
+        pltpu.SemaphoreType.DMA((GROUPS,)),
+        pltpu.SemaphoreType.DMA,
+    ]
+
+
+def legendre(own_ref, table_ref, out_ref, swap_refs):
+    other, table, send, recv, sem = swap_refs
+    swap = Swap(own_ref, other, table_ref, table, send, recv, sem)
+    swap.start()
+    swap.table.wait()
     for group in range(GROUPS):
+        swap.copies[group].wait_recv()
         both = jnp.concatenate(
-            [own_ref[:, group].reshape(192, DP), other_ref[:, group].reshape(192, DP)], axis=0
+            [own_ref[:, group].reshape(192, DP), other[:, group].reshape(192, DP)], axis=0
         )
-        total = dot(table_ref[0, group], both)
+        total = dot(table[group], both)
         out_ref[:, group] = total.astype(out_ref.dtype).reshape(24, GK, DP)
+    swap.finish()
 
 
 def fetch(w_ref, w_buf, sem, degree):
@@ -884,12 +928,10 @@
         parts_ref[owner, last] = jnp.where(lane < 16, one, two).astype(BF)
 
 
-def mix_kernel(
-    half_ref, own_ref, other_ref, table_ref, column_ref, w_ref, parts_ref, mixed_ref, coeff_ref, w_buf, sem,
-):
+def mix_kernel(own_ref, table_ref, column_ref, w_ref, parts_ref, mixed_ref, coeff_ref, w_buf, sem, *swap_refs):
     for degree in range(DEPTH):
         fetch(w_ref, w_buf, sem, degree).start()
-    legendre(table_ref, own_ref, other_ref, coeff_ref)
+    legendre(own_ref, table_ref, coeff_ref, swap_refs)
     pack_tiles(coeff_ref, parts_ref, ((0, 1, 2), (2, 3, 4)))
     lane = lax.broadcasted_iota(jnp.int32, (KP, 128), 1)
 
@@ -908,11 +950,11 @@
 
 
 def mix_back_kernel(
-    half_ref, own_ref, other_ref, table_ref, column_ref, w_ref, parts_ref, out_ref, grad_ref, w_buf, wide, sem,
+    own_ref, table_ref, column_ref, w_ref, parts_ref, out_ref, grad_ref, w_buf, wide, sem, *swap_refs
 ):
     for degree in range(DEPTH):
         fetch(w_ref, w_buf, sem, degree).start()
-    legendre(table_ref, own_ref, other_ref, grad_ref)
+    legendre(own_ref, table_ref, grad_ref, swap_refs)
     every = (0, 1, 2, 3, 4)
     pack_tiles(grad_ref, parts_ref, (every, every))
     keep = lax.broadcasted_iota(jnp.int32, (KP, DP), 1) < CIN
@@ -932,8 +974,11 @@
     lax.fori_loop(0, DEGS, one, 0)
 
 
-def mix(half, own, other, table, weights, column, back):
-    whole = fixed(24, GROUPS, GK, DP)
+def anywhere():
+    return pl.BlockSpec(memory_space=pl.ANY)
+
+
+def mix(own, table, weights, column, back):
     tiles = G_TILES if back else C_TILES
     scratch = [pltpu.VMEM((24, GROUPS, GK, DP), BF), pltpu.VMEM((DEPTH, WROWS, 640), BF)]
     if back:
@@ -941,42 +986,32 @@
     scratch.append(pltpu.SemaphoreType.DMA((DEPTH,)))
     return pl.pallas_call(
         mix_back_kernel if back else mix_kernel,
-        grid_spec=pltpu.PrefetchScalarGridSpec(
-            num_scalar_prefetch=1,
-            grid=(1,),
-            in_specs=[
-                whole,
-                whole,
-                table_spec(),
-                fixed(DEGS, DP),
-                pl.BlockSpec(memory_space=pl.ANY),
-            ],
-            out_specs=(fixed(OWNERS, tiles, KP, 128), whole),
-            scratch_shapes=scratch,
-        ),
+        in_specs=[vspec(), anywhere(), vspec(), anywhere()],
+        out_specs=(vspec(), vspec()),
+        scratch_shapes=scratch + swap_scratch(),
         out_shape=(
             jax.ShapeDtypeStruct((OWNERS, tiles, KP, 128), BF),
             jax.ShapeDtypeStruct((24, GROUPS, GK, DP), BF),
         ),
         cost_estimate=LIGHT,
-        compiler_params=params(),
-    )(half, own, other, table, column, weights)
+        compiler_params=params(collective_id=2 if back else 1, has_side_effects=True),
+    )(own, table, column, weights)
 
 
 HID_PARTS = ((0, 256), (256, 256), (512, 256), (768, 256), (1024, 256), (1280, 128))
 
 
 def feed_kernel(
-    half_ref, mask_ref, own_ref, other_ref, table_ref, inverse_ref, state_ref, vec_ref, in_ref, out_ref,
-    next_ref, middle_ref, hidden_ref, active_ref, slope_ref, lat,
+    mask_ref, own_ref, table_ref, inverse_ref, state_ref, vec_ref, in_ref, out_ref,
+    next_ref, middle_ref, hidden_ref, active_ref, slope_ref, lat, *swap_refs
 ):
     i = pl.program_id(0)
 
     @pl.when(i == 0)
     def _():
-        legendre(table_ref, own_ref, other_ref, lat)
-
-    mask = mask_ref[0]
+        legendre(own_ref, table_ref, lat, swap_refs)
+
+    mask = mask_ref[0:1, 0:1]
     parts = [split_dot(inverse_ref[...], lat[BLK * i + j].reshape(KP, DP)) for j in range(BLK)]
     middle = state_ref[...].astype(F32) + mask * jnp.concatenate(parts, axis=0)
     middle_ref[...] = middle
@@ -1002,30 +1037,23 @@
     return pl.BlockSpec(shape, lambda i, *h: (0,) * len(shape))
 
 
-def table_spec():
-    return pl.BlockSpec((1, GROUPS, 192, 384), lambda i, h, *m: (h[0], 0, 0, 0))
-
-
-def feed(half, mask, own, other, table, inverse_t, state, vectors, w_in, w_out, last):
+def feed(mask, own, table, inverse_t, state, vectors, w_in, w_out, last):
     cells = lambda width, kind: jax.ShapeDtypeStruct((CELLS, width), kind)
     return pl.pallas_call(
         feed_kernel,
-        grid_spec=pltpu.PrefetchScalarGridSpec(
-            num_scalar_prefetch=2,
-            grid=(ROWS // BLK,),
-            in_specs=[
-                fixed(24, GROUPS, GK, DP), fixed(24, GROUPS, GK, DP), table_spec(), fixed(NLON, 3 * KP), cell_spec(DP),
-                fixed(8, HP), fixed(DP, HP), fixed(HP, DP),
-            ],
-            out_specs=(cell_spec(DP), cell_spec(DP), cell_spec(DP), cell_spec(HP), cell_spec(HP)),
-            scratch_shapes=[pltpu.VMEM((24, GROUPS, GK, DP), F32)],
-        ),
+        grid=(ROWS // BLK,),
+        in_specs=[
+            fixed(1, 128), fixed(24, GROUPS, GK, DP), anywhere(), fixed(NLON, 3 * KP), cell_spec(DP),
+            fixed(8, HP), fixed(DP, HP), fixed(HP, DP),
+        ],
+        out_specs=(cell_spec(DP), cell_spec(DP), cell_spec(DP), cell_spec(HP), cell_spec(HP)),
+        scratch_shapes=[pltpu.VMEM((24, GROUPS, GK, DP), F32)] + swap_scratch(),
         out_shape=(
             cells(DP, BF if last else F32), cells(DP, F32), cells(DP, BF), cells(HP, BF), cells(HP, BF),
         ),
         cost_estimate=LIGHT,
-        compiler_params=params(),
-    )(half, mask, own, other, table, inverse_t, state, vectors, w_in, w_out)
+        compiler_params=params(collective_id=4 if last else 3, has_side_effects=True),
+    )(mask, own, table, inverse_t, state, vectors, w_in, w_out)
 
 
 def feed_back_kernel(
@@ -1038,7 +1066,7 @@
     def _():
         sums_ref[...] = jnp.zeros_like(sums_ref)
 
-    mask = mask_ref[0]
+    mask = mask_ref[0:1, 0:1]
     grad = grad_ref[...].astype(F32)
     result = (mask * grad).astype(BF)
     result_ref[...] = result
@@ -1065,17 +1093,14 @@
     cells = lambda width, kind: jax.ShapeDtypeStruct((CELLS, width), kind)
     return pl.pallas_call(
         feed_back_kernel,
-        grid_spec=pltpu.PrefetchScalarGridSpec(
-            num_scalar_prefetch=1,
-            grid=(ROWS // BLK,),
-            in_specs=[
-                cell_spec(DP), cell_spec(HP), cell_spec(DP), fixed(8, HP), fixed(DP, HP), fixed(HP, DP),
-                fixed(KP, 3 * NLON),
-            ],
-            out_specs=(
-                cell_spec(DP), cell_spec(HP), cell_spec(DP),
-                pl.BlockSpec((BLK, GROUPS, GK, DP), lambda i, *h: (i, 0, 0, 0)), fixed(8, HP),
-            ),
+        grid=(ROWS // BLK,),
+        in_specs=[
+            fixed(1, 128), cell_spec(DP), cell_spec(HP), cell_spec(DP), fixed(8, HP), fixed(DP, HP),
+            fixed(HP, DP), fixed(KP, 3 * NLON),
+        ],
+        out_specs=(
+            cell_spec(DP), cell_spec(HP), cell_spec(DP),
+            pl.BlockSpec((BLK, GROUPS, GK, DP), lambda i: (i, 0, 0, 0)), fixed(8, HP),
         ),
         out_shape=(
             cells(DP, BF), cells(HP, BF), cells(DP, F32), jax.ShapeDtypeStruct((ROWS, GROUPS, GK, DP), BF),
@@ -1087,13 +1112,13 @@
 
 
 def first_back_kernel(
-    half_ref, own_ref, other_ref, table_ref, fourier_ref, state_ref, gm_ref, vec_ref, out_ref, sums_ref, lat,
+    own_ref, table_ref, fourier_ref, state_ref, gm_ref, vec_ref, out_ref, sums_ref, lat, *swap_refs
 ):
     i = pl.program_id(0)
 
     @pl.when(i == 0)
     def _():
-        legendre(table_ref, own_ref, other_ref, lat)
+        legendre(own_ref, table_ref, lat, swap_refs)
         sums_ref[...] = jnp.zeros_like(sums_ref)
 
     parts = [split_dot(fourier_ref[...], lat[BLK * i + j].reshape(KP, DP)) for j in range(BLK)]
@@ -1105,25 +1130,22 @@
     out_ref[...] = total.astype(out_ref.dtype)
 
 
-def first_back(half, own, other, table, fourier, state, gm, vectors, last):
+def first_back(own, table, fourier, state, gm, vectors, last):
     return pl.pallas_call(
         first_back_kernel,
-        grid_spec=pltpu.PrefetchScalarGridSpec(
-            num_scalar_prefetch=1,
-            grid=(ROWS // BLK,),
-            in_specs=[
-                fixed(24, GROUPS, GK, DP), fixed(24, GROUPS, GK, DP), table_spec(), fixed(NLON, 3 * KP), cell_spec(DP),
-                cell_spec(DP), fixed(8, HP),
-            ],
-            out_specs=(cell_spec(DP), fixed(8, DP)),
-            scratch_shapes=[pltpu.VMEM((24, GROUPS, GK, DP), F32)],
-        ),
+        grid=(ROWS // BLK,),
+        in_specs=[
+            fixed(24, GROUPS, GK, DP), anywhere(), fixed(NLON, 3 * KP), cell_spec(DP), cell_spec(DP),
+            fixed(8, HP),
+        ],
+        out_specs=(cell_spec(DP), fixed(8, DP)),
+        scratch_shapes=[pltpu.VMEM((24, GROUPS, GK, DP), F32)] + swap_scratch(),
         out_shape=(
             jax.ShapeDtypeStruct((CELLS, DP), BF if last else F32), jax.ShapeDtypeStruct((8, DP), F32),
         ),
         cost_estimate=LIGHT,
-        compiler_params=params(),
-    )(half, own, other, table, fourier, state, gm, vectors)
+        compiler_params=params(collective_id=6 if last else 5, has_side_effects=True),
+    )(own, table, fourier, state, gm, vectors)
 
 
 def mlp_grad_kernel(h0, h1, p0, p1, a0, a1, r0, r1, tin, tout, turned):
@@ -1205,11 +1227,11 @@
     )(gin, gout, feed_sums, first_sums)
 
 
-def spectral_grad_kernel(odd_ref, c0, c1, g0, g1, tiles_ref, head_ref):
+def spectral_grad_kernel(odd_ref, c0, c1, g0, g1, out_ref, head_ref, tiles_ref):
     rows = OWNERS * KP
     lane = lax.broadcasted_iota(jnp.int32, (DP, 128), 1)
     tiles_ref[:, 0:16, :] = jnp.zeros((6, 16, 128), F32)
-    tiles_ref[:, 16 + 2 * CIN :, :] = jnp.zeros((6, 1384 - 16 - 2 * CIN, 128), F32)
+    tiles_ref[:, 16 + 2 * CIN :, :] = jnp.zeros((6, TROWS - 16 - 2 * CIN, 128), F32)
 
     def side(ref, first, count):
         take = [ref[:, m].reshape(rows, 128) for m in list(range(first, first + count)) + [ref.shape[1] - 1]]
@@ -1229,9 +1251,8 @@
             tiles_ref[m, start : start + count, :] = piece
 
     own = product(0, 5, 0)
-    head_ref[...] = jnp.concatenate(
-        [own[0:8, :640], jnp.where(lane[:8] < 1, own[0:8, 640:], 0.0)], axis=1
-    )
+    head = jnp.concatenate([own[0:16, :640], jnp.where(lane[:16] < 1, own[0:16, 640:], 0.0)], axis=1)
+    head_ref[...] = head.astype(BF)
     middle = product(5, 3, 5)
 
     @pl.when(odd_ref[0] == 0)
@@ -1247,26 +1268,38 @@
         save(16 + 640, middle, 400, 9, 16)
         save(16 + CIN, own, 0, CIN, 0)
 
+    out_ref[...] = tiles_ref[...].astype(BF)
+
 
 def spectral_grads(odd, coeffs, grads):
     return pl.pallas_call(
         spectral_grad_kernel,
-        out_shape=(jax.ShapeDtypeStruct((6, 1384, 128), F32), jax.ShapeDtypeStruct((8, DP), F32)),
+        out_shape=(jax.ShapeDtypeStruct((6, TROWS, 128), BF), jax.ShapeDtypeStruct((16, DP), BF)),
         in_specs=[pl.BlockSpec(memory_space=pltpu.SMEM)] + [vspec()] * 4,
         out_specs=(vspec(), vspec()),
+        scratch_shapes=[pltpu.VMEM((6, TROWS, 128), F32)],
         cost_estimate=LIGHT,
         compiler_params=params(),
     )(odd, *coeffs, *grads)
 
 
-def flatten_kernel(length, shard_ref, tiles_ref, next_ref, out_ref, tiles, flat):
+def flatten_kernel(length, shard_ref, own_ref, moved_ref, next_ref, out_ref, tiles, flat):
     chunks = length // 128
     shard = shard_ref[0]
     base, start, offset = shard_place(shard, length)
     move = base - CIN * ((3 * shard) // 2) + 16
-    tiles[...] = tiles_ref[...]
+
+    @pl.when(shard_ref[1] == 1)
+    def _():
+        tiles[...] = own_ref[...].astype(F32)
+
+    @pl.when(shard_ref[1] == 0)
+    def _():
+        tiles[...] = moved_ref[...].astype(F32)
+
     for m in range(6):
-        tiles[m, 16 + 2 * CIN : 24 + 2 * CIN, :] = next_ref[:, 128 * m : 128 * m + 128]
+        piece = next_ref[:, 128 * m : 128 * m + 128].astype(F32)
+        tiles[m, 16 + 2 * CIN : 24 + 2 * CIN, :] = piece[:8]
     flat[...] = jnp.zeros_like(flat)
 
     def get(m, t):
@@ -1286,16 +1319,16 @@
         out_ref[:, 128 * (chunks - rest) :] = piece
 
 
-def flatten(shard, tiles, after, length):
+def flatten(shard, own, moved, after, length):
     return pl.pallas_call(
         partial(flatten_kernel, length),
         out_shape=jax.ShapeDtypeStruct((1, length), F32),
-        in_specs=[pl.BlockSpec(memory_space=pltpu.SMEM), vspec(), vspec()],
+        in_specs=[pl.BlockSpec(memory_space=pltpu.SMEM), vspec(), vspec(), vspec()],
         out_specs=vspec(),
-        scratch_shapes=[pltpu.VMEM((6, 1384, 128), F32), pltpu.VMEM((5256, 128), F32)],
+        scratch_shapes=[pltpu.VMEM((6, TROWS, 128), F32), pltpu.VMEM((5256, 128), F32)],
         cost_estimate=LIGHT,
         compiler_params=params(),
-    )(shard, tiles, after)
+    )(shard, own, moved, after)
 
 
 def wide(block):
@@ -1313,50 +1346,57 @@
     places = [(d, y) for d in range(dp_count) for y in range(2)]
     number = lambda d, y: 2 * d + y
     mirror = [(number(d, y), number(d - d % 2 + y, d % 2)) for d, y in places]
+    crossing = [pair for pair in mirror if pair[0] != pair[1]]
     other_core = [(number(d, y), number(d + 1 - 2 * (d % 2), y)) for d, y in places]
     same_core = [[number(d, y) for d, y in places if d % 2 == c] for c in range(2)]
     stays = core == lat_index
 
     def mirrored(block):
-        moved = lax.ppermute(block, axes, [pair for pair in mirror if pair[0] != pair[1]])
+        moved = lax.ppermute(block, axes, crossing)
         return jnp.where(stays, block, moved)
 
     swapped = lambda a: lax.ppermute(a, axes, other_core)
-    half = core.astype(jnp.int32).reshape(1)
     tables = {name: jnp.asarray(value) for name, value in plan_tables().items()}
 
     main, side = spectral_window(dp_index.astype(jnp.int32).reshape(1), spectral_flat)
     weights, column = gather_rows(length, main, side)
     mlp_whole = lax.all_gather(mlp_flat.reshape(-1, 128), axes, axis=0, tiled=False)
-    mlp_whole, weights = lax.optimization_barrier((mlp_whole, weights))
+    moved = lax.ppermute(wide(cotangent), axes, crossing)
+    mlp_whole, weights, moved = lax.optimization_barrier((mlp_whole, weights, moved))
     state = mirrored(wide(fields))
     noise = mirrored(noise_fields).reshape(STEPS, CELLS, NOISE)
     noise = jnp.pad(noise, ((0, 0), (0, 0), (1, 128 - 1 - NOISE)))
     counts = mirrored(step_counts)
-    later, weights = lax.optimization_barrier((cotangent, weights))
-    grad = mirrored(wide(later))
     w_in, w_out, vectors = mlp_weights(mlp_whole)
 
     kept = []
     for step in range(STEPS):
-        mask = (step < counts).astype(F32)
+        mask = jnp.broadcast_to((step < counts).astype(F32).reshape(1, 1), (1, 128))
         lon_modes = modes(state, noise[step], vectors, tables["fourier_t"])
-        parts, mixed = mix(half, lon_modes, swapped(lon_modes), tables["analyse"], weights, column, False)
+        parts, mixed = mix(lon_modes, tables["analyse"], weights, column, False)
         following, middle, hidden, active, slope = feed(
-            half, mask, mixed, swapped(mixed), tables["synthesize"], tables["inverse_t"], state, vectors,
-            w_in, w_out, step == STEPS - 1,
+            mask, mixed, tables["synthesize"], tables["inverse_t"], state, vectors, w_in, w_out,
+            step == STEPS - 1,
         )
         kept.append((mask, state, parts, middle, hidden, active, slope))
         state = following
     output = mirrored(state)
+    grad = jnp.where(stays, wide(cotangent), moved)
 
     def to_owners(parts):
         return lax.all_to_all(
             parts, axes, split_axis=0, concat_axis=0, tiled=True, axis_index_groups=same_core
         )
 
-    coeff_parts = [to_owners(kept[step][2]) for step in range(STEPS)]
-    grad_parts = [None] * STEPS
+    received = []
+
+    def to_owners_next(parts):
+        if received:
+            parts, received[-1] = lax.optimization_barrier((parts, received[-1]))
+        received.append(to_owners(parts))
+
+    for step in range(STEPS):
+        to_owners_next(kept[step][2])
     results = [None] * STEPS
     pres = [None] * STEPS
     feed_sums = first_sums = 0.0
@@ -1367,11 +1407,11 @@
         )
         feed_sums = feed_sums + sums
         parts, grad_coeffs = mix(
-            half, grad_modes, swapped(grad_modes), tables["synthesize_back"], weights, column, True
+            grad_modes, tables["synthesize_back"], weights, column, True
         )
-        grad_parts[step] = to_owners(parts)
+        to_owners_next(parts)
         grad, sums = first_back(
-            half, grad_coeffs, swapped(grad_coeffs), tables["analyse_back"], tables["fourier"], state, gm,
+            grad_coeffs, tables["analyse_back"], tables["fourier"], state, gm,
             vectors, step == 0,
         )
         first_sums = first_sums + sums
@@ -1387,13 +1427,14 @@
     )
     mlp_grad = jnp.sum(pair.astype(F32), axis=0)[: mlp_flat.shape[0] // 128].reshape(-1)
 
-    owner = (dp_index - core + lat_index).astype(jnp.int32).reshape(1)
     odd = lat_index.astype(jnp.int32).reshape(1)
-    tiles, head = spectral_grads(odd, coeff_parts, grad_parts)
+    tiles, head = spectral_grads(odd, received[:2], [received[3], received[2]])
     spot = lambda s, c: number(s - s % 2 + c, s % 2)
-    earlier = [(spot(s, c), spot(s - 1, c)) for s in range(1, dp_count) for c in range(2)]
+    earlier = [(spot(s, c), number(s - 1, c)) for s in range(2, dp_count, 2) for c in range(2)]
     after = lax.ppermute(head, axes, earlier)
-    spectral_grad = mirrored(flatten(owner, tiles, after, length))
+    moved = lax.ppermute(tiles, axes, crossing)
+    place = jnp.stack([dp_index.astype(jnp.int32), stays.astype(jnp.int32)])
+    spectral_grad = flatten(place, tiles, moved, after, length)
     narrow = lambda a: a[:, :D].reshape(1, ROWS, NLON, D)
     return narrow(output), narrow(fields_grad), spectral_grad, mlp_grad
 

time: 778 us -> 748 us (0.961)
  starting transfers between devices: 130 us -> 74.5 us
  Pallas kernels: 500 us -> 536 us
    ppermute x7, starting transfers between devices: 66.5 us -> 24.8 us  [the longest x5 19.6 us: mirrored(): moved = lax.ppermute(block, axes, crossing)]
    pallas_call x10, Pallas kernels: 179 us -> 213 us  [the longest x4 86.3 us: mix(): pl.pallas_call(mix_back_kernel if back else mix_kernel, in_specs=[vspec()...]
    ppermute x9 -> x1, waiting for transfers between devices: 21.3 us -> 0.01 us  [shards_paired(): swapped = lambda a: lax.ppermute(a, axes, other_core)]
    ppermute x7, waiting for transfers between devices: 38.6 us -> 59.6 us  [the longest x5 45.3 us: mirrored(): moved = lax.ppermute(block, axes, crossing)]
    all_to_all x4, starting transfers between devices: 53.3 us -> 41.9 us  [to_owners(): lax.all_to_all(parts, axes, split_axis=0, concat_axis=0, tiled=True, axis...]
    select_n x6 -> x4, other arithmetic: 21.5 us -> 13.2 us  [mirrored(): return jnp.where(stays, block, moved)]
    unnamed x38 -> x34, local copies, waits for them, and re-layouts: 16.4 us -> 12.7 us
  transfers between devices with their start and end apart: 23 -> 15, of which waited for: 9 -> 6; matrix products, arithmetic and copies ran while one was open for 4% -> 5% of each run, Pallas kernels for 59% -> 64%
where the time goes in v3:
time: 748 us; the launch traced here: 739 us
  Pallas kernels  536 us (72%)
  starting transfers between devices  74.5 us (10%)
  waiting for transfers between devices  65.1 us (9%)
  local copies, waits for them, and re-layouts  25.6 us (3%)
  other arithmetic  22.2 us (3%)
  between operations  15.9 us (2%)
    pallas_call x1, Pallas kernels, gather_rows(): pl.pallas_call(partial(gather_kernel, length), out_shape=(jax.ShapeDtypeS...  182 us
    pallas_call x4, Pallas kernels, mix(): pl.pallas_call(mix_back_kernel if back else mix_kernel, in_specs=[vspec()...  86.3 us
    pallas_call x2, Pallas kernels, feed(): pl.pallas_call(feed_kernel, grid=(ROWS // BLK,), in_specs=[fixed(1, 128),...  50.4 us
    ppermute x5, waiting for transfers between devices, mirrored(): moved = lax.ppermute(block, axes, crossing)  45.3 us
    all_to_all x4, starting transfers between devices, to_owners(): lax.all_to_all(parts, axes, split_axis=0, concat_axis=0, tiled=True, axis...  41.9 us
    pallas_call x2, Pallas kernels, feed_back(): pl.pallas_call(feed_back_kernel, grid=(ROWS // BLK,), in_specs=[fixed(1,...  40.9 us
    pallas_call x1, Pallas kernels, mlp_grads(): pl.pallas_call(mlp_flat_kernel, out_shape=jax.ShapeDtypeStruct((2, 16, 41...  35.7 us
    pallas_call x2, Pallas kernels, first_back(): pl.pallas_call(first_back_kernel, grid=(ROWS // BLK,), in_specs=[fixed(24...  35.1 us
  transfers between devices with their start and end apart: 15, of which 6 were waited for; matrix products, arithmetic and copies ran while one was open for 5% of the time, Pallas kernels for 64%

profile of v3, /device:TPU:1, one launch (start us, length us, event | category | flops | bytes accessed | tf_op | source)
XLA Modules:
  0.0 739.4 jit_solution(3567003397492870117)
XLA Ops:
  7.2 0.7 all-gather.2.cloned.1.call-update
  7.9 3.7 pad.12
  11.6 4.5 collective-permute-start.1
  16.1 1.8 pad.14
  17.9 1.9 collective-permute-start.3
  19.8 3.6 collective-permute-start.2
  23.5 10.0 %shard_map.165 = (bf16[944,640]{1,0:T(8,128)(2,1)}, bf16[64,640]{1,0:T(8,128)(2,1)}) custom-call(s32[1]{0:T(128)} %bitcast.6.shard_ref, bf16[1,624128]{1,0:T(2,128)(2,1)} %flat_ref.1), custom_call_target="tpu_custom_call" | custom-call | flops 1 | bytes 1 | tf_op jit(solution)/shard_map/pallas_call | solution.py:491
  33.5 1.3 copy-done.1
  34.8 0.9 copy-done.3
  35.7 182.2 %shard_map.166 = (bf16[15584,640]{1,0:T(8,128)(2,1)S(1)}, f32[24,768]{1,0:T(8,128)S(1)}) custom-call(bf16[944,640]{1,0:T(8,128)(2,1)S(1)} %copy-done.1, bf16[64,640]{1,0:T(8,128)(2,1)S(1)} %copy-done.3), custom_call_target="tpu_custom_call" | custom-call | flops 1 | bytes 1 | tf_op jit(solution)/shard_map/pallas_call | solution.py:770
  217.9 6.7 copy-done
  224.6 0.6 copy-done.2
  225.2 0.6 broadcast_select_fusion.2
  225.9 1.5 reshape.47
  227.3 1.3 fusion.2
  228.6 3.9 broadcast_select_fusion.1.state_ref
  232.5 26.1 %shard_map.167 = (bf16[768,1408]{1,0:T(8,128)(2,1)}, bf16[1408,768]{1,0:T(8,128)(2,1)}, f32[8,1408]{1,0:T(8,128)}) custom-call(bf16[32,403,128]{2,1,0:T(8,128)(2,1)} %all-gather.2.cloned.1.call-done.flat_ref), custom_call_target="tpu_custom_call" | custom-call | flops 1 | bytes 1 | tf_op jit(solution)/shard_map/pallas_call | solution.py:548
  258.6 7.1 shard_map.168.own_ref
  265.7 19.6 %shard_map.169 = (bf16[16,9,72,128]{3,2,1,0:T(8,128)(2,1)}, bf16[24,9,8,768]{3,2,1,0:T(8,128)(2,1)}) custom-call(bf16[24,9,8,768]{3,2,1,0:T(8,128)(2,1)} %shard_map.168.own_ref, bf16[2,9,192,384]{3,2,1,0:T(8,128)(2,1)} %constant.59.clone.table_ref, f32[24,768]{1,0:T(8,128)} %copy-done.2, bf16[15584,640]{1,0:T(8,128)(2,1)} %copy-done), custom_call_target="tpu_custom_call" | custom-call | flops 1 | bytes 1 | tf_op jit(solution)/shard_map/pallas_call | solution.py:987
  285.4 8.9 %all-to-all-start = ((bf16[16,9,72,128]{3,2,1,0:T(8,128)(2,1)}), bf16[16,9,72,128]{3,2,1,0:T(8,128)(2,1)S(1)}, u32[]{:S(2)}, u32[]{:S(2)}) async-start(bf16[16,9,72,128]{3,2,1,0:T(8,128)(2,1)} %get-tuple-element.83), calls=%async_computation | async-start | bytes 5308416 | tf_op jit(solution)/shard_map/all_to_all | solution.py:1387
  294.3 5.9 collective-permute-start
  300.9 0.5 collective-permute-done
  302.0 0.5 broadcast_in_dim.23.mask_ref
  302.5 25.1 %shard_map.170 = (f32[1728,768]{1,0:T(8,128)}, f32[1728,768]{1,0:T(8,128)}, bf16[1728,768]{1,0:T(8,128)(2,1)}, bf16[1728,1408]{1,0:T(8,128)(2,1)}, bf16[1728,1408]{1,0:T(8,128)(2,1)}) custom-call(f32[1,128]{1,0:T(1,128)} %broadcast_in_dim.23.mask_ref, bf16[24,9,8,768]{3,2,1,0:T(8,128)(2,1)} %get-tuple-element.63.own_ref, ...), custom_call_target="tpu_custom_call" | custom-call | flops 1 | bytes 1 | tf_op jit(solution)/shard_map/pallas_call | solution.py:1042
  327.6 7.5 %shard_map.171.own_ref = bf16[24,9,8,768]{3,2,1,0:T(8,128)(2,1)} custom-call(f32[1728,768]{1,0:T(8,128)} %get-tuple-element.66.state_ref, bf16[1728,128]{1,0:T(8,128)(2,1)} %get-tuple-element.108.noise_ref, f32[8,1408]{1,0:T(8,128)} %get-tuple-element.60.vec_ref, bf16[72,216]{1,0:T(8,128)(2,1)} %constant.55.clone.table_ref), custom_call_target="tpu_custom_call" | custom-call | flops 1 | bytes 1 | tf_op jit(solution)/shard_map/pallas_call | solution.py:820
  335.1 19.8 %shard_map.172 = (bf16[16,9,72,128]{3,2,1,0:T(8,128)(2,1)}, bf16[24,9,8,768]{3,2,1,0:T(8,128)(2,1)}) custom-call(bf16[24,9,8,768]{3,2,1,0:T(8,128)(2,1)} %shard_map.171.own_ref, bf16[2,9,192,384]{3,2,1,0:T(8,128)(2,1)} %constant.59.clone.table_ref, f32[24,768]{1,0:T(8,128)} %copy-done.2, bf16[15584,640]{1,0:T(8,128)(2,1)} %copy-done), custom_call_target="tpu_custom_call" | custom-call | flops 1 | bytes 1 | tf_op jit(solution)/shard_map/pallas_call | solution.py:987
  354.9 1.5 copy-done.9
  356.4 10.9 %all-to-all-start.1 = ((bf16[16,9,72,128]{3,2,1,0:T(8,128)(2,1)}), bf16[16,9,72,128]{3,2,1,0:T(8,128)(2,1)}, u32[]{:S(2)}, u32[]{:S(2)}) async-start(bf16[16,9,72,128]{3,2,1,0:T(8,128)(2,1)} %get-tuple-element.86), calls=%async_computation.1 | async-start | bytes 5308416 | tf_op jit(solution)/shard_map/all_to_all | solution.py:1387
  367.3 0.5 broadcast_in_dim.20.mask_ref
  367.8 25.4 %shard_map.173 = (bf16[1728,768]{1,0:T(8,128)(2,1)}, f32[1728,768]{1,0:T(8,128)}, bf16[1728,768]{1,0:T(8,128)(2,1)}, bf16[1728,1408]{1,0:T(8,128)(2,1)}, bf16[1728,1408]{1,0:T(8,128)(2,1)}) custom-call(f32[1,128]{1,0:T(1,128)} %broadcast_in_dim.20.mask_ref, bf16[24,9,8,768]{3,2,1,0:T(8,128)(2,1)} %get-tuple-element.67.own_ref, ...), custom_call_target="tpu_custom_call" | custom-call | flops 1 | bytes 1 | tf_op jit(solution)/shard_map/pallas_call | solution.py:1042
  393.2 3.9 broadcast_select_fusion.grad_ref
  397.1 20.4 %shard_map.174 = (bf16[1728,768]{1,0:T(8,128)(2,1)}, bf16[1728,1408]{1,0:T(8,128)(2,1)}, f32[1728,768]{1,0:T(8,128)}, bf16[24,9,8,768]{3,2,1,0:T(8,128)(2,1)}, f32[8,1408]{1,0:T(8,128)}) custom-call(f32[1,128]{1,0:T(1,128)} %broadcast_in_dim.20.mask_ref, bf16[1728,768]{1,0:T(8,128)(2,1)} %broadcast_select_fusion.grad_ref, ...), custom_call_target="tpu_custom_call" | custom-call | flops 1 | bytes 1 | tf_op jit(solution)/shard_map/pallas_call | solution.py:1094
  417.5 23.4 %shard_map.175 = (bf16[16,11,72,128]{3,2,1,0:T(8,128)(2,1)}, bf16[24,9,8,768]{3,2,1,0:T(8,128)(2,1)}) custom-call(bf16[24,9,8,768]{3,2,1,0:T(8,128)(2,1)} %get-tuple-element.72.own_ref, bf16[2,9,192,384]{3,2,1,0:T(8,128)(2,1)} %constant.62.clone.table_ref, f32[24,768]{1,0:T(8,128)} %copy-done.2, bf16[15584,640]{1,0:T(8,128)(2,1)} %copy-done), custom_call_target="tpu_custom_call" | custom-call | flops 1 | bytes 1 | tf_op jit(solution)/shard_map/pallas_call | solution.py:987
  440.9 5.8 all-to-all-start.2
  446.7 17.0 %shard_map.176 = (f32[1728,768]{1,0:T(8,128)}, f32[8,768]{1,0:T(8,128)}) custom-call(bf16[24,9,8,768]{3,2,1,0:T(8,128)(2,1)} %get-tuple-element.73.own_ref, bf16[2,9,192,384]{3,2,1,0:T(8,128)(2,1)} %constant.61.clone.table_ref, bf16[72,216]{1,0:T(8,128)(2,1)} %constant.56.clone.fourier_ref, f32[1728,768]{1,0:T(8,128)} %get-tuple-element.66.state_ref, ...), custom_call_target="tpu_custom_call" | custom-call | flops 1 | bytes 1 | tf_op jit(solution)/shard_map/pallas_call | solution.py:1134
  463.8 20.5 %shard_map.177 = (bf16[1728,768]{1,0:T(8,128)(2,1)}, bf16[1728,1408]{1,0:T(8,128)(2,1)}, f32[1728,768]{1,0:T(8,128)}, bf16[24,9,8,768]{3,2,1,0:T(8,128)(2,1)}, f32[8,1408]{1,0:T(8,128)}) custom-call(f32[1,128]{1,0:T(1,128)} %broadcast_in_dim.23.mask_ref, f32[1728,768]{1,0:T(8,128)} %get-tuple-element.75.grad_ref, ...), custom_call_target="tpu_custom_call" | custom-call | flops 1 | bytes 1 | tf_op jit(solution)/shard_map/pallas_call | solution.py:1094
  484.3 23.5 %shard_map.178 = (bf16[16,11,72,128]{3,2,1,0:T(8,128)(2,1)}, bf16[24,9,8,768]{3,2,1,0:T(8,128)(2,1)}) custom-call(bf16[24,9,8,768]{3,2,1,0:T(8,128)(2,1)} %get-tuple-element.78.own_ref, bf16[2,9,192,384]{3,2,1,0:T(8,128)(2,1)} %constant.62.clone.table_ref, f32[24,768]{1,0:T(8,128)} %copy-done.2, bf16[15584,640]{1,0:T(8,128)(2,1)} %copy-done), custom_call_target="tpu_custom_call" | custom-call | flops 1 | bytes 1 | tf_op jit(solution)/shard_map/pallas_call | solution.py:987
  507.8 1.7 all-to-all-done.2.g1
  509.5 1.7 copy-done.5
  511.2 16.3 %all-to-all-start.3 = ((bf16[16,11,72,128]{3,2,1,0:T(8,128)(2,1)}), bf16[16,11,72,128]{3,2,1,0:T(8,128)(2,1)}, u32[]{:S(2)}, u32[]{:S(2)}) async-start(bf16[16,11,72,128]{3,2,1,0:T(8,128)(2,1)} %get-tuple-element.90), calls=%async_computation.3 | async-start | bytes 6488064 | tf_op jit(solution)/shard_map/all_to_all | solution.py:1387
  527.5 18.0 %shard_map.179 = (bf16[1728,768]{1,0:T(8,128)(2,1)}, f32[8,768]{1,0:T(8,128)}) custom-call(bf16[24,9,8,768]{3,2,1,0:T(8,128)(2,1)} %get-tuple-element.79.own_ref, bf16[2,9,192,384]{3,2,1,0:T(8,128)(2,1)} %constant.61.clone.table_ref, bf16[72,216]{1,0:T(8,128)(2,1)} %constant.56.clone.fourier_ref, bf16[1728,768]{1,0:T(8,128)(2,1)} %broadcast_select_fusion.1.state_ref, ...), custom_call_target="tpu_custom_call" | custom-call | flops 1 | bytes 1 | tf_op jit(solution)/shard_map/pallas_call | solution.py:1134
  545.5 31.6 %shard_map.182 = (f32[11,768,128]{2,1,0:T(8,128)}, f32[6,1408,128]{2,1,0:T(8,128)}) custom-call(bf16[1728,768]{1,0:T(8,128)(2,1)} %get-tuple-element.94.h0, bf16[1728,768]{1,0:T(8,128)(2,1)} %get-tuple-element.95.h1, bf16[1728,1408]{1,0:T(8,128)(2,1)} %get-tuple-element.96.p0, bf16[1728,1408]{1,0:T(8,128)(2,1)} %get-tuple-element.97.p1, ...), custom_call_target="tpu_custom_call" | custom-call | flops 1 | bytes 1 | tf_op jit(solution)/shard_map/pallas_call | solution.py:1206
  577.1 0.6 add.29.first_sums
  577.7 0.6 add.28.feed_sums
  578.4 35.7 %shard_map.183 = bf16[2,16,416,128]{3,2,1,0:T(8,128)(2,1)} custom-call(f32[11,768,128]{2,1,0:T(8,128)} %get-tuple-element.102.gin, f32[6,1408,128]{2,1,0:T(8,128)} %get-tuple-element.103.gout, f32[8,1408]{1,0:T(8,128)} %add.28.feed_sums, f32[8,768]{1,0:T(8,128)} %add.29.first_sums), custom_call_target="tpu_custom_call" | custom-call | flops 1 | bytes 1 | tf_op jit(solution)/shard_map/pallas_call | solution.py:1215
  614.0 2.9 dynamic-slice_bitcast_fusion
  616.9 0.5 collective-permute-start.8
  617.4 3.4 collective-permute-start.5
  620.8 2.2 collective-permute-start.4
  623.0 3.1 fusion
  626.1 5.9 all-to-all-start.4
  632.0 0.6 pad_add_fusion.shard_ref
  632.6 35.8 %collective-permute-done.5 = bf16[1728,768]{1,0:T(8,128)(2,1)} collective-permute-done((bf16[1728,768]{1,0:T(8,128)(2,1)}, bf16[1728,768]{1,0:T(8,128)(2,1)}, u32[]{:S(2)}, u32[]{:S(2)}) %collective-permute-start.5) | collective-permute-done | bytes 2654240 | tf_op jit(solution)/shard_map/ppermute | solution.py:1355
  668.4 4.3 slice_select_fusion
  672.7 11.6 %shard_map.180 = (bf16[6,1392,128]{2,1,0:T(8,128)(2,1)}, bf16[16,768]{1,0:T(8,128)(2,1)}) custom-call(s32[1]{0:T(128)} %bitcast.11.odd_ref, bf16[16,9,72,128]{3,2,1,0:T(8,128)(2,1)} %copy-done.9, bf16[16,9,72,128]{3,2,1,0:T(8,128)(2,1)} %all-to-all-done.1.c1, bf16[16,11,72,128]{3,2,1,0:T(8,128)(2,1)} %all-to-all-done.3.g0, bf16[16,11,72,128]{3,2,1,0:T(8,128)(2,1)} %copy-done.5), custom_call_target="tpu_custom_call" | custom-call | flops 1 | bytes 1 | tf_op jit(solution)/shard_map/pallas_call | solution.py:1275
  684.3 3.3 collective-permute-start.6
  687.6 9.0 %collective-permute-done.4 = bf16[1728,768]{1,0:T(8,128)(2,1)} collective-permute-done((bf16[1728,768]{1,0:T(8,128)(2,1)}, bf16[1728,768]{1,0:T(8,128)(2,1)}, u32[]{:S(2)}, u32[]{:S(2)}) %collective-permute-start.4) | collective-permute-done | bytes 2654240 | tf_op jit(solution)/shard_map/ppermute | solution.py:1355
  696.6 4.3 slice_select_fusion.1
  701.0 0.2 convert_reduce_fusion
  701.2 1.3 collective-permute-start.7
  702.5 0.7 slice_bitcast_fusion
  703.2 3.1 collective-permute-done.7.next_ref
  706.4 14.3 %collective-permute-done.6.moved_ref = bf16[6,1392,128]{2,1,0:T(8,128)(2,1)} collective-permute-done((bf16[6,1392,128]{2,1,0:T(8,128)(2,1)}, bf16[6,1392,128]{2,1,0:T(8,128)(2,1)}, u32[]{:S(2)}, u32[]{:S(2)}) %collective-permute-start.6) | collective-permute-done | bytes 2138144 | tf_op jit(solution)/shard_map/ppermute | solution.py:1435
  720.7 11.6 %shard_map.181 = f32[1,624128]{1,0:T(1,128)} custom-call(s32[2]{0:T(128)} %pad_add_fusion.shard_ref, bf16[6,1392,128]{2,1,0:T(8,128)(2,1)} %get-tuple-element.92.own_ref, bf16[6,1392,128]{2,1,0:T(8,128)(2,1)} %collective-permute-done.6.moved_ref, bf16[16,768]{1,0:T(8,128)(2,1)} %copy-done.13), custom_call_target="tpu_custom_call" | custom-call | flops 1 | bytes 1 | tf_op jit(solution)/shard_map/pallas_call | solution.py:1323
  (38 shorter events, 0.1 us)
Async XLA Ops:
  7.2 225.4 %all-gather.2.cloned.1.call-start = ((), (), s32[]{:S(2)}) async-start(), calls=%async_computation.5 | async-start | bytes 3446784 | tf_op jit(solution)/shard_map/all_gather | solution.py:1363
  7.9 8.2 %copy-start.7 = (bf16[1,24,72,641]{3,2,1,0:T(8,128)(2,1)S(1)}, bf16[1,24,72,641]{3,2,1,0:T(8,128)(2,1)}, u32[]{:S(2)}) copy-start(bf16[1,24,72,641]{3,2,1,0:T(8,128)(2,1)} %param.19) | copy-start | bytes 6645892
  11.6 217.1 %collective-permute-start.1 = (bf16[1728,768]{1,0:T(8,128)(2,1)}, bf16[1728,768]{1,0:T(8,128)(2,1)}, u32[]{:S(2)}, u32[]{:S(2)}) collective-permute-start(bf16[1728,768]{1,0:T(8,128)(2,1)} %pad.12), channel_id=1, source_target_pairs={{1,2},{2,1},{5,6},{6,5},{9,10},{10,9},{13,14},{14,13},{17,18},{18,... | collective-permute-start | bytes 7962632 | tf_op jit(solution)/shard_map/ppermute | solution.py:1355
  16.1 3.7 copy-start.10
  17.9 214.6 %collective-permute-start.3 = (bf16[1728,768]{1,0:T(8,128)(2,1)}, bf16[1728,768]{1,0:T(8,128)(2,1)}, u32[]{:S(2)}, u32[]{:S(2)}) collective-permute-start(bf16[1728,768]{1,0:T(8,128)(2,1)} %pad.14), channel_id=1, source_target_pairs={{1,2},{2,1},{5,6},{6,5},{9,10},{10,9},{13,14},{14,13},{17,18},{18,... | collective-permute-start | bytes 7962632 | tf_op jit(solution)/shard_map/ppermute | solution.py:1364
  19.8 205.4 %collective-permute-start.2 = (bf16[1,2,24,576]{3,2,1,0:T(8,128)(2,1)S(1)}, bf16[1,2,24,576]{3,2,1,0:T(8,128)(2,1)S(1)}, u32[]{:S(2)}, u32[]{:S(2)}) collective-permute-start(bf16[1,2,24,576]{3,2,1,0:T(8,128)(2,1)S(1)} %copy-done.10), channel_id=1, source_target_pairs={{1,2},{2,1},{5,6},{6,5},{9,10},{10,9},{13,14},{14,13},{17,18},{18,... | collective-permute-start | bytes 165896 | tf_op jit(solution)/shard_map/ppermute | solution.py:1355
  33.5 1.3 copy-start.1
  34.8 0.9 copy-start.3
  35.7 193.0 %copy-start.6 = (bf16[1,24,72,641]{3,2,1,0:T(8,128)(2,1)S(1)}, bf16[1,24,72,641]{3,2,1,0:T(8,128)(2,1)}, u32[]{:S(2)}) copy-start(bf16[1,24,72,641]{3,2,1,0:T(8,128)(2,1)} %param.14) | copy-start | bytes 6645892
  217.9 6.7 copy-start
  224.6 0.6 copy-start.2
  285.4 69.5 %all-to-all-start = ((bf16[16,9,72,128]{3,2,1,0:T(8,128)(2,1)}), bf16[16,9,72,128]{3,2,1,0:T(8,128)(2,1)S(1)}, u32[]{:S(2)}, u32[]{:S(2)}) async-start(bf16[16,9,72,128]{3,2,1,0:T(8,128)(2,1)} %get-tuple-element.83), calls=%async_computation | async-start | bytes 5308416 | tf_op jit(solution)/shard_map/all_to_all | solution.py:1387
  294.3 7.0 collective-permute-start
  354.9 1.5 copy-start.9
  356.4 84.5 %all-to-all-start.1 = ((bf16[16,9,72,128]{3,2,1,0:T(8,128)(2,1)}), bf16[16,9,72,128]{3,2,1,0:T(8,128)(2,1)}, u32[]{:S(2)}, u32[]{:S(2)}) async-start(bf16[16,9,72,128]{3,2,1,0:T(8,128)(2,1)} %get-tuple-element.86), calls=%async_computation.1 | async-start | bytes 5308416 | tf_op jit(solution)/shard_map/all_to_all | solution.py:1387
  367.8 25.4 %copy-start.8 = (bf16[1,24,72,641]{3,2,1,0:T(8,128)(2,1)S(1)}, bf16[1,24,72,641]{3,2,1,0:T(8,128)(2,1)}, u32[]{:S(2)}) copy-start(bf16[1,24,72,641]{3,2,1,0:T(8,128)(2,1)} %param.19) | copy-start | bytes 6645892
  440.9 68.5 %all-to-all-start.2 = ((bf16[16,11,72,128]{3,2,1,0:T(8,128)(2,1)}), bf16[16,11,72,128]{3,2,1,0:T(8,128)(2,1)S(1)}, u32[]{:S(2)}, u32[]{:S(2)}) async-start(bf16[16,11,72,128]{3,2,1,0:T(8,128)(2,1)} %get-tuple-element.89), calls=%async_computation.2 | async-start | bytes 6488064 | tf_op jit(solution)/shard_map/all_to_all | solution.py:1387
  509.5 1.7 copy-start.5
  511.2 115.0 %all-to-all-start.3 = ((bf16[16,11,72,128]{3,2,1,0:T(8,128)(2,1)}), bf16[16,11,72,128]{3,2,1,0:T(8,128)(2,1)}, u32[]{:S(2)}, u32[]{:S(2)}) async-start(bf16[16,11,72,128]{3,2,1,0:T(8,128)(2,1)} %get-tuple-element.90), calls=%async_computation.3 | async-start | bytes 6488064 | tf_op jit(solution)/shard_map/all_to_all | solution.py:1387
  545.5 31.6 %copy-start.14 = (f32[8,768]{1,0:T(8,128)S(1)}, f32[8,768]{1,0:T(8,128)}, u32[]{:S(2)}) copy-start(f32[8,768]{1,0:T(8,128)} %get-tuple-element.106) | copy-start | bytes 73732
  545.5 31.6 %copy-start.15 = (f32[8,768]{1,0:T(8,128)S(1)}, f32[8,768]{1,0:T(8,128)}, u32[]{:S(2)}) copy-start(f32[8,768]{1,0:T(8,128)} %get-tuple-element.107) | copy-start | bytes 73732
  545.5 32.2 %copy-start.11 = (f32[8,1408]{1,0:T(8,128)S(1)}, f32[8,1408]{1,0:T(8,128)}, u32[]{:S(2)}) copy-start(f32[8,1408]{1,0:T(8,128)} %get-tuple-element.104) | copy-start | bytes 135172
  545.5 32.2 %copy-start.12 = (f32[8,1408]{1,0:T(8,128)S(1)}, f32[8,1408]{1,0:T(8,128)}, u32[]{:S(2)}) copy-start(f32[8,1408]{1,0:T(8,128)} %get-tuple-element.105) | copy-start | bytes 135172
  614.0 9.0 %copy-start.4 = (bf16[2,16,416,128]{3,2,1,0:T(8,128)(2,1)S(1)}, bf16[2,16,416,128]{3,2,1,0:T(8,128)(2,1)}, u32[]{:S(2)}) copy-start(bf16[2,16,416,128]{3,2,1,0:T(8,128)(2,1)} %shard_map.183) | copy-start | bytes 10223620
  616.9 6.1 collective-permute-start.8
  617.4 50.9 %collective-permute-start.5 = (bf16[1728,768]{1,0:T(8,128)(2,1)}, bf16[1728,768]{1,0:T(8,128)(2,1)}, u32[]{:S(2)}, u32[]{:S(2)}) collective-permute-start(bf16[1728,768]{1,0:T(8,128)(2,1)} %get-tuple-element.81), channel_id=1, source_target_pairs={{1,2},{2,1},{5,6},{6,5},{9,10},{10,9},{13,14},{14,13},{17,18},{18,... | collective-permute-start | bytes 7962632 | tf_op jit(solution)/shard_map/ppermute | solution.py:1355
  620.8 75.8 %collective-permute-start.4 = (bf16[1728,768]{1,0:T(8,128)(2,1)}, bf16[1728,768]{1,0:T(8,128)(2,1)}, u32[]{:S(2)}, u32[]{:S(2)}) collective-permute-start(bf16[1728,768]{1,0:T(8,128)(2,1)} %get-tuple-element.68), channel_id=1, source_target_pairs={{1,2},{2,1},{5,6},{6,5},{9,10},{10,9},{13,14},{14,13},{17,18},{18,... | collective-permute-start | bytes 7962632 | tf_op jit(solution)/shard_map/ppermute | solution.py:1355
  626.1 74.8 %all-to-all-start.4 = ((bf16[16,416,128]{2,1,0:T(8,128)(2,1)}), bf16[16,416,128]{2,1,0:T(8,128)(2,1)S(1)}, u32[]{:S(2)}, u32[]{:S(2)}) async-start(bf16[16,416,128]{2,1,0:T(8,128)(2,1)} %fusion), calls=%async_computation.4 | async-start | bytes 3407872 | tf_op jit(solution)/shard_map/all_to_all | solution.py:1425
  684.3 16.9 %copy-start.16 = (bf16[16,768]{1,0:T(8,128)(2,1)S(1)}, bf16[16,768]{1,0:T(8,128)(2,1)}, u32[]{:S(2)}) copy-start(bf16[16,768]{1,0:T(8,128)(2,1)} %get-tuple-element.93) | copy-start | bytes 73732
  684.3 36.4 %collective-permute-start.6 = (bf16[6,1392,128]{2,1,0:T(8,128)(2,1)}, bf16[6,1392,128]{2,1,0:T(8,128)(2,1)}, u32[]{:S(2)}, u32[]{:S(2)}) collective-permute-start(bf16[6,1392,128]{2,1,0:T(8,128)(2,1)} %get-tuple-element.92.own_ref), channel_id=1, source_target_pairs={{1,2},{2,1},{5,6},{6,5},{9,10},{10,9},{13,14},{14,13},{17,18},{18,... | collective-permute-start | bytes 6414344 | tf_op jit(solution)/shard_map/ppermute | solution.py:1435
  701.2 5.1 collective-permute-start.7
  706.4 14.3 %copy-start.13 = (bf16[16,768]{1,0:T(8,128)(2,1)}, bf16[16,768]{1,0:T(8,128)(2,1)S(1)}, u32[]{:S(2)}) copy-start(bf16[16,768]{1,0:T(8,128)(2,1)S(1)} %collective-permute-done.7.next_ref) | copy-start | bytes 73732
Sparse Core Ops, SparseCore 0:
  10.9 70.0 all-gather.1

commit v4 on v3

--- a/solution.py
+++ b/solution.py
@@ -530,12 +530,12 @@
         def put_in(m, t, piece, part=part):
             tin[m, pl.ds(t + 512 * part, 8, stride=64), :] = piece
 
-        rows_out(flat, IN_AT // 128 + 641 * 8 * part, IN_AT % 128, 2, 10, 11, 2, put_in, 64, 2)
+        rows_out(flat, IN_AT // 128 + 641 * 8 * part, IN_AT % 128, 2, 10, 11, 2, put_in, 64, 4)
 
         def put_out(m, t, piece, part=part):
             tout[m, pl.ds(t + 1024 * part, 8, stride=128), :] = piece
 
-        rows_out(flat, OUT_AT // 128 + 641 * 8 * part, OUT_AT % 128, 1, 5, 6, 1, put_out, 128, 4)
+        rows_out(flat, OUT_AT // 128 + 641 * 8 * part, OUT_AT % 128, 1, 5, 6, 1, put_out, 128, 8)
     keep = lax.broadcasted_iota(jnp.int32, (DP, 128), 0) < D
     for m in range(11):
         in_ref[:, 128 * m : 128 * m + 128] = jnp.where(keep, tin[m, :DP, :], 0.0).astype(BF)
@@ -1184,14 +1184,14 @@
         def get_in(m, t, part=part):
             return tin[m, pl.ds(t + 512 * part, 8, stride=64), :]
 
-        rows_in(flat_ref, IN_AT // 128 + 641 * 8 * part, IN_AT % 128, 2, 10, 11, get_in, 64, 1)
+        rows_in(flat_ref, IN_AT // 128 + 641 * 8 * part, IN_AT % 128, 2, 10, 11, get_in, 64, 4)
 
     for part in range(2):
 
         def get_out(m, t, part=part):
             return tout[m, pl.ds(t + 1024 * part, 8, stride=128), :]
 
-        rows_in(flat_ref, OUT_AT // 128 + 641 * 8 * part, OUT_AT % 128, 1, 5, 6, get_out, 128, 2)
+        rows_in(flat_ref, OUT_AT // 128 + 641 * 8 * part, OUT_AT % 128, 1, 5, 6, get_out, 128, 8)
     for k in range(32):
         piece = flat_ref[SHARD_ROWS * k : SHARD_ROWS * k + SHARD_ROWS, :]
         piece = jnp.concatenate([piece, jnp.zeros((416 - SHARD_ROWS, 128), F32)], axis=0)
@@ -1305,7 +1305,7 @@
     def get(m, t):
         return tiles[m, pl.ds(t + move, 8, stride=128), :]
 
-    rows_in(flat, start, offset, 1, 5, 6, get, 128)
+    rows_in(flat, start, offset, 1, 5, 6, get, 128, 8)
 
     def save(i, carry):
         piece = flat[pl.ds(pl.multiple_of(88 + 8 * i, 8), 8), :].reshape(1, 1024)

time: 748 us -> 724 us (0.968)
  Pallas kernels: 536 us -> 512 us
    pallas_call x1, Pallas kernels: 35.7 us -> 19.9 us  [mlp_grads(): pl.pallas_call(mlp_flat_kernel, out_shape=jax.ShapeDtypeStruct((2, 16, 41...]
where the time goes in v4:
time: 724 us; the launch traced here: 715 us
  Pallas kernels  512 us (71%)
  starting transfers between devices  74.4 us (10%)
  waiting for transfers between devices  65.1 us (9%)
  local copies, waits for them, and re-layouts  25.6 us (4%)
  other arithmetic  22.2 us (3%)
  between operations  15.9 us (2%)
    pallas_call x1, Pallas kernels, gather_rows(): pl.pallas_call(partial(gather_kernel, length), out_shape=(jax.ShapeDtypeS...  182 us
    pallas_call x4, Pallas kernels, mix(): pl.pallas_call(mix_back_kernel if back else mix_kernel, in_specs=[vspec()...  86.3 us
    pallas_call x2, Pallas kernels, feed(): pl.pallas_call(feed_kernel, grid=(ROWS // BLK,), in_specs=[fixed(1, 128),...  50.4 us
    ppermute x5, waiting for transfers between devices, mirrored(): moved = lax.ppermute(block, axes, crossing)  45.3 us
    all_to_all x4, starting transfers between devices, to_owners(): lax.all_to_all(parts, axes, split_axis=0, concat_axis=0, tiled=True, axis...  41.9 us
    pallas_call x2, Pallas kernels, feed_back(): pl.pallas_call(feed_back_kernel, grid=(ROWS // BLK,), in_specs=[fixed(1,...  40.9 us
    pallas_call x2, Pallas kernels, first_back(): pl.pallas_call(first_back_kernel, grid=(ROWS // BLK,), in_specs=[fixed(24...  35.1 us
    pallas_call x1, Pallas kernels, mlp_grads(): pl.pallas_call(mlp_grad_kernel, out_shape=(jax.ShapeDtypeStruct((11, DP,...  31.6 us
  transfers between devices with their start and end apart: 15, of which 6 were waited for; matrix products, arithmetic and copies ran while one was open for 5% of the time, Pallas kernels for 64%

profile of v4, /device:TPU:1, one launch (start us, length us, event | category | flops | bytes accessed | tf_op | source)
XLA Modules:
  0.0 715.2 jit_solution(15532762663694058066)
XLA Ops:
  7.2 0.7 all-gather.2.cloned.1.call-update
  7.9 3.7 pad.12
  11.6 4.5 collective-permute-start.1
  16.1 1.8 pad.14
  17.9 1.9 collective-permute-start.3
  19.8 3.6 collective-permute-start.2
  23.5 10.0 %shard_map.165 = (bf16[944,640]{1,0:T(8,128)(2,1)}, bf16[64,640]{1,0:T(8,128)(2,1)}) custom-call(s32[1]{0:T(128)} %bitcast.6.shard_ref, bf16[1,624128]{1,0:T(2,128)(2,1)} %flat_ref.1), custom_call_target="tpu_custom_call" | custom-call | flops 1 | bytes 1 | tf_op jit(solution)/shard_map/pallas_call | solution.py:491
  33.5 1.3 copy-done.1
  34.8 0.9 copy-done.3
  35.7 182.2 %shard_map.166 = (bf16[15584,640]{1,0:T(8,128)(2,1)S(1)}, f32[24,768]{1,0:T(8,128)S(1)}) custom-call(bf16[944,640]{1,0:T(8,128)(2,1)S(1)} %copy-done.1, bf16[64,640]{1,0:T(8,128)(2,1)S(1)} %copy-done.3), custom_call_target="tpu_custom_call" | custom-call | flops 1 | bytes 1 | tf_op jit(solution)/shard_map/pallas_call | solution.py:770
  217.9 6.7 copy-done
  224.6 0.6 copy-done.2
  225.2 0.6 broadcast_select_fusion.2
  225.9 1.5 reshape.47
  227.3 1.3 fusion.2
  228.6 3.9 broadcast_select_fusion.1.state_ref
  232.5 21.0 %shard_map.167 = (bf16[768,1408]{1,0:T(8,128)(2,1)}, bf16[1408,768]{1,0:T(8,128)(2,1)}, f32[8,1408]{1,0:T(8,128)}) custom-call(bf16[32,403,128]{2,1,0:T(8,128)(2,1)} %all-gather.2.cloned.1.call-done.flat_ref), custom_call_target="tpu_custom_call" | custom-call | flops 1 | bytes 1 | tf_op jit(solution)/shard_map/pallas_call | solution.py:548
  253.5 7.1 shard_map.168.own_ref
  260.7 19.6 %shard_map.169 = (bf16[16,9,72,128]{3,2,1,0:T(8,128)(2,1)}, bf16[24,9,8,768]{3,2,1,0:T(8,128)(2,1)}) custom-call(bf16[24,9,8,768]{3,2,1,0:T(8,128)(2,1)} %shard_map.168.own_ref, bf16[2,9,192,384]{3,2,1,0:T(8,128)(2,1)} %constant.59.clone.table_ref, f32[24,768]{1,0:T(8,128)} %copy-done.2, bf16[15584,640]{1,0:T(8,128)(2,1)} %copy-done), custom_call_target="tpu_custom_call" | custom-call | flops 1 | bytes 1 | tf_op jit(solution)/shard_map/pallas_call | solution.py:987
  280.3 8.9 %all-to-all-start = ((bf16[16,9,72,128]{3,2,1,0:T(8,128)(2,1)}), bf16[16,9,72,128]{3,2,1,0:T(8,128)(2,1)S(1)}, u32[]{:S(2)}, u32[]{:S(2)}) async-start(bf16[16,9,72,128]{3,2,1,0:T(8,128)(2,1)} %get-tuple-element.83), calls=%async_computation | async-start | bytes 5308416 | tf_op jit(solution)/shard_map/all_to_all | solution.py:1387
  289.2 5.9 collective-permute-start
  295.8 0.5 collective-permute-done
  296.9 0.5 broadcast_in_dim.23.mask_ref
  297.4 25.1 %shard_map.170 = (f32[1728,768]{1,0:T(8,128)}, f32[1728,768]{1,0:T(8,128)}, bf16[1728,768]{1,0:T(8,128)(2,1)}, bf16[1728,1408]{1,0:T(8,128)(2,1)}, bf16[1728,1408]{1,0:T(8,128)(2,1)}) custom-call(f32[1,128]{1,0:T(1,128)} %broadcast_in_dim.23.mask_ref, bf16[24,9,8,768]{3,2,1,0:T(8,128)(2,1)} %get-tuple-element.63.own_ref, ...), custom_call_target="tpu_custom_call" | custom-call | flops 1 | bytes 1 | tf_op jit(solution)/shard_map/pallas_call | solution.py:1042
  322.5 7.5 %shard_map.171.own_ref = bf16[24,9,8,768]{3,2,1,0:T(8,128)(2,1)} custom-call(f32[1728,768]{1,0:T(8,128)} %get-tuple-element.66.state_ref, bf16[1728,128]{1,0:T(8,128)(2,1)} %get-tuple-element.108.noise_ref, f32[8,1408]{1,0:T(8,128)} %get-tuple-element.60.vec_ref, bf16[72,216]{1,0:T(8,128)(2,1)} %constant.55.clone.table_ref), custom_call_target="tpu_custom_call" | custom-call | flops 1 | bytes 1 | tf_op jit(solution)/shard_map/pallas_call | solution.py:820
  330.0 19.8 %shard_map.172 = (bf16[16,9,72,128]{3,2,1,0:T(8,128)(2,1)}, bf16[24,9,8,768]{3,2,1,0:T(8,128)(2,1)}) custom-call(bf16[24,9,8,768]{3,2,1,0:T(8,128)(2,1)} %shard_map.171.own_ref, bf16[2,9,192,384]{3,2,1,0:T(8,128)(2,1)} %constant.59.clone.table_ref, f32[24,768]{1,0:T(8,128)} %copy-done.2, bf16[15584,640]{1,0:T(8,128)(2,1)} %copy-done), custom_call_target="tpu_custom_call" | custom-call | flops 1 | bytes 1 | tf_op jit(solution)/shard_map/pallas_call | solution.py:987
  349.8 1.5 copy-done.9
  351.3 10.9 %all-to-all-start.1 = ((bf16[16,9,72,128]{3,2,1,0:T(8,128)(2,1)}), bf16[16,9,72,128]{3,2,1,0:T(8,128)(2,1)}, u32[]{:S(2)}, u32[]{:S(2)}) async-start(bf16[16,9,72,128]{3,2,1,0:T(8,128)(2,1)} %get-tuple-element.86), calls=%async_computation.1 | async-start | bytes 5308416 | tf_op jit(solution)/shard_map/all_to_all | solution.py:1387
  362.2 0.5 broadcast_in_dim.20.mask_ref
  362.7 25.4 %shard_map.173 = (bf16[1728,768]{1,0:T(8,128)(2,1)}, f32[1728,768]{1,0:T(8,128)}, bf16[1728,768]{1,0:T(8,128)(2,1)}, bf16[1728,1408]{1,0:T(8,128)(2,1)}, bf16[1728,1408]{1,0:T(8,128)(2,1)}) custom-call(f32[1,128]{1,0:T(1,128)} %broadcast_in_dim.20.mask_ref, bf16[24,9,8,768]{3,2,1,0:T(8,128)(2,1)} %get-tuple-element.67.own_ref, ...), custom_call_target="tpu_custom_call" | custom-call | flops 1 | bytes 1 | tf_op jit(solution)/shard_map/pallas_call | solution.py:1042
  388.1 3.9 broadcast_select_fusion.grad_ref
  392.0 20.4 %shard_map.174 = (bf16[1728,768]{1,0:T(8,128)(2,1)}, bf16[1728,1408]{1,0:T(8,128)(2,1)}, f32[1728,768]{1,0:T(8,128)}, bf16[24,9,8,768]{3,2,1,0:T(8,128)(2,1)}, f32[8,1408]{1,0:T(8,128)}) custom-call(f32[1,128]{1,0:T(1,128)} %broadcast_in_dim.20.mask_ref, bf16[1728,768]{1,0:T(8,128)(2,1)} %broadcast_select_fusion.grad_ref, ...), custom_call_target="tpu_custom_call" | custom-call | flops 1 | bytes 1 | tf_op jit(solution)/shard_map/pallas_call | solution.py:1094
  412.4 23.4 %shard_map.175 = (bf16[16,11,72,128]{3,2,1,0:T(8,128)(2,1)}, bf16[24,9,8,768]{3,2,1,0:T(8,128)(2,1)}) custom-call(bf16[24,9,8,768]{3,2,1,0:T(8,128)(2,1)} %get-tuple-element.72.own_ref, bf16[2,9,192,384]{3,2,1,0:T(8,128)(2,1)} %constant.62.clone.table_ref, f32[24,768]{1,0:T(8,128)} %copy-done.2, bf16[15584,640]{1,0:T(8,128)(2,1)} %copy-done), custom_call_target="tpu_custom_call" | custom-call | flops 1 | bytes 1 | tf_op jit(solution)/shard_map/pallas_call | solution.py:987
  435.8 5.8 all-to-all-start.2
  441.7 17.0 %shard_map.176 = (f32[1728,768]{1,0:T(8,128)}, f32[8,768]{1,0:T(8,128)}) custom-call(bf16[24,9,8,768]{3,2,1,0:T(8,128)(2,1)} %get-tuple-element.73.own_ref, bf16[2,9,192,384]{3,2,1,0:T(8,128)(2,1)} %constant.61.clone.table_ref, bf16[72,216]{1,0:T(8,128)(2,1)} %constant.56.clone.fourier_ref, f32[1728,768]{1,0:T(8,128)} %get-tuple-element.66.state_ref, ...), custom_call_target="tpu_custom_call" | custom-call | flops 1 | bytes 1 | tf_op jit(solution)/shard_map/pallas_call | solution.py:1134
  458.7 20.5 %shard_map.177 = (bf16[1728,768]{1,0:T(8,128)(2,1)}, bf16[1728,1408]{1,0:T(8,128)(2,1)}, f32[1728,768]{1,0:T(8,128)}, bf16[24,9,8,768]{3,2,1,0:T(8,128)(2,1)}, f32[8,1408]{1,0:T(8,128)}) custom-call(f32[1,128]{1,0:T(1,128)} %broadcast_in_dim.23.mask_ref, f32[1728,768]{1,0:T(8,128)} %get-tuple-element.75.grad_ref, ...), custom_call_target="tpu_custom_call" | custom-call | flops 1 | bytes 1 | tf_op jit(solution)/shard_map/pallas_call | solution.py:1094
  479.2 23.5 %shard_map.178 = (bf16[16,11,72,128]{3,2,1,0:T(8,128)(2,1)}, bf16[24,9,8,768]{3,2,1,0:T(8,128)(2,1)}) custom-call(bf16[24,9,8,768]{3,2,1,0:T(8,128)(2,1)} %get-tuple-element.78.own_ref, bf16[2,9,192,384]{3,2,1,0:T(8,128)(2,1)} %constant.62.clone.table_ref, f32[24,768]{1,0:T(8,128)} %copy-done.2, bf16[15584,640]{1,0:T(8,128)(2,1)} %copy-done), custom_call_target="tpu_custom_call" | custom-call | flops 1 | bytes 1 | tf_op jit(solution)/shard_map/pallas_call | solution.py:987
  502.7 1.7 all-to-all-done.2.g1
  504.4 1.7 copy-done.5
  506.1 16.3 %all-to-all-start.3 = ((bf16[16,11,72,128]{3,2,1,0:T(8,128)(2,1)}), bf16[16,11,72,128]{3,2,1,0:T(8,128)(2,1)}, u32[]{:S(2)}, u32[]{:S(2)}) async-start(bf16[16,11,72,128]{3,2,1,0:T(8,128)(2,1)} %get-tuple-element.90), calls=%async_computation.3 | async-start | bytes 6488064 | tf_op jit(solution)/shard_map/all_to_all | solution.py:1387
  522.4 18.0 %shard_map.179 = (bf16[1728,768]{1,0:T(8,128)(2,1)}, f32[8,768]{1,0:T(8,128)}) custom-call(bf16[24,9,8,768]{3,2,1,0:T(8,128)(2,1)} %get-tuple-element.79.own_ref, bf16[2,9,192,384]{3,2,1,0:T(8,128)(2,1)} %constant.61.clone.table_ref, bf16[72,216]{1,0:T(8,128)(2,1)} %constant.56.clone.fourier_ref, bf16[1728,768]{1,0:T(8,128)(2,1)} %broadcast_select_fusion.1.state_ref, ...), custom_call_target="tpu_custom_call" | custom-call | flops 1 | bytes 1 | tf_op jit(solution)/shard_map/pallas_call | solution.py:1134
  540.5 31.6 %shard_map.182 = (f32[11,768,128]{2,1,0:T(8,128)}, f32[6,1408,128]{2,1,0:T(8,128)}) custom-call(bf16[1728,768]{1,0:T(8,128)(2,1)} %get-tuple-element.94.h0, bf16[1728,768]{1,0:T(8,128)(2,1)} %get-tuple-element.95.h1, bf16[1728,1408]{1,0:T(8,128)(2,1)} %get-tuple-element.96.p0, bf16[1728,1408]{1,0:T(8,128)(2,1)} %get-tuple-element.97.p1, ...), custom_call_target="tpu_custom_call" | custom-call | flops 1 | bytes 1 | tf_op jit(solution)/shard_map/pallas_call | solution.py:1206
  572.0 0.6 add.29.first_sums
  572.7 0.6 add.28.feed_sums
  573.3 19.9 %shard_map.183 = bf16[2,16,416,128]{3,2,1,0:T(8,128)(2,1)} custom-call(f32[11,768,128]{2,1,0:T(8,128)} %get-tuple-element.102.gin, f32[6,1408,128]{2,1,0:T(8,128)} %get-tuple-element.103.gout, f32[8,1408]{1,0:T(8,128)} %add.28.feed_sums, f32[8,768]{1,0:T(8,128)} %add.29.first_sums), custom_call_target="tpu_custom_call" | custom-call | flops 1 | bytes 1 | tf_op jit(solution)/shard_map/pallas_call | solution.py:1215
  593.2 2.9 dynamic-slice_bitcast_fusion
  596.1 0.5 collective-permute-start.8
  596.6 3.4 collective-permute-start.5
  600.0 2.2 collective-permute-start.4
  602.2 3.1 fusion
  605.3 5.9 all-to-all-start.4
  611.2 0.6 pad_add_fusion.shard_ref
  611.8 35.8 %collective-permute-done.5 = bf16[1728,768]{1,0:T(8,128)(2,1)} collective-permute-done((bf16[1728,768]{1,0:T(8,128)(2,1)}, bf16[1728,768]{1,0:T(8,128)(2,1)}, u32[]{:S(2)}, u32[]{:S(2)}) %collective-permute-start.5) | collective-permute-done | bytes 2654240 | tf_op jit(solution)/shard_map/ppermute | solution.py:1355
  647.5 4.3 slice_select_fusion
  651.9 11.6 %shard_map.180 = (bf16[6,1392,128]{2,1,0:T(8,128)(2,1)}, bf16[16,768]{1,0:T(8,128)(2,1)}) custom-call(s32[1]{0:T(128)} %bitcast.11.odd_ref, bf16[16,9,72,128]{3,2,1,0:T(8,128)(2,1)} %copy-done.9, bf16[16,9,72,128]{3,2,1,0:T(8,128)(2,1)} %all-to-all-done.1.c1, bf16[16,11,72,128]{3,2,1,0:T(8,128)(2,1)} %all-to-all-done.3.g0, bf16[16,11,72,128]{3,2,1,0:T(8,128)(2,1)} %copy-done.5), custom_call_target="tpu_custom_call" | custom-call | flops 1 | bytes 1 | tf_op jit(solution)/shard_map/pallas_call | solution.py:1275
  663.5 3.3 collective-permute-start.6
  666.8 9.0 %collective-permute-done.4 = bf16[1728,768]{1,0:T(8,128)(2,1)} collective-permute-done((bf16[1728,768]{1,0:T(8,128)(2,1)}, bf16[1728,768]{1,0:T(8,128)(2,1)}, u32[]{:S(2)}, u32[]{:S(2)}) %collective-permute-start.4) | collective-permute-done | bytes 2654240 | tf_op jit(solution)/shard_map/ppermute | solution.py:1355
  675.8 4.3 slice_select_fusion.1
  680.1 0.2 convert_reduce_fusion
  680.4 1.3 collective-permute-start.7
  681.7 0.7 slice_bitcast_fusion
  682.4 3.1 collective-permute-done.7.next_ref
  685.5 14.3 %collective-permute-done.6.moved_ref = bf16[6,1392,128]{2,1,0:T(8,128)(2,1)} collective-permute-done((bf16[6,1392,128]{2,1,0:T(8,128)(2,1)}, bf16[6,1392,128]{2,1,0:T(8,128)(2,1)}, u32[]{:S(2)}, u32[]{:S(2)}) %collective-permute-start.6) | collective-permute-done | bytes 2138144 | tf_op jit(solution)/shard_map/ppermute | solution.py:1435
  699.9 8.2 %shard_map.181 = f32[1,624128]{1,0:T(1,128)} custom-call(s32[2]{0:T(128)} %pad_add_fusion.shard_ref, bf16[6,1392,128]{2,1,0:T(8,128)(2,1)} %get-tuple-element.92.own_ref, bf16[6,1392,128]{2,1,0:T(8,128)(2,1)} %collective-permute-done.6.moved_ref, bf16[16,768]{1,0:T(8,128)(2,1)} %copy-done.13), custom_call_target="tpu_custom_call" | custom-call | flops 1 | bytes 1 | tf_op jit(solution)/shard_map/pallas_call | solution.py:1323
  (38 shorter events, 0.1 us)
Async XLA Ops:
  7.2 225.4 %all-gather.2.cloned.1.call-start = ((), (), s32[]{:S(2)}) async-start(), calls=%async_computation.5 | async-start | bytes 3446784 | tf_op jit(solution)/shard_map/all_gather | solution.py:1363
  7.9 8.2 %copy-start.7 = (bf16[1,24,72,641]{3,2,1,0:T(8,128)(2,1)S(1)}, bf16[1,24,72,641]{3,2,1,0:T(8,128)(2,1)}, u32[]{:S(2)}) copy-start(bf16[1,24,72,641]{3,2,1,0:T(8,128)(2,1)} %param.19) | copy-start | bytes 6645892
  11.6 217.1 %collective-permute-start.1 = (bf16[1728,768]{1,0:T(8,128)(2,1)}, bf16[1728,768]{1,0:T(8,128)(2,1)}, u32[]{:S(2)}, u32[]{:S(2)}) collective-permute-start(bf16[1728,768]{1,0:T(8,128)(2,1)} %pad.12), channel_id=1, source_target_pairs={{1,2},{2,1},{5,6},{6,5},{9,10},{10,9},{13,14},{14,13},{17,18},{18,... | collective-permute-start | bytes 7962632 | tf_op jit(solution)/shard_map/ppermute | solution.py:1355
  16.1 3.7 copy-start.10
  17.9 214.6 %collective-permute-start.3 = (bf16[1728,768]{1,0:T(8,128)(2,1)}, bf16[1728,768]{1,0:T(8,128)(2,1)}, u32[]{:S(2)}, u32[]{:S(2)}) collective-permute-start(bf16[1728,768]{1,0:T(8,128)(2,1)} %pad.14), channel_id=1, source_target_pairs={{1,2},{2,1},{5,6},{6,5},{9,10},{10,9},{13,14},{14,13},{17,18},{18,... | collective-permute-start | bytes 7962632 | tf_op jit(solution)/shard_map/ppermute | solution.py:1364
  19.8 205.4 %collective-permute-start.2 = (bf16[1,2,24,576]{3,2,1,0:T(8,128)(2,1)S(1)}, bf16[1,2,24,576]{3,2,1,0:T(8,128)(2,1)S(1)}, u32[]{:S(2)}, u32[]{:S(2)}) collective-permute-start(bf16[1,2,24,576]{3,2,1,0:T(8,128)(2,1)S(1)} %copy-done.10), channel_id=1, source_target_pairs={{1,2},{2,1},{5,6},{6,5},{9,10},{10,9},{13,14},{14,13},{17,18},{18,... | collective-permute-start | bytes 165896 | tf_op jit(solution)/shard_map/ppermute | solution.py:1355
  33.5 1.3 copy-start.1
  34.8 0.9 copy-start.3
  35.7 193.0 %copy-start.6 = (bf16[1,24,72,641]{3,2,1,0:T(8,128)(2,1)S(1)}, bf16[1,24,72,641]{3,2,1,0:T(8,128)(2,1)}, u32[]{:S(2)}) copy-start(bf16[1,24,72,641]{3,2,1,0:T(8,128)(2,1)} %param.14) | copy-start | bytes 6645892
  217.9 6.7 copy-start
  224.6 0.6 copy-start.2
  280.3 69.5 %all-to-all-start = ((bf16[16,9,72,128]{3,2,1,0:T(8,128)(2,1)}), bf16[16,9,72,128]{3,2,1,0:T(8,128)(2,1)S(1)}, u32[]{:S(2)}, u32[]{:S(2)}) async-start(bf16[16,9,72,128]{3,2,1,0:T(8,128)(2,1)} %get-tuple-element.83), calls=%async_computation | async-start | bytes 5308416 | tf_op jit(solution)/shard_map/all_to_all | solution.py:1387
  289.2 7.0 collective-permute-start
  349.8 1.5 copy-start.9
  351.3 84.5 %all-to-all-start.1 = ((bf16[16,9,72,128]{3,2,1,0:T(8,128)(2,1)}), bf16[16,9,72,128]{3,2,1,0:T(8,128)(2,1)}, u32[]{:S(2)}, u32[]{:S(2)}) async-start(bf16[16,9,72,128]{3,2,1,0:T(8,128)(2,1)} %get-tuple-element.86), calls=%async_computation.1 | async-start | bytes 5308416 | tf_op jit(solution)/shard_map/all_to_all | solution.py:1387
  362.7 25.4 %copy-start.8 = (bf16[1,24,72,641]{3,2,1,0:T(8,128)(2,1)S(1)}, bf16[1,24,72,641]{3,2,1,0:T(8,128)(2,1)}, u32[]{:S(2)}) copy-start(bf16[1,24,72,641]{3,2,1,0:T(8,128)(2,1)} %param.19) | copy-start | bytes 6645892
  435.8 68.5 %all-to-all-start.2 = ((bf16[16,11,72,128]{3,2,1,0:T(8,128)(2,1)}), bf16[16,11,72,128]{3,2,1,0:T(8,128)(2,1)S(1)}, u32[]{:S(2)}, u32[]{:S(2)}) async-start(bf16[16,11,72,128]{3,2,1,0:T(8,128)(2,1)} %get-tuple-element.89), calls=%async_computation.2 | async-start | bytes 6488064 | tf_op jit(solution)/shard_map/all_to_all | solution.py:1387
  504.4 1.7 copy-start.5
  506.1 99.2 %all-to-all-start.3 = ((bf16[16,11,72,128]{3,2,1,0:T(8,128)(2,1)}), bf16[16,11,72,128]{3,2,1,0:T(8,128)(2,1)}, u32[]{:S(2)}, u32[]{:S(2)}) async-start(bf16[16,11,72,128]{3,2,1,0:T(8,128)(2,1)} %get-tuple-element.90), calls=%async_computation.3 | async-start | bytes 6488064 | tf_op jit(solution)/shard_map/all_to_all | solution.py:1387
  540.4 31.6 %copy-start.14 = (f32[8,768]{1,0:T(8,128)S(1)}, f32[8,768]{1,0:T(8,128)}, u32[]{:S(2)}) copy-start(f32[8,768]{1,0:T(8,128)} %get-tuple-element.106) | copy-start | bytes 73732
  540.4 31.6 %copy-start.15 = (f32[8,768]{1,0:T(8,128)S(1)}, f32[8,768]{1,0:T(8,128)}, u32[]{:S(2)}) copy-start(f32[8,768]{1,0:T(8,128)} %get-tuple-element.107) | copy-start | bytes 73732
  540.4 32.2 %copy-start.11 = (f32[8,1408]{1,0:T(8,128)S(1)}, f32[8,1408]{1,0:T(8,128)}, u32[]{:S(2)}) copy-start(f32[8,1408]{1,0:T(8,128)} %get-tuple-element.104) | copy-start | bytes 135172
  540.5 32.2 %copy-start.12 = (f32[8,1408]{1,0:T(8,128)S(1)}, f32[8,1408]{1,0:T(8,128)}, u32[]{:S(2)}) copy-start(f32[8,1408]{1,0:T(8,128)} %get-tuple-element.105) | copy-start | bytes 135172
  593.2 9.0 %copy-start.4 = (bf16[2,16,416,128]{3,2,1,0:T(8,128)(2,1)S(1)}, bf16[2,16,416,128]{3,2,1,0:T(8,128)(2,1)}, u32[]{:S(2)}) copy-start(bf16[2,16,416,128]{3,2,1,0:T(8,128)(2,1)} %shard_map.183) | copy-start | bytes 10223620
  596.1 6.1 collective-permute-start.8
  596.6 50.9 %collective-permute-start.5 = (bf16[1728,768]{1,0:T(8,128)(2,1)}, bf16[1728,768]{1,0:T(8,128)(2,1)}, u32[]{:S(2)}, u32[]{:S(2)}) collective-permute-start(bf16[1728,768]{1,0:T(8,128)(2,1)} %get-tuple-element.81), channel_id=1, source_target_pairs={{1,2},{2,1},{5,6},{6,5},{9,10},{10,9},{13,14},{14,13},{17,18},{18,... | collective-permute-start | bytes 7962632 | tf_op jit(solution)/shard_map/ppermute | solution.py:1355
  600.0 75.8 %collective-permute-start.4 = (bf16[1728,768]{1,0:T(8,128)(2,1)}, bf16[1728,768]{1,0:T(8,128)(2,1)}, u32[]{:S(2)}, u32[]{:S(2)}) collective-permute-start(bf16[1728,768]{1,0:T(8,128)(2,1)} %get-tuple-element.68), channel_id=1, source_target_pairs={{1,2},{2,1},{5,6},{6,5},{9,10},{10,9},{13,14},{14,13},{17,18},{18,... | collective-permute-start | bytes 7962632 | tf_op jit(solution)/shard_map/ppermute | solution.py:1355
  605.3 74.8 %all-to-all-start.4 = ((bf16[16,416,128]{2,1,0:T(8,128)(2,1)}), bf16[16,416,128]{2,1,0:T(8,128)(2,1)S(1)}, u32[]{:S(2)}, u32[]{:S(2)}) async-start(bf16[16,416,128]{2,1,0:T(8,128)(2,1)} %fusion), calls=%async_computation.4 | async-start | bytes 3407872 | tf_op jit(solution)/shard_map/all_to_all | solution.py:1425
  663.5 16.9 %copy-start.16 = (bf16[16,768]{1,0:T(8,128)(2,1)S(1)}, bf16[16,768]{1,0:T(8,128)(2,1)}, u32[]{:S(2)}) copy-start(bf16[16,768]{1,0:T(8,128)(2,1)} %get-tuple-element.93) | copy-start | bytes 73732
  663.5 36.4 %collective-permute-start.6 = (bf16[6,1392,128]{2,1,0:T(8,128)(2,1)}, bf16[6,1392,128]{2,1,0:T(8,128)(2,1)}, u32[]{:S(2)}, u32[]{:S(2)}) collective-permute-start(bf16[6,1392,128]{2,1,0:T(8,128)(2,1)} %get-tuple-element.92.own_ref), channel_id=1, source_target_pairs={{1,2},{2,1},{5,6},{6,5},{9,10},{10,9},{13,14},{14,13},{17,18},{18,... | collective-permute-start | bytes 6414344 | tf_op jit(solution)/shard_map/ppermute | solution.py:1435
  680.4 5.1 collective-permute-start.7
  685.5 14.3 %copy-start.13 = (bf16[16,768]{1,0:T(8,128)(2,1)}, bf16[16,768]{1,0:T(8,128)(2,1)S(1)}, u32[]{:S(2)}) copy-start(bf16[16,768]{1,0:T(8,128)(2,1)S(1)} %collective-permute-done.7.next_ref) | copy-start | bytes 73732
Sparse Core Ops, SparseCore 0:
  10.9 70.0 all-gather.1
